TPU v7x, 32 devices: a whole 2x2x4 slice. The times are simulated.
32 devices in a mesh: grp: 2 (over y), row: 4 (over z), col: 2 (over core), chan: 2 (over x).
Axes of the slice: x: 2, y: 2, z: 4, core: 2. Of those that a mesh axis runs over, the one named last changes fastest.
Arguments:
- theta: bfloat16 [2048, 16, 1024], P(('grp', 'row'), None, ('col', 'chan')), parts along dimension 0, may hold values from -6 to 6
- left_env: bfloat16 [2048, 12, 1024], P(('grp', 'row')), parts along dimension 0, may hold values from -0.25 to 0.25
- right_env: bfloat16 [2048, 12, 1024], P('grp', None, ('col', 'chan')), parts along dimension 0, may hold values from -0.078125 to 0.078125
- mpo_left: float32 [12, 12, 4, 4], replicated, may hold values from -0.875 to 0.875
- mpo_right: float32 [12, 12, 4, 4], replicated, may hold values from -0.875 to 0.875
Outputs:
- residual: bfloat16 [2048, 16384], P(('grp', 'col', 'chan'), 'row'), parts along dimension 0
- hvp: bfloat16 [2048, 16, 1024], P(('grp', 'row'), None, ('col', 'chan')), parts along dimension 0
There are 2 independent parts, one for each index of `grp`. A program takes and returns all parts, laid end to end along the dimension named above; an argument that names none is the same for every part. Nothing has to cross between parts.
All inputs are finite; a program needn't handle non-finite values.
Results may differ from a plain program's by a relative error of at most 0.025.
Values may be sent and summed in bfloat16 or wider, within the bound.
No kernel may reach another device: no remote copies, remote signals or barrier semaphores. Data moves between devices by JAX's collectives and lax.ppermute only.
A program may use at most 128 MiB of HBM per device.

v0:
```python
import jax
import jax.numpy as jnp
from jax import lax
from jax.sharding import PartitionSpec as P


def shards(theta, left_env, right_env, mpo_left, mpo_right):
    left_rows = left_env.shape[0]
    channels = left_env.shape[1]
    phys = mpo_left.shape[2]
    phys_pair = theta.shape[1]
    right_rows = theta.shape[2]
    paired = jnp.einsum("wuxs,uvyt->wstxyv", mpo_left, mpo_right, precision=lax.Precision.HIGHEST)
    mpo_pair = paired.reshape(channels * phys * phys, phys * phys * channels).astype(jnp.bfloat16)
    env_block = left_env
    section_one = jnp.einsum(
        "awk,ksb->awsb",
        env_block,
        lax.all_gather(theta, "row", axis=0, tiled=True),
        preferred_element_type=jnp.float32,
    )
    section_one = section_one.astype(jnp.bfloat16).reshape(
        left_rows, channels * phys_pair, right_rows
    )
    section_three = jnp.einsum(
        "pq,apb->aqb", mpo_pair, section_one, preferred_element_type=jnp.float32
    )
    section_three = section_three.astype(jnp.bfloat16).reshape(
        left_rows, phys_pair, channels, right_rows
    )
    env_block = right_env
    term = jnp.einsum("kvb,asvb->kas", env_block, section_three, preferred_element_type=jnp.float32)
    residual_block = lax.psum_scatter(
        term.reshape(right_rows * lax.axis_size(("col", "chan")), left_rows * phys_pair).astype(
            jnp.bfloat16
        ),
        ("col", "chan"),
        scatter_dimension=0,
        tiled=True,
    )
    env_block = right_env
    back_one = jnp.einsum(
        "kp,kvb->pvb",
        lax.all_gather(residual_block, ("col", "chan"), axis=0, tiled=True),
        env_block,
        preferred_element_type=jnp.float32,
    )
    back_one = back_one.astype(jnp.bfloat16).reshape(left_rows, phys_pair * channels, right_rows)
    back_two = jnp.einsum("pq,aqb->apb", mpo_pair, back_one, preferred_element_type=jnp.float32)
    back_two = back_two.astype(jnp.bfloat16).reshape(left_rows, channels, phys_pair, right_rows)
    env_block = left_env
    product = lax.psum_scatter(
        jnp.einsum("awk,awsb->ksb", env_block, back_two, preferred_element_type=jnp.float32).astype(
            jnp.bfloat16
        ),
        "row",
        scatter_dimension=0,
        tiled=True,
    )
    return (residual_block, product)


def solution(mesh):
    in_specs = (
        P(("grp", "row"), None, ("col", "chan")),
        P(("grp", "row"), None, None),
        P("grp", None, ("col", "chan")),
        P(),
        P(),
    )
    out_specs = (P(("grp", "col", "chan"), "row"), P(("grp", "row"), None, ("col", "chan")))
    return jax.shard_map(shards, mesh=mesh, in_specs=in_specs, out_specs=out_specs, check_vma=False)
```

profile of v0, /device:TPU:16, one launch (start us, length us, event | category | flops | bytes accessed | tf_op | source)
XLA Modules:
  0.0 790.4 jit_solution(15360294067785528244)
XLA Ops:
  7.2 3.6 copy.16
  10.9 0.0 reduce-scatter.3.cloned.1.call-start
  10.9 2.8 fusion.21
  13.7 2.3 copy.19
  16.0 0.8 convert_element_type.46
  16.7 143.2 %all-gather.3.cloned.1.call-done = bf16[1024,16,256]{2,0,1:T(8,128)(2,1)} async-done(((bf16[256,16,256]{2,0,1:T(8,128)(2,1)}), bf16[1024,16,256]{2,0,1:T(8,128)(2,1)}) %all-gather.3.cloned.1.call-update) | async-done | bytes 8388624 | tf_op jit(solution)/shard_map/all_gather | solution.py:19
  160.0 33.8 %convolution_convert_fusion.2 = bf16[256,12,16,256]{3,0,2,1:T(8,128)(2,1)} fusion(bf16[1024,16,256]{2,0,1:T(8,128)(2,1)} %all-gather.3.cloned.1.call-done, bf16[256,12,1024]{2,0,1:T(8,128)(2,1)} %param.6), kind=kOutput, calls=%fused_computation.9 | convolution fusion | flops 25782386688 | bytes 39845888 | tf_op jit(solution)/shard_map/awk,ksb->awsb/dot_general | solution.py:16
  193.7 71.4 %convert_bitcast_fusion = bf16[256,192,256]{2,1,0:T(8,128)(2,1)} fusion(bf16[256,192,256]{2,0,1:T(8,128)(2,1)} %bitcast.55, bf16[192,192]{1,0:T(8,128)(2,1)S(1)} %convert_element_type.46), kind=kOutput, calls=%fused_computation.4 | convolution fusion | flops 4844421120 | bytes 50405376 | tf_op jit(solution)/shard_map/pq,apb->aqb/dot_general | solution.py:25
  265.1 23.8 %copy.22 = bf16[256,192,256]{2,0,1:T(8,128)(2,1)} copy(bf16[256,192,256]{2,1,0:T(8,128)(2,1)} %convert_bitcast_fusion) | data formatting | bytes 50331648 | tf_op jit(solution)/shard_map/convert_element_type | solution.py:28
  288.9 32.7 %fusion.13 = bf16[1024,256,16]{0,1,2:T(8,128)(2,1)} fusion(bf16[256,16,12,256]{3,0,2,1:T(8,128)(2,1)} %bitcast.57, bf16[1024,12,256]{2,0,1:T(8,128)(2,1)} %param.7), kind=kOutput, calls=%fused_computation.15 | convolution fusion | flops 25773998080 | bytes 39845888 | tf_op jit(solution)/shard_map/kvb,asvb->kas/dot_general | solution.py:32
  321.6 11.3 %copy.23 = bf16[1024,256,16]{0,2,1:T(8,128)(2,1)} copy(bf16[1024,256,16]{0,1,2:T(8,128)(2,1)} %fusion.13) | data formatting | bytes 16777216 | tf_op jit(solution)/shard_map/convert_element_type | solution.py:34
  332.9 0.0 all-gather.5.cloned.1.call-start
  333.0 71.7 %reduce-scatter.3.cloned.1.call-done = bf16[256,4096]{0,1:T(8,128)(2,1)} async-done(((bf16[1024,4096]{0,1:T(8,128)(2,1)}), bf16[256,4096]{0,1:T(8,128)(2,1)}) %reduce-scatter.3.cloned.1.call-update) | async-done | bytes 2097168 | tf_op jit(solution)/shard_map/reduce_scatter | solution.py:33
  404.8 0.8 reshape.33
  405.6 60.3 %all-gather.5.cloned.1.call-done = bf16[1024,4096]{0,1:T(8,128)(2,1)} async-done(((bf16[256,4096]{0,1:T(8,128)(2,1)}), bf16[1024,4096]{0,1:T(8,128)(2,1)}) %all-gather.5.cloned.1.call-update) | async-done | bytes 8388624 | tf_op jit(solution)/shard_map/all_gather | solution.py:44
  465.8 34.2 %convolution_convert_fusion = bf16[4096,12,256]{2,0,1:T(8,128)(2,1)} fusion(bf16[1024,12,256]{2,0,1:T(8,128)(2,1)} %param.7, bf16[1024,4096]{0,1:T(8,128)(2,1)} %all-gather.5.cloned.1.call-done), kind=kOutput, calls=%fused_computation.7 | convolution fusion | flops 25782386688 | bytes 39845888 | tf_op jit(solution)/shard_map/kp,kvb->pvb/dot_general | solution.py:42
  500.0 26.9 %copy.24 = bf16[4096,12,256]{2,1,0:T(8,128)(2,1)} copy(bf16[4096,12,256]{2,0,1:T(8,128)(2,1)} %convolution_convert_fusion) | data formatting | bytes 50331648 | tf_op jit(solution)/shard_map/convert_element_type | solution.py:48
  526.9 40.2 %reshape.23 = bf16[256,192,256]{2,1,0:T(8,128)(2,1)} reshape(bf16[4096,12,256]{2,1,0:T(8,128)(2,1)} %copy.24) | data formatting | bytes 50331648 | tf_op jit(solution)/shard_map/reshape | solution.py:48
  567.1 22.0 %convolution_convert_fusion.1 = bf16[256,256,192]{1,2,0:T(8,128)(2,1)} fusion(bf16[192,192,1]{1,0,2:T(8,128)(2,1)S(1)} %reshape.33, bf16[256,192,256]{2,1,0:T(8,128)(2,1)} %reshape.23), kind=kOutput, calls=%fused_computation.8 | convolution fusion | flops 4844421120 | bytes 50405376 | tf_op jit(solution)/shard_map/pq,aqb->apb/dot_general | solution.py:49
  589.1 44.5 %fusion.16 = bf16[1024,16,256]{0,2,1:T(8,128)(2,1)} fusion(bf16[256,12,1024]{2,0,1:T(8,128)(2,1)} %param.6, bf16[256,12,16,256]{3,2,1,0:T(8,128)(2,1)} %bitcast.54), kind=kOutput, calls=%fused_computation.16 | convolution fusion | flops 25773998080 | bytes 39845888 | tf_op jit(solution)/shard_map/awk,awsb->ksb/dot_general | solution.py:53
  633.6 1.6 copy-done.2
  635.1 2.8 copy.26
  638.0 141.0 %reduce-scatter.5.cloned.1.call-done = bf16[256,16,256]{0,2,1:T(8,128)(2,1)} async-done(((bf16[1024,16,256]{0,2,1:T(8,128)(2,1)}), bf16[256,16,256]{0,2,1:T(8,128)(2,1)}) %reduce-scatter.5.cloned.1.call-update) | async-done | bytes 2097168 | tf_op jit(solution)/shard_map/reduce_scatter | solution.py:52
  778.9 4.5 copy.27
  (11 shorter events, 0.2 us)
Async XLA Ops:
  7.2 3.8 copy-start
  7.2 152.8 %all-gather.3.cloned.1.call-start = ((), (), s32[]{:S(2)}) async-start(), calls=%async_computation.2 | async-start | bytes 10485760 | tf_op jit(solution)/shard_map/all_gather | solution.py:19
  10.9 393.9 %reduce-scatter.3.cloned.1.call-start = ((), (), s32[]{:S(2)}) async-start(), calls=%async_computation.3 | async-start | bytes 10485760 | tf_op jit(solution)/shard_map/reduce_scatter | solution.py:33
  332.9 132.9 %all-gather.5.cloned.1.call-start = ((), (), s32[]{:S(2)}) async-start(), calls=%async_computation.4 | async-start | bytes 10485760 | tf_op jit(solution)/shard_map/all_gather | solution.py:44
  404.8 374.2 %reduce-scatter.5.cloned.1.call-start = ((), (), s32[]{:S(2)}) async-start(), calls=%async_computation.5 | async-start | bytes 10485760 | tf_op jit(solution)/shard_map/reduce_scatter | solution.py:52
  633.5 1.6 copy-start.2
  633.5 149.9 %copy-start.1 = (f32[12,12,4,4]{1,3,2,0:T(4,128)S(1)}, f32[12,12,4,4]{1,3,2,0:T(4,128)}, u32[]{:S(2)}) copy-start(f32[12,12,4,4]{1,3,2,0:T(4,128)} %param.8) | copy-start | bytes 27652
Sparse Core Ops, SparseCore 0:
  11.0 148.9 all-gather.2
  333.1 71.6 reduce-scatter.2
  406.4 59.4 all-gather.4
  633.7 145.2 reduce-scatter.4
where the time goes:
time: 800 us; the launch traced here: 790 us
  waiting for transfers between devices  416 us (52%)
  matrix products  241 us (30%)
  local copies, waits for them, and re-layouts  119 us (15%)
  between operations  14.3 us (2%)
    all_gather x1, waiting for transfers between devices, shards(): lax.all_gather(theta, 'row', axis=0, tiled=True)  143 us
    reduce_scatter x1, waiting for transfers between devices, shards(): lax.psum_scatter(jnp.einsum('awk,awsb->ksb', env_block, back_two, preferr...  141 us
    reduce_scatter x1, waiting for transfers between devices, shards(): lax.psum_scatter(term.reshape(right_rows * lax.axis_size(('col', 'chan'))...  71.7 us
    dot_general x1, matrix products, shards(): jnp.einsum('pq,apb->aqb', mpo_pair, section_one, preferred_element_type=j...  71.4 us
    all_gather x1, waiting for transfers between devices, shards(): lax.all_gather(residual_block, ('col', 'chan'), axis=0, tiled=True)  60.3 us
    dot_general x1, matrix products, shards(): jnp.einsum('awk,awsb->ksb', env_block, back_two, preferred_element_type=j...  44.5 us
    reshape x1, local copies, waits for them, and re-layouts, shards(): back_one.astype(jnp.bfloat16)  40.2 us
    dot_general x1, matrix products, shards(): jnp.einsum('kp,kvb->pvb', lax.all_gather(residual_block, ('col', 'chan'),...  34.2 us
  transfers between devices with their start and end apart: 4, of which 4 were waited for; matrix products, arithmetic and copies ran while one was open for 1% of the time, Pallas kernels for 0%

commit v1 on v0

v1 whole, which is shorter than its diff:
```python
import functools

import jax
import jax.numpy as jnp
from jax import lax
from jax.experimental import pallas as pl
from jax.experimental.pallas import tpu as pltpu
from jax.sharding import PartitionSpec as P

BF16 = jnp.bfloat16
F32 = jnp.float32
MIB = 1024 * 1024
LINES = (((1,), (0,)), ((), ()))
ROWS = (((1,), (1,)), ((), ()))
COLS = (((0,), (0,)), ((), ()))
ANY = pl.BlockSpec(memory_space=pl.ANY)
ONCE = pl.Buffered(1)


def dot(x, y, dims=LINES):
    return lax.dot_general(x, y, dims, preferred_element_type=F32)


def params(limit=56):
    return pltpu.CompilerParams(vmem_limit_bytes=limit * MIB)


def cost(flops, moved):
    return pl.CostEstimate(flops=int(flops), bytes_accessed=int(moved), transcendentals=0)


def run(copies):
    for condition, copy in copies:
        pl.when(condition)(copy.start)
    for condition, copy in copies:
        pl.when(condition)(copy.wait)


def theta_copies(blocks, held, sems, n_rows):
    depth = blocks[0].shape[0]
    row = lax.axis_index("row")
    copies = []
    for k, block in enumerate(blocks):
        source = row + (k - (n_rows - 1))
        target = held.at[pl.ds(pl.multiple_of(source * depth, depth), depth), :]
        copies.append(
            ((source >= 0) & (source < n_rows), pltpu.make_async_copy(block, target, sems.at[k]))
        )
    return copies


def right_copies(right, held, sems, half, lanes):
    return [
        (
            True,
            pltpu.make_async_copy(
                right.at[v, :, pl.ds(half * lanes, lanes)],
                held.at[:, pl.ds(v * lanes, lanes)],
                sems.at[v],
            ),
        )
        for v in range(right.shape[0])
    ]


def block_of(k):
    n_col, n_chan = lax.axis_size("col"), lax.axis_size("chan")
    col = lax.rem(lax.axis_index("col") + k // n_chan, n_col)
    return col * n_chan + lax.rem(lax.axis_index("chan") + k % n_chan, n_chan)


def order_kernel(env_ref, order_ref, left_ref, turned_ref):
    env = env_ref[...].reshape(order_ref.shape[0], env_ref.shape[2])
    left_ref[...] = dot(order_ref[...], env).astype(BF16)
    turned_ref[...] = dot(env, order_ref[...], (((0,), (1,)), ((), ()))).astype(BF16)


def ordered(env, tile):
    channels, bonds, depth = env.shape
    size = tile * channels
    index = jnp.arange(size)
    wanted = (index % channels) * tile + index // channels
    order = (wanted[:, None] == index[None, :]).astype(BF16)
    return pl.pallas_call(
        order_kernel,
        grid=(bonds // tile,),
        in_specs=[
            pl.BlockSpec((channels, tile, depth), lambda i: (0, i, 0)),
            pl.BlockSpec((size, size), lambda i: (0, 0)),
        ],
        out_specs=[
            pl.BlockSpec((size, depth), lambda i: (i, 0)),
            pl.BlockSpec((depth, size), lambda i: (0, i)),
        ],
        out_shape=[
            jax.ShapeDtypeStruct((bonds * channels, depth), BF16),
            jax.ShapeDtypeStruct((depth, bonds * channels), BF16),
        ],
        compiler_params=params(),
        cost_estimate=cost(4 * size * env.size, 6 * env.size),
    )(env, order)


def fore_kernel(n_rows, half, has_total, n_outs, n_deps, *refs):
    refs = list(refs)
    blocks = refs[: 2 * n_rows - 1]
    left_ref, mpo_ref, right = refs[2 * n_rows - 1 : 2 * n_rows + 2]
    rest = refs[2 * n_rows + 2 :]
    total_ref = rest.pop(0) if has_total else None
    del rest[:n_deps]
    outs = rest[:n_outs]
    held, right_held, ones, threes, acc, block_sems, right_sems = rest[n_outs:]
    channels = right.shape[0]
    lanes = right_held.shape[1] // channels
    phys_pair = held.shape[1] // lanes
    pair, step = 2 * channels, 2 * phys_pair
    pairs = left_ref.shape[0] // pair

    @pl.when(pl.program_id(0) == 0)
    def _():
        run(
            theta_copies(blocks, held, block_sems, n_rows)
            + right_copies(right, right_held, right_sems, half, lanes)
        )

    full = dot(left_ref[...], held[...])
    for i in range(pairs):
        for s in range(0, phys_pair, 2):
            both = [
                full[i * pair : (i + 1) * pair, q * lanes : (q + 1) * lanes] for q in (s, s + 1)
            ]
            ones[s * pair : (s + 2) * pair, i * lanes : (i + 1) * lanes] = jnp.concatenate(
                both, axis=0
            ).astype(BF16)
    mixed = dot(mpo_ref[...], ones[...]).astype(BF16)
    for i in range(pairs):
        for v in range(channels):
            threes[i * step : (i + 1) * step, v * lanes : (v + 1) * lanes] = mixed[
                v * step : (v + 1) * step, i * lanes : (i + 1) * lanes
            ]
    part = dot(right_held[...], threes[...], ROWS)
    if has_total:
        part = part + total_ref[...]
    if n_outs == 1:
        outs[0][...] = part.astype(outs[0].dtype)
    else:
        acc[...] = part
        n_blocks = lax.axis_size("col") * lax.axis_size("chan")
        height = acc.shape[0] // n_blocks
        per = n_blocks // n_outs
        for k in range(n_blocks):
            rows = pl.ds(pl.multiple_of(block_of(k) * height, height), height)
            first = k % per * height
            outs[k // per][first : first + height] = acc[rows].astype(BF16)


def fore(blocks, left, mpo, right, total, half, lanes, group, groups, n_outs, kind, tile, deps):
    depth, columns = blocks[0].shape
    n_rows = (len(blocks) + 1) // 2
    channels, far, _ = right.shape
    phys_pair = columns // lanes
    bonds = left.shape[0] // channels // groups
    steps = bonds // tile
    has_total = total is not None
    acc_spec = pl.BlockSpec((far, tile * phys_pair), lambda i: (0, group * steps + i))
    return pl.pallas_call(
        functools.partial(fore_kernel, n_rows, half, has_total, n_outs, len(deps)),
        grid=(steps,),
        in_specs=[ANY] * len(blocks)
        + [
            pl.BlockSpec((tile * channels, left.shape[1]), lambda i: (group * steps + i, 0)),
            pl.BlockSpec(mpo.shape, lambda i: (0, 0)),
            ANY,
        ]
        + [acc_spec] * has_total
        + [ANY] * len(deps),
        out_specs=[pl.BlockSpec((far // n_outs, tile * phys_pair), lambda i: (0, i))] * n_outs,
        out_shape=[jax.ShapeDtypeStruct((far // n_outs, bonds * phys_pair), kind)] * n_outs,
        scratch_shapes=[
            pltpu.VMEM((depth * n_rows, columns), BF16),
            pltpu.VMEM((far, channels * lanes), BF16),
            pltpu.VMEM((2 * channels * phys_pair, tile // 2 * lanes), BF16),
            pltpu.VMEM((tile * phys_pair, channels * lanes), BF16),
            pltpu.VMEM((far, tile * phys_pair) if n_outs > 1 else (8, 128), F32),
            pltpu.SemaphoreType.DMA((len(blocks),)),
            pltpu.SemaphoreType.DMA((channels,)),
        ],
        compiler_params=params(),
        cost_estimate=cost(
            2 * bonds * phys_pair * lanes * channels * (left.shape[1] + far)
            + bonds * mpo.size * lanes,
            2 * (depth * n_rows * columns + far * channels * lanes + bonds * channels * depth)
            + 4 * far * bonds * phys_pair,
        ),
    )(*blocks, left, mpo, right, *([total] if has_total else []), *deps)


def back_kernel(n_parts, half, scattered, n_deps, *refs):
    parts = refs[:n_parts]
    mpo_ref, right = refs[n_parts : n_parts + 2]
    out_ref, right_held, joined, ones, right_sems = refs[n_parts + 2 + n_deps :]
    channels = right.shape[0]
    lanes = right_held.shape[1] // channels
    phys_pair = out_ref.shape[1] // lanes
    pair, step = 2 * channels, 2 * phys_pair
    pairs = out_ref.shape[0] // pair

    @pl.when(pl.program_id(0) == 0)
    def _():
        run(right_copies(right, right_held, right_sems, half, lanes))

    height = parts[0].shape[0]
    for k, part in enumerate(parts):
        place = block_of(k) if scattered else k
        joined[pl.ds(pl.multiple_of(place * height, height), height), :] = part[...]
    full = dot(joined[...], right_held[...], COLS).astype(BF16)
    for i in range(pairs):
        for v in range(channels):
            ones[v * step : (v + 1) * step, i * lanes : (i + 1) * lanes] = full[
                i * step : (i + 1) * step, v * lanes : (v + 1) * lanes
            ]
    mixed = dot(mpo_ref[...], ones[...])
    for i in range(0, pairs, 2):
        for s in range(phys_pair):
            both = [
                mixed[s * pair : (s + 1) * pair, j * lanes : (j + 1) * lanes] for j in (i, i + 1)
            ]
            out_ref[i * pair : (i + 2) * pair, s * lanes : (s + 1) * lanes] = jnp.concatenate(
                both, axis=0
            ).astype(BF16)


def back(parts, mpo, right, half, lanes, phys_pair, scattered, tile, deps):
    columns = parts[0].shape[1]
    bonds = columns // phys_pair
    channels, far, _ = right.shape
    return pl.pallas_call(
        functools.partial(back_kernel, len(parts), half, scattered, len(deps)),
        grid=(bonds // tile,),
        in_specs=[pl.BlockSpec((p.shape[0], tile * phys_pair), lambda i: (0, i)) for p in parts]
        + [pl.BlockSpec(mpo.shape, lambda i: (0, 0)), ANY]
        + [ANY] * len(deps),
        out_specs=pl.BlockSpec((tile * channels, phys_pair * lanes), lambda i: (i, 0)),
        out_shape=jax.ShapeDtypeStruct((bonds * channels, phys_pair * lanes), BF16),
        scratch_shapes=[
            pltpu.VMEM((far, channels * lanes), BF16),
            pltpu.VMEM((far, tile * phys_pair), BF16),
            pltpu.VMEM((2 * channels * phys_pair, tile // 2 * lanes), BF16),
            pltpu.SemaphoreType.DMA((channels,)),
        ],
        compiler_params=params(),
        cost_estimate=cost(
            2 * far * channels * lanes * columns + bonds * mpo.size * lanes,
            2 * (far * channels * lanes + far * columns + bonds * channels * phys_pair * lanes),
        ),
    )(*parts, mpo, right, *deps)


def last_kernel(n_rows, n_groups, n_deps, *refs):
    left_ref = refs[0]
    backs = refs[1 : 1 + n_groups]
    outs = refs[1 + n_groups + n_deps : -1]
    acc = refs[-1]
    height = outs[0].shape[0]
    depth = backs[0].shape[0]
    for g, part in enumerate(backs):
        term = dot(left_ref[:, g * depth : (g + 1) * depth], part[...])
        if g == 0:
            acc[...] = term
        else:
            acc[...] += term
    for d, out in enumerate(outs):
        j = lax.rem(lax.axis_index("row") + d, n_rows)
        out[...] = acc[pl.ds(pl.multiple_of(j * height, height), height), :].astype(BF16)


def last(left_t, backs, chunk, n_chunks, n_rows, deps):
    columns = backs[0].shape[1] // n_chunks
    steps = 2
    height = left_t.shape[0] // n_rows
    return pl.pallas_call(
        functools.partial(last_kernel, n_rows, len(backs), len(deps)),
        grid=(steps,),
        in_specs=[pl.BlockSpec(left_t.shape, lambda i: (0, 0), pipeline_mode=ONCE)]
        + [
            pl.BlockSpec((b.shape[0], columns // steps), lambda i: (0, chunk * steps + i))
            for b in backs
        ]
        + [ANY] * len(deps),
        out_specs=[pl.BlockSpec((height, columns // steps), lambda i: (0, i))] * n_rows,
        out_shape=[jax.ShapeDtypeStruct((height, columns), BF16)] * n_rows,
        scratch_shapes=[pltpu.VMEM((left_t.shape[0], columns // steps), F32)],
        compiler_params=params(),
        cost_estimate=cost(
            2 * left_t.size * columns,
            2 * (left_t.size + left_t.shape[1] * columns + left_t.shape[0] * columns),
        ),
    )(left_t, *backs, *deps)


def gather_rows(block, n_rows):
    above, below = [], []
    up = down = block
    for t in range(1, n_rows):
        up = lax.ppermute(up, "row", [(r, r + 1) for r in range(t - 1, n_rows - 1)])
        down = lax.ppermute(down, "row", [(r, r - 1) for r in range(1, n_rows - t + 1)])
        above.append(up)
        below.append(down)
    return above[::-1] + [block] + below


def scatter_rows(terms, n_rows):
    up = down = None
    for t in range(1, n_rows):
        mine, other = terms[n_rows - t], terms[t]
        if up is not None:
            mine = (mine.astype(F32) + up.astype(F32)).astype(BF16)
            other = (other.astype(F32) + down.astype(F32)).astype(BF16)
        up = lax.ppermute(mine, "row", [(r, r + 1) for r in range(t)])
        down = lax.ppermute(other, "row", [(n_rows - 1 - r, n_rows - 2 - r) for r in range(t)])
        if t == 1:
            early = up
    return terms[0].astype(F32) + up.astype(F32) + down.astype(F32), early


def add(x, y):
    return (x.astype(F32) + y.astype(F32)).astype(BF16)


def shards(theta, left_env, right_env, mpo_left, mpo_right):
    bonds, channels, depth = left_env.shape
    rows, phys_pair, width = theta.shape
    n_rows = lax.axis_size("row")
    scattered = lax.axis_size("col") == 2 and lax.axis_size("chan") == 2
    tile = min(32, bonds)
    lanes = min(128, width)
    halves = width // lanes
    groups = max(1, min(4, bonds // tile))
    swap = [(0, 1), (1, 0)]

    pieces = [
        theta[:, :, h * lanes : (h + 1) * lanes].reshape(rows, phys_pair * lanes)
        for h in range(halves)
    ]
    gathered = [gather_rows(p, n_rows) for p in pieces]

    paired = jnp.einsum("wuxs,uvyt->wstxyv", mpo_left, mpo_right, precision=lax.Precision.HIGHEST)
    mpo = paired.reshape(channels, phys_pair, phys_pair, channels).astype(BF16)
    twice = jnp.einsum("wsxv,jk->sjwvkx", mpo, jnp.eye(2, dtype=BF16))
    size = 2 * channels * phys_pair
    mpo_back = twice.reshape(size, size)
    mpo_fore = mpo_back.T

    left, left_t = ordered(left_env.transpose(1, 0, 2), tile)
    right = right_env.transpose(1, 0, 2)

    total = None
    for h in range(halves - 1):
        (total,) = fore(
            gathered[h], left, mpo_fore, right, total, h, lanes, 0, 1, 1, F32, tile, []
        )

    own, everyone = [], []
    for g in range(groups):
        terms = fore(
            gathered[-1], left, mpo_fore, right, total, halves - 1, lanes, g, groups,
            2 if scattered else 1, BF16, tile, [own[g - 2]] if g > 1 else [],
        )
        if scattered:
            near = add(terms[0], lax.ppermute(terms[1], "col", swap))
            half = near.shape[0] // 2
            mine = add(near[:half], lax.ppermute(near[half:], "chan", swap))
            across = lax.ppermute(mine, "chan", swap)
            parts = [mine, across] + [lax.ppermute(p, "col", swap) for p in (mine, across)]
        else:
            mine = lax.psum_scatter(terms[0], ("col", "chan"), scatter_dimension=0, tiled=True)
            parts = [lax.all_gather(mine, ("col", "chan"), axis=0, tiled=True)]
        own.append(mine)
        everyone.append(parts)

    n_chunks = 2
    per = phys_pair // n_chunks
    products, deps, early = [], [], []
    for h in range(halves):
        backs = [
            back(parts, mpo_back, right, h, lanes, phys_pair, scattered, tile, deps)
            for parts in everyone
        ]
        chunks = []
        for c in range(n_chunks):
            terms = last(left_t, backs, c, n_chunks, n_rows, early[-2:-1])
            deps = [terms[0]]
            chunk, first = scatter_rows(terms, n_rows)
            early.append(first)
            chunks.append(chunk.astype(BF16).reshape(rows, per, lanes))
        products.append(jnp.concatenate(chunks, axis=1))
    return jnp.concatenate(own, axis=1), jnp.concatenate(products, axis=2)


def solution(mesh):
    in_specs = (
        P(("grp", "row"), None, ("col", "chan")),
        P(("grp", "row"), None, None),
        P("grp", None, ("col", "chan")),
        P(),
        P(),
    )
    out_specs = (P(("grp", "col", "chan"), "row"), P(("grp", "row"), None, ("col", "chan")))
    return jax.shard_map(shards, mesh=mesh, in_specs=in_specs, out_specs=out_specs, check_vma=False)
```

time: 800 us -> 567 us (0.71)
  waiting for transfers between devices: 416 us -> 154 us
  Pallas kernels: 0 us -> 251 us
  matrix products: 241 us -> 2.83 us
  starting transfers between devices: 0.16 us -> 105 us
  local copies, waits for them, and re-layouts: 119 us -> 28 us
  other arithmetic: 0 us -> 17.5 us
  between operations: 14.3 us -> 2.24 us
    pallas_call x0 -> x18, Pallas kernels: none -> 251 us  [the longest x5 104 us: fore(): pl.pallas_call(functools.partial(fore_kernel, n_rows, half, has_total, n_...]
    dot_general x6 -> x0, matrix products: 238 us -> none  [the longest x1 71.4 us: shards(): jnp.einsum('pq,apb->aqb', mpo_pair, section_one, preferred_element_type=j...]
    reduce_scatter x2 -> x0, waiting for transfers between devices: 213 us -> none  [the longest x1 141 us: shards(): lax.psum_scatter(jnp.einsum('awk,awsb->ksb', env_block, back_two, preferr...]
    all_gather x2 -> x0, waiting for transfers between devices: 203 us -> none  [the longest x1 143 us: shards(): lax.all_gather(theta, 'row', axis=0, tiled=True)]
    ppermute x0 -> x56, waiting for transfers between devices: none -> 154 us  [the longest x6 45.4 us: gather_rows(): up = lax.ppermute(up, 'row', [(r, r + 1) for r in range(t - 1, n_rows - 1)])]
    ppermute x0 -> x56, starting transfers between devices: none -> 105 us  [the longest x12 42.3 us: scatter_rows(): lax.ppermute(other, 'row', [(n_rows - 1 - r, n_rows - 2 - r) for r in ran...]
    convert_element_type x6 -> x2, local copies, waits for them, and re-layouts: 65.8 us -> 7.15 us  [shards(): mpo = paired.reshape(channels, phys_pair, phys_pair, channels).astype(BF16)]
    reshape x1, local copies, waits for them, and re-layouts: 40.2 us -> 7.42 us  [shards(): mpo_back = twice.reshape(size, size)]
  transfers between devices with their start and end apart: 4 -> 56, of which waited for: 4 -> 22; matrix products, arithmetic and copies ran while one was open for 1% -> 6% of each run, Pallas kernels for 0% -> 36%
where the time goes in v1:
time: 567 us; the launch traced here: 561 us
  Pallas kernels  251 us (44%)
  waiting for transfers between devices  154 us (27%)
  starting transfers between devices  105 us (19%)
  local copies, waits for them, and re-layouts  28 us (5%)
  other arithmetic  17.5 us (3%)
    pallas_call x5, Pallas kernels, fore(): pl.pallas_call(functools.partial(fore_kernel, n_rows, half, has_total, n_...  104 us
    pallas_call x8, Pallas kernels, back(): pl.pallas_call(functools.partial(back_kernel, len(parts), half, scattered...  84.1 us
    pallas_call x4, Pallas kernels, last(): pl.pallas_call(functools.partial(last_kernel, n_rows, len(backs), len(dep...  50.2 us
    ppermute x6, waiting for transfers between devices, gather_rows(): up = lax.ppermute(up, 'row', [(r, r + 1) for r in range(t - 1, n_rows - 1)])  45.4 us
    ppermute x12, starting transfers between devices, scatter_rows(): lax.ppermute(other, 'row', [(n_rows - 1 - r, n_rows - 2 - r) for r in ran...  42.3 us
    ppermute x12, waiting for transfers between devices, scatter_rows(): lax.ppermute(other, 'row', [(n_rows - 1 - r, n_rows - 2 - r) for r in ran...  39.2 us
    ppermute x4, waiting for transfers between devices, shards(): mine = add(near[:half], lax.ppermute(near[half:], 'chan', swap))  32.1 us
    ppermute x4, waiting for transfers between devices, shards(): across = lax.ppermute(mine, 'chan', swap)  21.8 us
  transfers between devices with their start and end apart: 56, of which 22 were waited for; matrix products, arithmetic and copies ran while one was open for 6% of the time, Pallas kernels for 36%

profile of v1, /device:TPU:16, one launch (start us, length us, event | category | flops | bytes accessed | tf_op | source)
XLA Modules:
  0.0 560.7 jit_solution(13945890910358572583)
XLA Ops:
  15.4 15.5 %collective-permute-done.6.refs_2_ = bf16[256,2048]{1,0:T(8,128)(2,1)} collective-permute-done((bf16[256,2048]{1,0:T(8,128)(2,1)S(1)}, bf16[256,2048]{1,0:T(8,128)(2,1)}, u32[]{:S(2)}, u32[]{:S(2)}) %collective-permute-start.6) | collective-permute-done | bytes 1048608 | tf_op jit(solution)/shard_map/ppermute | solution.py:305
  60.2 15.7 %collective-permute-done.7.refs_1_ = bf16[256,2048]{1,0:T(8,128)(2,1)} collective-permute-done((bf16[256,2048]{1,0:T(8,128)(2,1)}, bf16[256,2048]{1,0:T(8,128)(2,1)}, u32[]{:S(2)}, u32[]{:S(2)}) %collective-permute-start.7) | collective-permute-done | bytes 1048608 | tf_op jit(solution)/shard_map/ppermute | solution.py:305
  95.9 12.0 %shard_map.68 = (bf16[3072,1024]{1,0:T(8,128)(2,1)}, bf16[1024,3072]{1,0:T(8,128)(2,1)}) custom-call(bf16[12,256,1024]{2,1,0:T(8,128)(2,1)} %bitcast.62, bf16[384,384]{1,0:T(8,128)(2,1)} %fusion.9.order_ref), custom_call_target="tpu_custom_call" | custom-call | flops 4831838208 | bytes 18874368 | tf_op jit(solution)/shard_map/pallas_call | solution.py:84
  119.9 41.1 %shard_map.69.refs_10_ = f32[1024,4096]{1,0:T(8,128)} custom-call(bf16[256,2048]{1,0:T(8,128)(2,1)} %collective-permute-done.8.refs_0_, bf16[256,2048]{1,0:T(8,128)(2,1)} %collective-permute-done.7.refs_1_, bf16[256,2048]{1,0:T(8,128)(2,1)} %collective-permute-done.6.refs_2_, bf16[256,2048]{1,0:T(8,128)(2,1)} %bitcast.60, ...), custom_call_target="tpu_custom_call" | custom-call | flops 30601641984 | bytes 25690112 | tf_op jit(solution)/shard_map/pallas_call | solution.py:166
  163.0 15.6 %shard_map.70 = (bf16[512,1024]{1,0:T(8,128)(2,1)}, bf16[512,1024]{1,0:T(8,128)(2,1)}) custom-call(bf16[256,2048]{1,0:T(8,128)(2,1)} %copy-done.6, bf16[256,2048]{1,0:T(8,128)(2,1)} %collective-permute-done.1.refs_1_, bf16[256,2048]{1,0:T(8,128)(2,1)} %copy-done.3, bf16[256,2048]{1,0:T(8,128)(2,1)} %bitcast.46, bf16[256,2048]{1,0:T(8,128)(2,1)} %copy-done.4, ...), custom_call_target="tpu_custom_call" | custom-call | flops 7650410496 | bytes 11927552 | tf_op jit(solution)/shard_map/pallas_call | solution.py:166
  178.7 15.6 %shard_map.71 = (bf16[512,1024]{1,0:T(8,128)(2,1)}, bf16[512,1024]{1,0:T(8,128)(2,1)}) custom-call(bf16[256,2048]{1,0:T(8,128)(2,1)} %copy-done.6, bf16[256,2048]{1,0:T(8,128)(2,1)} %collective-permute-done.1.refs_1_, bf16[256,2048]{1,0:T(8,128)(2,1)} %copy-done.3, bf16[256,2048]{1,0:T(8,128)(2,1)} %bitcast.47, bf16[256,2048]{1,0:T(8,128)(2,1)} %copy-done.4, ...), custom_call_target="tpu_custom_call" | custom-call | flops 7650410496 | bytes 11927552 | tf_op jit(solution)/shard_map/pallas_call | solution.py:166
  199.3 10.8 %collective-permute-done.13 = bf16[256,1024]{1,0:T(8,128)(2,1)S(1)} collective-permute-done((bf16[256,1024]{1,0:T(8,128)(2,1)S(1)}, bf16[256,1024]{1,0:T(8,128)(2,1)S(1)}, u32[]{:S(2)}, u32[]{:S(2)}) %collective-permute-start.13) | collective-permute-done | bytes 524320 | tf_op jit(solution)/shard_map/ppermute | solution.py:372
  211.1 15.9 %shard_map.72 = (bf16[512,1024]{1,0:T(8,128)(2,1)}, bf16[512,1024]{1,0:T(8,128)(2,1)}) custom-call(bf16[256,2048]{1,0:T(8,128)(2,1)} %copy-done.6, bf16[256,2048]{1,0:T(8,128)(2,1)} %collective-permute-done.1.refs_1_, bf16[256,2048]{1,0:T(8,128)(2,1)} %copy-done.3, bf16[256,2048]{1,0:T(8,128)(2,1)} %bitcast.48, bf16[256,2048]{1,0:T(8,128)(2,1)} %copy-done.4, ...), custom_call_target="tpu_custom_call" | custom-call | flops 7650410496 | bytes 11927552 | tf_op jit(solution)/shard_map/pallas_call | solution.py:166
  228.1 16.0 %shard_map.73 = (bf16[512,1024]{1,0:T(8,128)(2,1)}, bf16[512,1024]{1,0:T(8,128)(2,1)}) custom-call(bf16[256,2048]{1,0:T(8,128)(2,1)} %copy-done.6, bf16[256,2048]{1,0:T(8,128)(2,1)} %collective-permute-done.1.refs_1_, bf16[256,2048]{1,0:T(8,128)(2,1)} %copy-done.3, bf16[256,2048]{1,0:T(8,128)(2,1)} %bitcast.49, bf16[256,2048]{1,0:T(8,128)(2,1)} %copy-done.4, ...), custom_call_target="tpu_custom_call" | custom-call | flops 7650410496 | bytes 11927552 | tf_op jit(solution)/shard_map/pallas_call | solution.py:166
  259.5 11.2 %collective-permute-done.23.refs_1_ = bf16[256,1024]{1,0:T(8,128)(2,1)S(1)} collective-permute-done((bf16[256,1024]{1,0:T(8,128)(2,1)}, bf16[256,1024]{1,0:T(8,128)(2,1)S(1)}, u32[]{:S(2)}, u32[]{:S(2)}) %collective-permute-start.23) | collective-permute-done | bytes 524320 | tf_op jit(solution)/shard_map/ppermute | solution.py:373
  270.7 11.2 %collective-permute-done.17 = bf16[256,1024]{1,0:T(8,128)(2,1)S(1)} collective-permute-done((bf16[256,1024]{1,0:T(8,128)(2,1)S(1)}, bf16[256,1024]{1,0:T(8,128)(2,1)S(1)}, u32[]{:S(2)}, u32[]{:S(2)}) %collective-permute-start.17) | collective-permute-done | bytes 524320 | tf_op jit(solution)/shard_map/ppermute | solution.py:372
  295.7 10.5 %shard_map.74.refs_1_ = bf16[768,2048]{1,0:T(8,128)(2,1)} custom-call(bf16[256,1024]{1,0:T(8,128)(2,1)} %add_convert_fusion.19.refs_11_.refs_0_, bf16[256,1024]{1,0:T(8,128)(2,1)} %copy-done.40, bf16[256,1024]{1,0:T(8,128)(2,1)} %copy-done.41, bf16[256,1024]{1,0:T(8,128)(2,1)} %copy-done.43, bf16[384,384]{1,0:T(8,128)(2,1)} %copy-done.12, ...), custom_call_target="tpu_custom_call" | custom-call | flops 4429185024 | bytes 8388608 | tf_op jit(solution)/shard_map/pallas_call | solution.py:237
  308.8 10.6 %shard_map.75.refs_2_ = bf16[768,2048]{1,0:T(8,128)(2,1)} custom-call(bf16[256,1024]{1,0:T(8,128)(2,1)} %add_convert_fusion.18.refs_11_.refs_0_, bf16[256,1024]{1,0:T(8,128)(2,1)} %copy-done.39, bf16[256,1024]{1,0:T(8,128)(2,1)} %copy-done.42, bf16[256,1024]{1,0:T(8,128)(2,1)} %copy-done.44, bf16[384,384]{1,0:T(8,128)(2,1)} %copy-done.12, ...), custom_call_target="tpu_custom_call" | custom-call | flops 4429185024 | bytes 8388608 | tf_op jit(solution)/shard_map/pallas_call | solution.py:237
  324.3 10.4 %shard_map.76.refs_3_ = bf16[768,2048]{1,0:T(8,128)(2,1)} custom-call(bf16[256,1024]{1,0:T(8,128)(2,1)} %copy-done.10, bf16[256,1024]{1,0:T(8,128)(2,1)} %copy-done.45, bf16[256,1024]{1,0:T(8,128)(2,1)} %copy-done.47, bf16[256,1024]{1,0:T(8,128)(2,1)} %copy-done.48, bf16[384,384]{1,0:T(8,128)(2,1)} %copy-done.12, bf16[12,1024,256]{2,1,0:T(8,128)(2,1)} %bitcast.38), custom_call_target="tpu_custom_call" | custom-call | flops 4429185024 | bytes 8388608 | tf_op jit(solution)/shard_map/pallas_call | solution.py:237
  336.4 10.5 %shard_map.77.refs_4_ = bf16[768,2048]{1,0:T(8,128)(2,1)} custom-call(bf16[256,1024]{1,0:T(8,128)(2,1)} %copy-done.11, bf16[256,1024]{1,0:T(8,128)(2,1)} %copy-done.46, bf16[256,1024]{1,0:T(8,128)(2,1)} %copy-done.49, bf16[256,1024]{1,0:T(8,128)(2,1)} %copy-done.50, bf16[384,384]{1,0:T(8,128)(2,1)} %copy-done.12, bf16[12,1024,256]{2,1,0:T(8,128)(2,1)} %bitcast.39), custom_call_target="tpu_custom_call" | custom-call | flops 4429185024 | bytes 8388608 | tf_op jit(solution)/shard_map/pallas_call | solution.py:237
  346.9 12.5 %shard_map.79 = (bf16[256,1024]{1,0:T(8,128)(2,1)}, bf16[256,1024]{1,0:T(8,128)(2,1)}, bf16[256,1024]{1,0:T(8,128)(2,1)}, bf16[256,1024]{1,0:T(8,128)(2,1)}) custom-call(bf16[1024,3072]{1,0:T(8,128)(2,1)} %get-tuple-element.37.refs_0_, bf16[768,2048]{1,0:T(8,128)(2,1)} %shard_map.74.refs_1_, bf16[768,2048]{1,0:T(8,128)(2,1)} %shard_map.75.refs_2_, ...), custom_call_target="tpu_custom_call" | custom-call | flops 6442450944 | bytes 14680064 | tf_op jit(solution)/shard_map/pallas_call | solution.py:281
  359.4 12.5 %shard_map.78 = (bf16[256,1024]{1,0:T(8,128)(2,1)}, bf16[256,1024]{1,0:T(8,128)(2,1)}, bf16[256,1024]{1,0:T(8,128)(2,1)}, bf16[256,1024]{1,0:T(8,128)(2,1)}) custom-call(bf16[1024,3072]{1,0:T(8,128)(2,1)} %get-tuple-element.37.refs_0_, bf16[768,2048]{1,0:T(8,128)(2,1)} %shard_map.74.refs_1_, bf16[768,2048]{1,0:T(8,128)(2,1)} %shard_map.75.refs_2_, ...), custom_call_target="tpu_custom_call" | custom-call | flops 6442450944 | bytes 14680064 | tf_op jit(solution)/shard_map/pallas_call | solution.py:281
  376.0 10.7 %shard_map.80.refs_1_ = bf16[768,2048]{1,0:T(8,128)(2,1)} custom-call(bf16[256,1024]{1,0:T(8,128)(2,1)} %add_convert_fusion.19.refs_11_.refs_0_, bf16[256,1024]{1,0:T(8,128)(2,1)} %copy-done.40, bf16[256,1024]{1,0:T(8,128)(2,1)} %copy-done.41, bf16[256,1024]{1,0:T(8,128)(2,1)} %copy-done.43, bf16[384,384]{1,0:T(8,128)(2,1)} %copy-done.12, ...), custom_call_target="tpu_custom_call" | custom-call | flops 4429185024 | bytes 8388608 | tf_op jit(solution)/shard_map/pallas_call | solution.py:237
  386.7 10.5 %shard_map.81.refs_2_ = bf16[768,2048]{1,0:T(8,128)(2,1)} custom-call(bf16[256,1024]{1,0:T(8,128)(2,1)} %add_convert_fusion.18.refs_11_.refs_0_, bf16[256,1024]{1,0:T(8,128)(2,1)} %copy-done.39, bf16[256,1024]{1,0:T(8,128)(2,1)} %copy-done.42, bf16[256,1024]{1,0:T(8,128)(2,1)} %copy-done.44, bf16[384,384]{1,0:T(8,128)(2,1)} %copy-done.12, ...), custom_call_target="tpu_custom_call" | custom-call | flops 4429185024 | bytes 8388608 | tf_op jit(solution)/shard_map/pallas_call | solution.py:237
  397.2 10.5 %shard_map.82.refs_3_ = bf16[768,2048]{1,0:T(8,128)(2,1)} custom-call(bf16[256,1024]{1,0:T(8,128)(2,1)} %copy-done.10, bf16[256,1024]{1,0:T(8,128)(2,1)} %copy-done.45, bf16[256,1024]{1,0:T(8,128)(2,1)} %copy-done.47, bf16[256,1024]{1,0:T(8,128)(2,1)} %copy-done.48, bf16[384,384]{1,0:T(8,128)(2,1)} %copy-done.12, bf16[12,1024,256]{2,1,0:T(8,128)(2,1)} %bitcast.42, ...), custom_call_target="tpu_custom_call" | custom-call | flops 4429185024 | bytes 8388608 | tf_op jit(solution)/shard_map/pallas_call | solution.py:237
  407.6 10.5 %shard_map.83.refs_4_ = bf16[768,2048]{1,0:T(8,128)(2,1)} custom-call(bf16[256,1024]{1,0:T(8,128)(2,1)} %copy-done.11, bf16[256,1024]{1,0:T(8,128)(2,1)} %copy-done.46, bf16[256,1024]{1,0:T(8,128)(2,1)} %copy-done.49, bf16[256,1024]{1,0:T(8,128)(2,1)} %copy-done.50, bf16[384,384]{1,0:T(8,128)(2,1)} %copy-done.12, bf16[12,1024,256]{2,1,0:T(8,128)(2,1)} %bitcast.43, ...), custom_call_target="tpu_custom_call" | custom-call | flops 4429185024 | bytes 8388608 | tf_op jit(solution)/shard_map/pallas_call | solution.py:237
  418.9 12.4 %shard_map.85 = (bf16[256,1024]{1,0:T(8,128)(2,1)}, bf16[256,1024]{1,0:T(8,128)(2,1)}, bf16[256,1024]{1,0:T(8,128)(2,1)}, bf16[256,1024]{1,0:T(8,128)(2,1)}) custom-call(bf16[1024,3072]{1,0:T(8,128)(2,1)} %get-tuple-element.37.refs_0_, bf16[768,2048]{1,0:T(8,128)(2,1)} %shard_map.80.refs_1_, bf16[768,2048]{1,0:T(8,128)(2,1)} %shard_map.81.refs_2_, ...), custom_call_target="tpu_custom_call" | custom-call | flops 6442450944 | bytes 14680064 | tf_op jit(solution)/shard_map/pallas_call | solution.py:281
  434.3 12.7 %shard_map.84 = (bf16[256,1024]{1,0:T(8,128)(2,1)}, bf16[256,1024]{1,0:T(8,128)(2,1)}, bf16[256,1024]{1,0:T(8,128)(2,1)}, bf16[256,1024]{1,0:T(8,128)(2,1)}) custom-call(bf16[1024,3072]{1,0:T(8,128)(2,1)} %get-tuple-element.37.refs_0_, bf16[768,2048]{1,0:T(8,128)(2,1)} %shard_map.80.refs_1_, bf16[768,2048]{1,0:T(8,128)(2,1)} %shard_map.81.refs_2_, ...), custom_call_target="tpu_custom_call" | custom-call | flops 6442450944 | bytes 14680064 | tf_op jit(solution)/shard_map/pallas_call | solution.py:281
  493.7 16.1 %collective-permute-done.43 = bf16[256,1024]{1,0:T(8,128)(2,1)S(1)} collective-permute-done((bf16[256,1024]{1,0:T(8,128)(2,1)S(1)}, bf16[256,1024]{1,0:T(8,128)(2,1)S(1)}, u32[]{:S(2)}, u32[]{:S(2)}) %collective-permute-start.43) | collective-permute-done | bytes 524320 | tf_op jit(solution)/shard_map/ppermute | solution.py:320
  (254 shorter events, 227.5 us)
Async XLA Ops:
  9.0 44.2 %collective-permute-start = (bf16[256,2048]{1,0:T(8,128)(2,1)S(1)}, bf16[256,2048]{1,0:T(8,128)(2,1)S(1)}, u32[]{:S(2)}, u32[]{:S(2)}) collective-permute-start(bf16[256,2048]{1,0:T(8,128)(2,1)S(1)} %bitcast.44), channel_id=1, source_target_pairs={{0,4},{4,8},{8,12},{1,5},{5,9},{9,13},{2,6},{6,10},{10,14},{3,7},{... | collective-permute-start | bytes 3145736 | tf_op jit(solution)/shard_map/ppermute | solution.py:305
  13.5 43.3 %collective-permute-start.3 = (bf16[256,2048]{1,0:T(8,128)(2,1)S(1)}, bf16[256,2048]{1,0:T(8,128)(2,1)S(1)}, u32[]{:S(2)}, u32[]{:S(2)}) collective-permute-start(bf16[256,2048]{1,0:T(8,128)(2,1)S(1)} %bitcast.45), channel_id=1, source_target_pairs={{4,0},{8,4},{12,8},{5,1},{9,5},{13,9},{6,2},{10,6},{14,10},{7,3},{... | collective-permute-start | bytes 3145736 | tf_op jit(solution)/shard_map/ppermute | solution.py:306
  30.9 44.9 %collective-permute-start.7 = (bf16[256,2048]{1,0:T(8,128)(2,1)}, bf16[256,2048]{1,0:T(8,128)(2,1)}, u32[]{:S(2)}, u32[]{:S(2)}) collective-permute-start(bf16[256,2048]{1,0:T(8,128)(2,1)} %collective-permute-done.6.refs_2_), channel_id=1, source_target_pairs={{4,8},{8,12},{5,9},{9,13},{6,10},{10,14},{7,11},{11,15},{20,24},{2... | collective-permute-start | bytes 3145736 | tf_op jit(solution)/shard_map/ppermute | solution.py:305
  34.5 45.9 %collective-permute-start.10 = (bf16[256,2048]{1,0:T(8,128)(2,1)}, bf16[256,2048]{1,0:T(8,128)(2,1)}, u32[]{:S(2)}, u32[]{:S(2)}) collective-permute-start(bf16[256,2048]{1,0:T(8,128)(2,1)} %collective-permute-done.9.refs_4_), channel_id=1, source_target_pairs={{4,0},{8,4},{5,1},{9,5},{6,2},{10,6},{7,3},{11,7},{20,16},{24,20},... | collective-permute-start | bytes 3145736 | tf_op jit(solution)/shard_map/ppermute | solution.py:306
  53.3 54.7 %collective-permute-start.1 = (bf16[256,2048]{1,0:T(8,128)(2,1)S(1)}, bf16[256,2048]{1,0:T(8,128)(2,1)}, u32[]{:S(2)}, u32[]{:S(2)}) collective-permute-start(bf16[256,2048]{1,0:T(8,128)(2,1)S(1)} %collective-permute-done.refs_2_), channel_id=1, source_target_pairs={{4,8},{8,12},{5,9},{9,13},{6,10},{10,14},{7,11},{11,15},{20,24},{2... | collective-permute-start | bytes 3145736 | tf_op jit(solution)/shard_map/ppermute | solution.py:305
  56.8 52.5 %collective-permute-start.4 = (bf16[256,2048]{1,0:T(8,128)(2,1)S(1)}, bf16[256,2048]{1,0:T(8,128)(2,1)S(1)}, u32[]{:S(2)}, u32[]{:S(2)}) collective-permute-start(bf16[256,2048]{1,0:T(8,128)(2,1)S(1)} %collective-permute-done.3.refs_4_), channel_id=1, source_target_pairs={{4,0},{8,4},{5,1},{9,5},{6,2},{10,6},{7,3},{11,7},{20,16},{24,20},... | collective-permute-start | bytes 3145736 | tf_op jit(solution)/shard_map/ppermute | solution.py:306
  75.9 44.0 %collective-permute-start.8 = (bf16[256,2048]{1,0:T(8,128)(2,1)}, bf16[256,2048]{1,0:T(8,128)(2,1)}, u32[]{:S(2)}, u32[]{:S(2)}) collective-permute-start(bf16[256,2048]{1,0:T(8,128)(2,1)} %collective-permute-done.7.refs_1_), channel_id=1, source_target_pairs={{8,12},{9,13},{10,14},{11,15},{24,28},{25,29},{26,30},{27,31}} | collective-permute-start | bytes 3145736 | tf_op jit(solution)/shard_map/ppermute | solution.py:305
  80.3 39.6 %collective-permute-start.11 = (bf16[256,2048]{1,0:T(8,128)(2,1)}, bf16[256,2048]{1,0:T(8,128)(2,1)}, u32[]{:S(2)}, u32[]{:S(2)}) collective-permute-start(bf16[256,2048]{1,0:T(8,128)(2,1)} %collective-permute-done.10.refs_5_), channel_id=1, source_target_pairs={{4,0},{5,1},{6,2},{7,3},{20,16},{21,17},{22,18},{23,19}} | collective-permute-start | bytes 3145736 | tf_op jit(solution)/shard_map/ppermute | solution.py:306
  108.0 53.1 %collective-permute-start.2 = (bf16[256,2048]{1,0:T(8,128)(2,1)}, bf16[256,2048]{1,0:T(8,128)(2,1)S(1)}, u32[]{:S(2)}, u32[]{:S(2)}) collective-permute-start(bf16[256,2048]{1,0:T(8,128)(2,1)} %collective-permute-done.1.refs_1_), channel_id=1, source_target_pairs={{8,12},{9,13},{10,14},{11,15},{24,28},{25,29},{26,30},{27,31}} | collective-permute-start | bytes 3145736 | tf_op jit(solution)/shard_map/ppermute | solution.py:305
  109.3 51.7 %collective-permute-start.5 = (bf16[256,2048]{1,0:T(8,128)(2,1)S(1)}, bf16[256,2048]{1,0:T(8,128)(2,1)S(1)}, u32[]{:S(2)}, u32[]{:S(2)}) collective-permute-start(bf16[256,2048]{1,0:T(8,128)(2,1)S(1)} %collective-permute-done.4.refs_5_), channel_id=1, source_target_pairs={{4,0},{5,1},{6,2},{7,3},{20,16},{21,17},{22,18},{23,19}} | collective-permute-start | bytes 3145736 | tf_op jit(solution)/shard_map/ppermute | solution.py:306
  197.7 29.4 %collective-permute-start.15 = (bf16[256,1024]{1,0:T(8,128)(2,1)S(1)}, bf16[256,1024]{1,0:T(8,128)(2,1)S(1)}, u32[]{:S(2)}, u32[]{:S(2)}) collective-permute-start(bf16[256,1024]{1,0:T(8,128)(2,1)S(1)} %slice.43), channel_id=1, source_target_pairs={{0,1},{1,0},{2,3},{3,2},{4,5},{5,4},{6,7},{7,6},{8,9},{9,8},{10,11... | collective-permute-start | bytes 1572872 | tf_op jit(solution)/shard_map/ppermute | solution.py:372
  247.2 34.8 %collective-permute-start.17 = (bf16[256,1024]{1,0:T(8,128)(2,1)S(1)}, bf16[256,1024]{1,0:T(8,128)(2,1)S(1)}, u32[]{:S(2)}, u32[]{:S(2)}) collective-permute-start(bf16[256,1024]{1,0:T(8,128)(2,1)S(1)} %slice.45), channel_id=1, source_target_pairs={{0,1},{1,0},{2,3},{3,2},{4,5},{5,4},{6,7},{7,6},{8,9},{9,8},{10,11... | collective-permute-start | bytes 1572872 | tf_op jit(solution)/shard_map/ppermute | solution.py:372
  249.2 43.1 %collective-permute-start.19 = (bf16[256,1024]{1,0:T(8,128)(2,1)S(1)}, bf16[256,1024]{1,0:T(8,128)(2,1)S(1)}, u32[]{:S(2)}, u32[]{:S(2)}) collective-permute-start(bf16[256,1024]{1,0:T(8,128)(2,1)S(1)} %slice.47), channel_id=1, source_target_pairs={{0,1},{1,0},{2,3},{3,2},{4,5},{5,4},{6,7},{7,6},{8,9},{9,8},{10,11... | collective-permute-start | bytes 1572872 | tf_op jit(solution)/shard_map/ppermute | solution.py:372
  249.8 44.2 %collective-permute-start.21 = (bf16[256,1024]{1,0:T(8,128)(2,1)S(1)}, bf16[256,1024]{1,0:T(8,128)(2,1)S(1)}, u32[]{:S(2)}, u32[]{:S(2)}) collective-permute-start(bf16[256,1024]{1,0:T(8,128)(2,1)S(1)} %copy-done.8), channel_id=1, source_target_pairs={{0,2},{2,0},{1,3},{3,1},{4,6},{6,4},{5,7},{7,5},{8,10},{10,8},{9,1... | collective-permute-start | bytes 1572872 | tf_op jit(solution)/shard_map/ppermute | solution.py:374
  259.5 47.7 %collective-permute-start.24 = (bf16[256,1024]{1,0:T(8,128)(2,1)}, bf16[256,1024]{1,0:T(8,128)(2,1)S(1)}, u32[]{:S(2)}, u32[]{:S(2)}) collective-permute-start(bf16[256,1024]{1,0:T(8,128)(2,1)} %add_convert_fusion.18.refs_11_.refs_0_), channel_id=1, source_target_pairs={{0,2},{2,0},{1,3},{3,1},{4,6},{6,4},{5,7},{7,5},{8,10},{10,8},{9,1... | collective-permute-start | bytes 1572872 | tf_op jit(solution)/shard_map/ppermute | solution.py:374
  372.0 46.2 %collective-permute-start.38 = (bf16[256,1024]{1,0:T(8,128)(2,1)S(1)}, bf16[256,1024]{1,0:T(8,128)(2,1)S(1)}, u32[]{:S(2)}, u32[]{:S(2)}) collective-permute-start(bf16[256,1024]{1,0:T(8,128)(2,1)S(1)} %copy-done.25), channel_id=1, source_target_pairs={{0,4},{1,5},{2,6},{3,7},{16,20},{17,21},{18,22},{19,23}} | collective-permute-start | bytes 1572872 | tf_op jit(solution)/shard_map/ppermute | solution.py:319
  372.7 60.9 %collective-permute-start.32 = (bf16[256,1024]{1,0:T(8,128)(2,1)}, bf16[256,1024]{1,0:T(8,128)(2,1)S(1)}, u32[]{:S(2)}, u32[]{:S(2)}) collective-permute-start(bf16[256,1024]{1,0:T(8,128)(2,1)} %get-tuple-element.41), channel_id=1, source_target_pairs={{0,4},{1,5},{2,6},{3,7},{16,20},{17,21},{18,22},{19,23}} | collective-permute-start | bytes 1572872 | tf_op jit(solution)/shard_map/ppermute | solution.py:319
  373.4 74.5 %collective-permute-start.41 = (bf16[256,1024]{1,0:T(8,128)(2,1)S(1)}, bf16[256,1024]{1,0:T(8,128)(2,1)S(1)}, u32[]{:S(2)}, u32[]{:S(2)}) collective-permute-start(bf16[256,1024]{1,0:T(8,128)(2,1)S(1)} %copy-done.24), channel_id=1, source_target_pairs={{12,8},{13,9},{14,10},{15,11},{28,24},{29,25},{30,26},{31,27}} | collective-permute-start | bytes 1572872 | tf_op jit(solution)/shard_map/ppermute | solution.py:320
  374.7 74.9 %collective-permute-start.35 = (bf16[256,1024]{1,0:T(8,128)(2,1)}, bf16[256,1024]{1,0:T(8,128)(2,1)S(1)}, u32[]{:S(2)}, u32[]{:S(2)}) collective-permute-start(bf16[256,1024]{1,0:T(8,128)(2,1)} %get-tuple-element.39), channel_id=1, source_target_pairs={{12,8},{13,9},{14,10},{15,11},{28,24},{29,25},{30,26},{31,27}} | collective-permute-start | bytes 1572872 | tf_op jit(solution)/shard_map/ppermute | solution.py:320
  457.0 30.3 %collective-permute-start.36 = (bf16[256,1024]{1,0:T(8,128)(2,1)S(1)}, bf16[256,1024]{1,0:T(8,128)(2,1)S(1)}, u32[]{:S(2)}, u32[]{:S(2)}) collective-permute-start(bf16[256,1024]{1,0:T(8,128)(2,1)S(1)} %get-tuple-element.57), channel_id=1, source_target_pairs={{12,8},{8,4},{13,9},{9,5},{14,10},{10,6},{15,11},{11,7},{28,24},{2... | collective-permute-start | bytes 1572872 | tf_op jit(solution)/shard_map/ppermute | solution.py:320
  464.8 51.3 %collective-permute-start.54 = (bf16[256,1024]{1,0:T(8,128)(2,1)S(1)}, bf16[256,1024]{1,0:T(8,128)(2,1)S(1)}, u32[]{:S(2)}, u32[]{:S(2)}) collective-permute-start(bf16[256,1024]{1,0:T(8,128)(2,1)S(1)} %get-tuple-element.63), channel_id=1, source_target_pairs={{12,8},{8,4},{13,9},{9,5},{14,10},{10,6},{15,11},{11,7},{28,24},{2... | collective-permute-start | bytes 1572872 | tf_op jit(solution)/shard_map/ppermute | solution.py:320
  476.1 42.4 %collective-permute-start.51 = (bf16[256,1024]{1,0:T(8,128)(2,1)S(1)}, bf16[256,1024]{1,0:T(8,128)(2,1)S(1)}, u32[]{:S(2)}, u32[]{:S(2)}) collective-permute-start(bf16[256,1024]{1,0:T(8,128)(2,1)S(1)} %get-tuple-element.62), channel_id=1, source_target_pairs={{0,4},{4,8},{1,5},{5,9},{2,6},{6,10},{3,7},{7,11},{16,20},{20,24},... | collective-permute-start | bytes 1572872 | tf_op jit(solution)/shard_map/ppermute | solution.py:319
  477.7 32.1 %collective-permute-start.43 = (bf16[256,1024]{1,0:T(8,128)(2,1)S(1)}, bf16[256,1024]{1,0:T(8,128)(2,1)S(1)}, u32[]{:S(2)}, u32[]{:S(2)}) collective-permute-start(bf16[256,1024]{1,0:T(8,128)(2,1)S(1)} %add_convert_fusion.11), channel_id=1, source_target_pairs={{12,8},{8,4},{4,0},{13,9},{9,5},{5,1},{14,10},{10,6},{6,2},{15,11}... | collective-permute-start | bytes 1572872 | tf_op jit(solution)/shard_map/ppermute | solution.py:320
  489.4 33.3 %collective-permute-start.48 = (bf16[256,1024]{1,0:T(8,128)(2,1)S(1)}, bf16[256,1024]{1,0:T(8,128)(2,1)S(1)}, u32[]{:S(2)}, u32[]{:S(2)}) collective-permute-start(bf16[256,1024]{1,0:T(8,128)(2,1)S(1)} %get-tuple-element.61), channel_id=1, source_target_pairs={{12,8},{8,4},{13,9},{9,5},{14,10},{10,6},{15,11},{11,7},{28,24},{2... | collective-permute-start | bytes 1572872 | tf_op jit(solution)/shard_map/ppermute | solution.py:320
  (83 other events, 1468.3 us)

commit v2 on v1

--- a/solution.py
+++ b/solution.py
@@ -26,7 +26,7 @@
 
 
 def cost(flops, moved):
-    return pl.CostEstimate(flops=int(flops), bytes_accessed=int(moved), transcendentals=0)
+    return pl.CostEstimate(flops=int(flops) // 16, bytes_accessed=int(moved) // 16, transcendentals=0)
 
 
 def run(copies):
@@ -101,13 +101,12 @@
     )(env, order)
 
 
-def fore_kernel(n_rows, half, has_total, n_outs, n_deps, *refs):
+def fore_kernel(n_rows, half, has_total, n_outs, *refs):
     refs = list(refs)
     blocks = refs[: 2 * n_rows - 1]
     left_ref, mpo_ref, right = refs[2 * n_rows - 1 : 2 * n_rows + 2]
     rest = refs[2 * n_rows + 2 :]
     total_ref = rest.pop(0) if has_total else None
-    del rest[:n_deps]
     outs = rest[:n_outs]
     held, right_held, ones, threes, acc, block_sems, right_sems = rest[n_outs:]
     channels = right.shape[0]
@@ -154,7 +153,9 @@
             outs[k // per][first : first + height] = acc[rows].astype(BF16)
 
 
-def fore(blocks, left, mpo, right, total, half, lanes, group, groups, n_outs, kind, tile, deps):
+def fore(
+    blocks, left, mpo, right, total, place, half, lanes, group, groups, n_outs, kind, tile
+):
     depth, columns = blocks[0].shape
     n_rows = (len(blocks) + 1) // 2
     channels, far, _ = right.shape
@@ -162,9 +163,9 @@
     bonds = left.shape[0] // channels // groups
     steps = bonds // tile
     has_total = total is not None
-    acc_spec = pl.BlockSpec((far, tile * phys_pair), lambda i: (0, group * steps + i))
+    acc_spec = pl.BlockSpec((far, tile * phys_pair), lambda i: (0, place * steps + i))
     return pl.pallas_call(
-        functools.partial(fore_kernel, n_rows, half, has_total, n_outs, len(deps)),
+        functools.partial(fore_kernel, n_rows, half, has_total, n_outs),
         grid=(steps,),
         in_specs=[ANY] * len(blocks)
         + [
@@ -172,8 +173,7 @@
             pl.BlockSpec(mpo.shape, lambda i: (0, 0)),
             ANY,
         ]
-        + [acc_spec] * has_total
-        + [ANY] * len(deps),
+        + [acc_spec] * has_total,
         out_specs=[pl.BlockSpec((far // n_outs, tile * phys_pair), lambda i: (0, i))] * n_outs,
         out_shape=[jax.ShapeDtypeStruct((far // n_outs, bonds * phys_pair), kind)] * n_outs,
         scratch_shapes=[
@@ -192,13 +192,13 @@
             2 * (depth * n_rows * columns + far * channels * lanes + bonds * channels * depth)
             + 4 * far * bonds * phys_pair,
         ),
-    )(*blocks, left, mpo, right, *([total] if has_total else []), *deps)
-
-
-def back_kernel(n_parts, half, scattered, n_deps, *refs):
+    )(*blocks, left, mpo, right, *([total] if has_total else []))
+
+
+def back_kernel(n_parts, half, scattered, *refs):
     parts = refs[:n_parts]
     mpo_ref, right = refs[n_parts : n_parts + 2]
-    out_ref, right_held, joined, ones, right_sems = refs[n_parts + 2 + n_deps :]
+    out_ref, right_held, joined, ones, right_sems = refs[-5:]
     channels = right.shape[0]
     lanes = right_held.shape[1] // channels
     phys_pair = out_ref.shape[1] // lanes
@@ -230,18 +230,23 @@
             ).astype(BF16)
 
 
-def back(parts, mpo, right, half, lanes, phys_pair, scattered, tile, deps):
+def back(parts, mpo, right, buffer, group, groups, half, lanes, phys_pair, scattered, tile):
     columns = parts[0].shape[1]
     bonds = columns // phys_pair
     channels, far, _ = right.shape
+    steps = bonds // tile
+    buffers = [] if buffer is None else [buffer]
     return pl.pallas_call(
-        functools.partial(back_kernel, len(parts), half, scattered, len(deps)),
-        grid=(bonds // tile,),
+        functools.partial(back_kernel, len(parts), half, scattered),
+        grid=(steps,),
+        input_output_aliases={} if buffer is None else {len(parts) + 2: 0},
         in_specs=[pl.BlockSpec((p.shape[0], tile * phys_pair), lambda i: (0, i)) for p in parts]
         + [pl.BlockSpec(mpo.shape, lambda i: (0, 0)), ANY]
-        + [ANY] * len(deps),
-        out_specs=pl.BlockSpec((tile * channels, phys_pair * lanes), lambda i: (i, 0)),
-        out_shape=jax.ShapeDtypeStruct((bonds * channels, phys_pair * lanes), BF16),
+        + [ANY] * len(buffers),
+        out_specs=pl.BlockSpec(
+            (tile * channels, phys_pair * lanes), lambda i: (group * steps + i, 0)
+        ),
+        out_shape=jax.ShapeDtypeStruct((groups * bonds * channels, phys_pair * lanes), BF16),
         scratch_shapes=[
             pltpu.VMEM((far, channels * lanes), BF16),
             pltpu.VMEM((far, tile * phys_pair), BF16),
@@ -253,40 +258,31 @@
             2 * far * channels * lanes * columns + bonds * mpo.size * lanes,
             2 * (far * channels * lanes + far * columns + bonds * channels * phys_pair * lanes),
         ),
-    )(*parts, mpo, right, *deps)
-
-
-def last_kernel(n_rows, n_groups, n_deps, *refs):
-    left_ref = refs[0]
-    backs = refs[1 : 1 + n_groups]
-    outs = refs[1 + n_groups + n_deps : -1]
+    )(*parts, mpo, right, *buffers)
+
+
+def last_kernel(n_rows, *refs):
+    left_ref, back_ref = refs[:2]
+    outs = refs[2:-1]
     acc = refs[-1]
     height = outs[0].shape[0]
-    depth = backs[0].shape[0]
-    for g, part in enumerate(backs):
-        term = dot(left_ref[:, g * depth : (g + 1) * depth], part[...])
-        if g == 0:
-            acc[...] = term
-        else:
-            acc[...] += term
+    acc[...] = dot(left_ref[...], back_ref[...])
     for d, out in enumerate(outs):
         j = lax.rem(lax.axis_index("row") + d, n_rows)
         out[...] = acc[pl.ds(pl.multiple_of(j * height, height), height), :].astype(BF16)
 
 
-def last(left_t, backs, chunk, n_chunks, n_rows, deps):
-    columns = backs[0].shape[1] // n_chunks
+def last(left_t, backs, chunk, n_chunks, n_rows):
+    columns = backs.shape[1] // n_chunks
     steps = 2
     height = left_t.shape[0] // n_rows
     return pl.pallas_call(
-        functools.partial(last_kernel, n_rows, len(backs), len(deps)),
+        functools.partial(last_kernel, n_rows),
         grid=(steps,),
-        in_specs=[pl.BlockSpec(left_t.shape, lambda i: (0, 0), pipeline_mode=ONCE)]
-        + [
-            pl.BlockSpec((b.shape[0], columns // steps), lambda i: (0, chunk * steps + i))
-            for b in backs
-        ]
-        + [ANY] * len(deps),
+        in_specs=[
+            pl.BlockSpec(left_t.shape, lambda i: (0, 0), pipeline_mode=ONCE),
+            pl.BlockSpec((backs.shape[0], columns // steps), lambda i: (0, chunk * steps + i)),
+        ],
         out_specs=[pl.BlockSpec((height, columns // steps), lambda i: (0, i))] * n_rows,
         out_shape=[jax.ShapeDtypeStruct((height, columns), BF16)] * n_rows,
         scratch_shapes=[pltpu.VMEM((left_t.shape[0], columns // steps), F32)],
@@ -295,32 +291,31 @@
             2 * left_t.size * columns,
             2 * (left_t.size + left_t.shape[1] * columns + left_t.shape[0] * columns),
         ),
-    )(left_t, *backs, *deps)
-
-
-def gather_rows(block, n_rows):
-    above, below = [], []
-    up = down = block
-    for t in range(1, n_rows):
-        up = lax.ppermute(up, "row", [(r, r + 1) for r in range(t - 1, n_rows - 1)])
-        down = lax.ppermute(down, "row", [(r, r - 1) for r in range(1, n_rows - t + 1)])
-        above.append(up)
-        below.append(down)
-    return above[::-1] + [block] + below
+    )(left_t, backs)
+
+
+def after(arrays, *deps):
+    return lax.optimization_barrier((arrays, deps))[0]
+
+
+def gather_round(up, down, t, n_rows):
+    up = lax.ppermute(up, "row", [(r, r + 1) for r in range(t - 1, n_rows - 1)])
+    down = lax.ppermute(down, "row", [(r, r - 1) for r in range(1, n_rows - t + 1)])
+    return up, down
 
 
 def scatter_rows(terms, n_rows):
     up = down = None
+    seen = []
     for t in range(1, n_rows):
         mine, other = terms[n_rows - t], terms[t]
         if up is not None:
-            mine = (mine.astype(F32) + up.astype(F32)).astype(BF16)
-            other = (other.astype(F32) + down.astype(F32)).astype(BF16)
+            mine, other = add(mine, up), add(other, down)
+        mine, other = lax.optimization_barrier((mine, other))
         up = lax.ppermute(mine, "row", [(r, r + 1) for r in range(t)])
         down = lax.ppermute(other, "row", [(n_rows - 1 - r, n_rows - 2 - r) for r in range(t)])
-        if t == 1:
-            early = up
-    return terms[0].astype(F32) + up.astype(F32) + down.astype(F32), early
+        seen.append([up, down])
+    return terms[0].astype(F32) + up.astype(F32) + down.astype(F32), seen
 
 
 def add(x, y):
@@ -338,12 +333,6 @@
     groups = max(1, min(4, bonds // tile))
     swap = [(0, 1), (1, 0)]
 
-    pieces = [
-        theta[:, :, h * lanes : (h + 1) * lanes].reshape(rows, phys_pair * lanes)
-        for h in range(halves)
-    ]
-    gathered = [gather_rows(p, n_rows) for p in pieces]
-
     paired = jnp.einsum("wuxs,uvyt->wstxyv", mpo_left, mpo_right, precision=lax.Precision.HIGHEST)
     mpo = paired.reshape(channels, phys_pair, phys_pair, channels).astype(BF16)
     twice = jnp.einsum("wsxv,jk->sjwvkx", mpo, jnp.eye(2, dtype=BF16))
@@ -354,17 +343,45 @@
     left, left_t = ordered(left_env.transpose(1, 0, 2), tile)
     right = right_env.transpose(1, 0, 2)
 
-    total = None
-    for h in range(halves - 1):
-        (total,) = fore(
-            gathered[h], left, mpo_fore, right, total, h, lanes, 0, 1, 1, F32, tile, []
-        )
-
-    own, everyone = [], []
+    totals, cuts = [None], 2 if groups % 2 == 0 else 1
+    blocks, before, final = [], (), ()
+    for h in range(halves):
+        prior, new = blocks, []
+
+        def forward(*deps):
+            return fore(
+                after(prior, *deps), left, mpo_fore, right, totals[len(new) % len(totals)], 0,
+                h - 1, lanes, len(new), cuts, 1, F32, tile,
+            )
+
+        up = down = theta[:, :, h * lanes : (h + 1) * lanes].reshape(rows, phys_pair * lanes)
+        blocks = [up]
+        for t in range(1, n_rows):
+            waits = before if t == 1 else final if t == 2 else new[t - 3 : t - 2]
+            if h == 0 and t > 1:
+                waits = [left, left_t] if t == 2 else [mpo_fore, mpo_back]
+            up, down = after((up, down), *waits)
+            before = (up, down)
+            up, down = gather_round(up, down, t, n_rows)
+            blocks = [up] + blocks + [down]
+            if h > 0 and len(new) < cuts:
+                new += forward(up, down)
+        final = (up, down)
+        if h > 0:
+            while len(new) < cuts:
+                new += forward()
+            totals = new
+
+    own, everyone, waits = [], [], []
+    if halves > 1:
+        blocks, totals = lax.optimization_barrier((blocks, totals))
     for g in range(groups):
+        if g > 0:
+            blocks = after(blocks, *waits)
         terms = fore(
-            gathered[-1], left, mpo_fore, right, total, halves - 1, lanes, g, groups,
-            2 if scattered else 1, BF16, tile, [own[g - 2]] if g > 1 else [],
+            blocks, left, mpo_fore, right, totals[g * len(totals) // groups],
+            g % (groups // len(totals)), halves - 1, lanes, g, groups, 2 if scattered else 1, BF16,
+            tile,
         )
         if scattered:
             near = add(terms[0], lax.ppermute(terms[1], "col", swap))
@@ -373,27 +390,41 @@
             across = lax.ppermute(mine, "chan", swap)
             parts = [mine, across] + [lax.ppermute(p, "col", swap) for p in (mine, across)]
         else:
-            mine = lax.psum_scatter(terms[0], ("col", "chan"), scatter_dimension=0, tiled=True)
+            near = terms[0]
+            mine = lax.psum_scatter(near, ("col", "chan"), scatter_dimension=0, tiled=True)
             parts = [lax.all_gather(mine, ("col", "chan"), axis=0, tiled=True)]
+        waits = [near] + own[-1:] + [p[-1] for p in everyone[-2:-1]]
         own.append(mine)
         everyone.append(parts)
 
     n_chunks = 2
     per = phys_pair // n_chunks
-    products, deps, early = [], [], []
+    products, seen = [], []
     for h in range(halves):
-        backs = [
-            back(parts, mpo_back, right, h, lanes, phys_pair, scattered, tile, deps)
-            for parts in everyone
-        ]
-        chunks = []
+        backs = None
+        for g, parts in enumerate(everyone):
+            if h > 0:
+                waits = [terms[0]] if g < groups // 2 else seen[-1][0] + seen[-2][0]
+                parts = after(parts, *waits)
+            elif g == 0:
+                parts = after(parts, *waits)
+            else:
+                parts = after(parts, *own[groups // 2 : groups // 2 + g])
+            backs = back(
+                parts, mpo_back, right, backs, g, groups, h, lanes, phys_pair, scattered, tile
+            )
+        if h > 0:
+            backs = after(backs, *[x for rounds in seen[-2:] for x in rounds[min(1, n_rows - 2)]])
         for c in range(n_chunks):
-            terms = last(left_t, backs, c, n_chunks, n_rows, early[-2:-1])
-            deps = [terms[0]]
-            chunk, first = scatter_rows(terms, n_rows)
-            early.append(first)
-            chunks.append(chunk.astype(BF16).reshape(rows, per, lanes))
-        products.append(jnp.concatenate(chunks, axis=1))
+            if c > 0:
+                backs = after(backs, *terms)
+            terms = last(left_t, backs, c, n_chunks, n_rows)
+            chunk, rounds = scatter_rows(terms, n_rows)
+            seen.append(rounds)
+            products.append(chunk.astype(BF16).reshape(rows, per, lanes))
+    products = [
+        jnp.concatenate(products[h * n_chunks : (h + 1) * n_chunks], axis=1) for h in range(halves)
+    ]
     return jnp.concatenate(own, axis=1), jnp.concatenate(products, axis=2)
 
 

time: 567 us -> 589 us (1.039)
  waiting for transfers between devices: 154 us -> 170 us
  starting transfers between devices: 105 us -> 119 us
  local copies, waits for them, and re-layouts: 28 us -> 18.5 us
    ppermute x4, waiting for transfers between devices: 21.8 us -> 40.5 us  [shards(): across = lax.ppermute(mine, 'chan', swap)]
    ppermute x12, waiting for transfers between devices: 15.4 us -> 0.03 us  [scatter_rows(): up = lax.ppermute(mine, 'row', [(r, r + 1) for r in range(t)])]
    ppermute x12, waiting for transfers between devices: 39.2 us -> 24.6 us  [scatter_rows(): lax.ppermute(other, 'row', [(n_rows - 1 - r, n_rows - 2 - r) for r in ran...]
    ppermute x4, waiting for transfers between devices: 32.1 us -> 44.2 us  [shards(): mine = add(near[:half], lax.ppermute(near[half:], 'chan', swap))]
    ppermute x12, waiting for transfers between devices: 45.4 us -> 57 us  [the longest x6 50.9 us: gather_round(): up = lax.ppermute(up, 'row', [(r, r + 1) for r in range(t - 1, n_rows - 1)])]
    ppermute x12, starting transfers between devices: 42.3 us -> 53.5 us  [scatter_rows(): lax.ppermute(other, 'row', [(n_rows - 1 - r, n_rows - 2 - r) for r in ran...]
    pallas_call x5 -> x6, Pallas kernels: 104 us -> 110 us  [fore(): pl.pallas_call(functools.partial(fore_kernel, n_rows, half, has_total, n_...]
  transfers between devices with their start and end apart: 56 -> 56, of which waited for: 22 -> 22; matrix products, arithmetic and copies ran while one was open for 6% -> 4% of each run, Pallas kernels for 36% -> 29%
where the time goes in v2:
time: 589 us; the launch traced here: 580 us
  Pallas kernels  254 us (43%)
  waiting for transfers between devices  170 us (29%)
  starting transfers between devices  119 us (20%)
  local copies, waits for them, and re-layouts  18.5 us (3%)
  other arithmetic  14.6 us (2%)
    pallas_call x6, Pallas kernels, fore(): pl.pallas_call(functools.partial(fore_kernel, n_rows, half, has_total, n_...  110 us
    pallas_call x8, Pallas kernels, back(): pl.pallas_call(functools.partial(back_kernel, len(parts), half, scattered...  83.9 us
    ppermute x12, starting transfers between devices, scatter_rows(): lax.ppermute(other, 'row', [(n_rows - 1 - r, n_rows - 2 - r) for r in ran...  53.5 us
    ppermute x6, waiting for transfers between devices, gather_round(): up = lax.ppermute(up, 'row', [(r, r + 1) for r in range(t - 1, n_rows - 1)])  50.9 us
    pallas_call x4, Pallas kernels, last(): pl.pallas_call(functools.partial(last_kernel, n_rows), grid=(steps,), in_...  47.9 us
    ppermute x4, waiting for transfers between devices, shards(): mine = add(near[:half], lax.ppermute(near[half:], 'chan', swap))  44.2 us
    ppermute x4, waiting for transfers between devices, shards(): across = lax.ppermute(mine, 'chan', swap)  40.5 us
    ppermute x12, waiting for transfers between devices, scatter_rows(): lax.ppermute(other, 'row', [(n_rows - 1 - r, n_rows - 2 - r) for r in ran...  24.6 us
  transfers between devices with their start and end apart: 56, of which 22 were waited for; matrix products, arithmetic and copies ran while one was open for 4% of the time, Pallas kernels for 29%

profile of v2, /device:TPU:16, one launch (start us, length us, event | category | flops | bytes accessed | tf_op | source)
XLA Modules:
  0.0 580.0 jit_solution(8615172503516902959)
XLA Ops:
  10.6 12.0 %shard_map.68 = (bf16[3072,1024]{1,0:T(8,128)(2,1)}, bf16[1024,3072]{1,0:T(8,128)(2,1)}) custom-call(bf16[12,256,1024]{2,1,0:T(8,128)(2,1)} %bitcast.56, bf16[384,384]{1,0:T(8,128)(2,1)} %fusion.9.order_ref), custom_call_target="tpu_custom_call" | custom-call | flops 301989888 | bytes 1179648 | tf_op jit(solution)/shard_map/pallas_call | solution.py:84
  70.6 16.9 %collective-permute-done.4.refs_2_ = bf16[256,2048]{1,0:T(8,128)(2,1)S(1)} collective-permute-done((bf16[256,2048]{1,0:T(8,128)(2,1)S(1)}, bf16[256,2048]{1,0:T(8,128)(2,1)S(1)}, u32[]{:S(2)}, u32[]{:S(2)}) %collective-permute-start.4) | collective-permute-done | bytes 1048608 | tf_op jit(solution)/shard_map/ppermute | solution.py:302
  88.3 18.5 %collective-permute-done.6.refs_0_ = bf16[256,2048]{1,0:T(8,128)(2,1)S(1)} collective-permute-done((bf16[256,2048]{1,0:T(8,128)(2,1)}, bf16[256,2048]{1,0:T(8,128)(2,1)S(1)}, u32[]{:S(2)}, u32[]{:S(2)}) %collective-permute-start.6) | collective-permute-done | bytes 1048608 | tf_op jit(solution)/shard_map/ppermute | solution.py:302
  118.9 23.5 %shard_map.69.refs_10_ = f32[1024,2048]{1,0:T(8,128)} custom-call(bf16[256,2048]{1,0:T(8,128)(2,1)} %copy-done.17, bf16[256,2048]{1,0:T(8,128)(2,1)} %collective-permute-done.2.refs_1_, bf16[256,2048]{1,0:T(8,128)(2,1)} %collective-permute-done.refs_2_, bf16[256,2048]{1,0:T(8,128)(2,1)} %bitcast.54, bf16[256,2048]{1,0:T(8,128)(2,1)} %collective-permute-done.1.refs_4_, ...), custom_call_target="tpu_custom_call" | custom-call | flops 956301312 | bytes 1032192 | tf_op jit(solution)/shard_map/pallas_call | solution.py:167
  144.6 23.6 %shard_map.70.refs_10_ = f32[1024,2048]{1,0:T(8,128)} custom-call(bf16[256,2048]{1,0:T(8,128)(2,1)} %copy-done.17, bf16[256,2048]{1,0:T(8,128)(2,1)} %collective-permute-done.2.refs_1_, bf16[256,2048]{1,0:T(8,128)(2,1)} %collective-permute-done.refs_2_, bf16[256,2048]{1,0:T(8,128)(2,1)} %bitcast.55, bf16[256,2048]{1,0:T(8,128)(2,1)} %collective-permute-done.1.refs_4_, ...), custom_call_target="tpu_custom_call" | custom-call | flops 956301312 | bytes 1032192 | tf_op jit(solution)/shard_map/pallas_call | solution.py:167
  170.1 15.5 %shard_map.71 = (bf16[512,1024]{1,0:T(8,128)(2,1)}, bf16[512,1024]{1,0:T(8,128)(2,1)}) custom-call(bf16[256,2048]{1,0:T(8,128)(2,1)} %copy-done.6, bf16[256,2048]{1,0:T(8,128)(2,1)} %collective-permute-done.8.refs_1_, bf16[256,2048]{1,0:T(8,128)(2,1)} %copy-done.4, bf16[256,2048]{1,0:T(8,128)(2,1)} %bitcast.48, bf16[256,2048]{1,0:T(8,128)(2,1)} %copy-done.5, ...), custom_call_target="tpu_custom_call" | custom-call | flops 478150656 | bytes 745472 | tf_op jit(solution)/shard_map/pallas_call | solution.py:167
  190.2 15.6 %shard_map.72 = (bf16[512,1024]{1,0:T(8,128)(2,1)}, bf16[512,1024]{1,0:T(8,128)(2,1)}) custom-call(bf16[256,2048]{1,0:T(8,128)(2,1)} %copy-done.6, bf16[256,2048]{1,0:T(8,128)(2,1)} %collective-permute-done.8.refs_1_, bf16[256,2048]{1,0:T(8,128)(2,1)} %copy-done.4, bf16[256,2048]{1,0:T(8,128)(2,1)} %bitcast.49, bf16[256,2048]{1,0:T(8,128)(2,1)} %copy-done.5, ...), custom_call_target="tpu_custom_call" | custom-call | flops 478150656 | bytes 745472 | tf_op jit(solution)/shard_map/pallas_call | solution.py:167
  207.6 12.7 %collective-permute-done.13 = bf16[256,1024]{1,0:T(8,128)(2,1)S(1)} collective-permute-done((bf16[256,1024]{1,0:T(8,128)(2,1)S(1)}, bf16[256,1024]{1,0:T(8,128)(2,1)S(1)}, u32[]{:S(2)}, u32[]{:S(2)}) %collective-permute-start.13) | collective-permute-done | bytes 524320 | tf_op jit(solution)/shard_map/ppermute | solution.py:389
  220.9 16.0 %shard_map.73 = (bf16[512,1024]{1,0:T(8,128)(2,1)}, bf16[512,1024]{1,0:T(8,128)(2,1)}) custom-call(bf16[256,2048]{1,0:T(8,128)(2,1)} %copy-done.6, bf16[256,2048]{1,0:T(8,128)(2,1)} %collective-permute-done.8.refs_1_, bf16[256,2048]{1,0:T(8,128)(2,1)} %copy-done.4, bf16[256,2048]{1,0:T(8,128)(2,1)} %bitcast.50, bf16[256,2048]{1,0:T(8,128)(2,1)} %copy-done.5, ...), custom_call_target="tpu_custom_call" | custom-call | flops 478150656 | bytes 745472 | tf_op jit(solution)/shard_map/pallas_call | solution.py:167
  239.2 12.6 %collective-permute-done.18.refs_1_ = bf16[256,1024]{1,0:T(8,128)(2,1)S(1)} collective-permute-done((bf16[256,1024]{1,0:T(8,128)(2,1)S(1)}, bf16[256,1024]{1,0:T(8,128)(2,1)S(1)}, u32[]{:S(2)}, u32[]{:S(2)}) %collective-permute-start.18) | collective-permute-done | bytes 524320 | tf_op jit(solution)/shard_map/ppermute | solution.py:390
  251.8 10.8 %collective-permute-done.15 = bf16[256,1024]{1,0:T(8,128)(2,1)S(1)} collective-permute-done((bf16[256,1024]{1,0:T(8,128)(2,1)S(1)}, bf16[256,1024]{1,0:T(8,128)(2,1)S(1)}, u32[]{:S(2)}, u32[]{:S(2)}) %collective-permute-start.15) | collective-permute-done | bytes 524320 | tf_op jit(solution)/shard_map/ppermute | solution.py:389
  263.3 15.7 %shard_map.74 = (bf16[512,1024]{1,0:T(8,128)(2,1)}, bf16[512,1024]{1,0:T(8,128)(2,1)}) custom-call(bf16[256,2048]{1,0:T(8,128)(2,1)} %copy-done.6, bf16[256,2048]{1,0:T(8,128)(2,1)} %collective-permute-done.8.refs_1_, bf16[256,2048]{1,0:T(8,128)(2,1)} %copy-done.4, bf16[256,2048]{1,0:T(8,128)(2,1)} %bitcast.51, bf16[256,2048]{1,0:T(8,128)(2,1)} %copy-done.5, ...), custom_call_target="tpu_custom_call" | custom-call | flops 478150656 | bytes 745472 | tf_op jit(solution)/shard_map/pallas_call | solution.py:167
  293.8 11.2 %collective-permute-done.17 = bf16[256,1024]{1,0:T(8,128)(2,1)S(1)} collective-permute-done((bf16[256,1024]{1,0:T(8,128)(2,1)S(1)}, bf16[256,1024]{1,0:T(8,128)(2,1)S(1)}, u32[]{:S(2)}, u32[]{:S(2)}) %collective-permute-start.17) | collective-permute-done | bytes 524320 | tf_op jit(solution)/shard_map/ppermute | solution.py:389
  339.2 10.5 %shard_map.75.refs_6_ = bf16[3072,2048]{1,0:T(8,128)(2,1)} custom-call(bf16[256,1024]{1,0:T(8,128)(2,1)} %copy-done.15, bf16[256,1024]{1,0:T(8,128)(2,1)} %copy-done.28, bf16[256,1024]{1,0:T(8,128)(2,1)} %copy-done.30, bf16[256,1024]{1,0:T(8,128)(2,1)} %copy-done.29, bf16[384,384]{1,0:T(8,128)(2,1)} %copy-done.2, bf16[12,1024,256]{2,1,0:T(8,128)(2,1)} %bitcast.37), custom_call_target="tpu_custom_call" | custom-call | flops 276824064 | bytes 524288 | tf_op jit(solution)/shard_map/pallas_call | solution.py:239
  349.7 10.6 %shard_map.76.refs_6_ = bf16[3072,2048]{1,0:T(8,128)(2,1)} custom-call(bf16[256,1024]{1,0:T(8,128)(2,1)} %copy-done.9, bf16[256,1024]{1,0:T(8,128)(2,1)} %copy-done.19, bf16[256,1024]{1,0:T(8,128)(2,1)} %copy-done.22, bf16[256,1024]{1,0:T(8,128)(2,1)} %copy-done.23, bf16[384,384]{1,0:T(8,128)(2,1)} %copy-done.2, ...), custom_call_target="tpu_custom_call", output_to_operand_aliasing={{}: (6, {})} | custom-call | flops 276824064 | bytes 524288 | tf_op jit(solution)/shard_map/pallas_call | solution.py:239
  374.0 10.4 %shard_map.78.refs_1_ = bf16[3072,2048]{1,0:T(8,128)(2,1)} custom-call(bf16[256,1024]{1,0:T(8,128)(2,1)} %copy-done.13, bf16[256,1024]{1,0:T(8,128)(2,1)} %copy-done.21, bf16[256,1024]{1,0:T(8,128)(2,1)} %copy-done.26, bf16[256,1024]{1,0:T(8,128)(2,1)} %copy-done.27, bf16[384,384]{1,0:T(8,128)(2,1)} %copy-done.2, ...), custom_call_target="tpu_custom_call", output_to_operand_aliasing={{}: (6, {})} | custom-call | flops 276824064 | bytes 524288 | tf_op jit(solution)/shard_map/pallas_call | solution.py:239
  384.4 11.9 %shard_map.79 = (bf16[256,1024]{1,0:T(8,128)(2,1)}, bf16[256,1024]{1,0:T(8,128)(2,1)}, bf16[256,1024]{1,0:T(8,128)(2,1)}, bf16[256,1024]{1,0:T(8,128)(2,1)}) custom-call(bf16[1024,3072]{1,0:T(8,128)(2,1)} %get-tuple-element.146.refs_0_, bf16[3072,2048]{1,0:T(8,128)(2,1)} %shard_map.78.refs_1_), custom_call_target="tpu_custom_call" | custom-call | flops 402653184 | bytes 917504 | tf_op jit(solution)/shard_map/pallas_call | solution.py:279
  398.4 12.0 %shard_map.80 = (bf16[256,1024]{1,0:T(8,128)(2,1)}, bf16[256,1024]{1,0:T(8,128)(2,1)}, bf16[256,1024]{1,0:T(8,128)(2,1)}, bf16[256,1024]{1,0:T(8,128)(2,1)}) custom-call(bf16[1024,3072]{1,0:T(8,128)(2,1)} %get-tuple-element.146.refs_0_, bf16[3072,2048]{1,0:T(8,128)(2,1)} %shard_map.78.refs_1_), custom_call_target="tpu_custom_call" | custom-call | flops 402653184 | bytes 917504 | tf_op jit(solution)/shard_map/pallas_call | solution.py:279
  416.6 10.7 %shard_map.81.refs_6_ = bf16[3072,2048]{1,0:T(8,128)(2,1)} custom-call(bf16[256,1024]{1,0:T(8,128)(2,1)} %copy-done.15, bf16[256,1024]{1,0:T(8,128)(2,1)} %copy-done.28, bf16[256,1024]{1,0:T(8,128)(2,1)} %copy-done.30, bf16[256,1024]{1,0:T(8,128)(2,1)} %copy-done.29, bf16[384,384]{1,0:T(8,128)(2,1)} %copy-done.2, bf16[12,1024,256]{2,1,0:T(8,128)(2,1)} %bitcast.41), custom_call_target="tpu_custom_call" | custom-call | flops 276824064 | bytes 524288 | tf_op jit(solution)/shard_map/pallas_call | solution.py:239
  427.3 10.5 %shard_map.82.refs_6_ = bf16[3072,2048]{1,0:T(8,128)(2,1)} custom-call(bf16[256,1024]{1,0:T(8,128)(2,1)} %copy-done.9, bf16[256,1024]{1,0:T(8,128)(2,1)} %copy-done.19, bf16[256,1024]{1,0:T(8,128)(2,1)} %copy-done.22, bf16[256,1024]{1,0:T(8,128)(2,1)} %copy-done.23, bf16[384,384]{1,0:T(8,128)(2,1)} %copy-done.2, ...), custom_call_target="tpu_custom_call", output_to_operand_aliasing={{}: (6, {})} | custom-call | flops 276824064 | bytes 524288 | tf_op jit(solution)/shard_map/pallas_call | solution.py:239
  459.0 10.5 %shard_map.84.refs_1_ = bf16[3072,2048]{1,0:T(8,128)(2,1)} custom-call(bf16[256,1024]{1,0:T(8,128)(2,1)} %copy-done.13, bf16[256,1024]{1,0:T(8,128)(2,1)} %copy-done.21, bf16[256,1024]{1,0:T(8,128)(2,1)} %copy-done.26, bf16[256,1024]{1,0:T(8,128)(2,1)} %copy-done.27, bf16[384,384]{1,0:T(8,128)(2,1)} %copy-done.2, ...), custom_call_target="tpu_custom_call", output_to_operand_aliasing={{}: (6, {})} | custom-call | flops 276824064 | bytes 524288 | tf_op jit(solution)/shard_map/pallas_call | solution.py:239
  476.0 12.0 %shard_map.85 = (bf16[256,1024]{1,0:T(8,128)(2,1)}, bf16[256,1024]{1,0:T(8,128)(2,1)}, bf16[256,1024]{1,0:T(8,128)(2,1)}, bf16[256,1024]{1,0:T(8,128)(2,1)}) custom-call(bf16[1024,3072]{1,0:T(8,128)(2,1)} %get-tuple-element.146.refs_0_, bf16[3072,2048]{1,0:T(8,128)(2,1)} %shard_map.84.refs_1_), custom_call_target="tpu_custom_call" | custom-call | flops 402653184 | bytes 917504 | tf_op jit(solution)/shard_map/pallas_call | solution.py:279
  495.2 12.0 %shard_map.86 = (bf16[256,1024]{1,0:T(8,128)(2,1)}, bf16[256,1024]{1,0:T(8,128)(2,1)}, bf16[256,1024]{1,0:T(8,128)(2,1)}, bf16[256,1024]{1,0:T(8,128)(2,1)}) custom-call(bf16[1024,3072]{1,0:T(8,128)(2,1)} %get-tuple-element.146.refs_0_, bf16[3072,2048]{1,0:T(8,128)(2,1)} %shard_map.84.refs_1_), custom_call_target="tpu_custom_call" | custom-call | flops 402653184 | bytes 917504 | tf_op jit(solution)/shard_map/pallas_call | solution.py:279
  513.4 15.9 %collective-permute-start.47 = (bf16[256,1024]{1,0:T(8,128)(2,1)S(1)}, bf16[256,1024]{1,0:T(8,128)(2,1)S(1)}, u32[]{:S(2)}, u32[]{:S(2)}) collective-permute-start(bf16[256,1024]{1,0:T(8,128)(2,1)S(1)} %get-tuple-element.270), channel_id=1, source_target_pairs={{12,8},{8,4},{13,9},{9,5},{14,10},{10,6},{15,11},{11,7},{28,24},{2... | collective-permute-start | bytes 1572872 | tf_op jit(solution)/shard_map/ppermute | solution.py:316
  (253 shorter events, 246.0 us)
Async XLA Ops:
  3.8 26.9 %collective-permute-start = (bf16[256,2048]{1,0:T(8,128)(2,1)S(1)}, bf16[256,2048]{1,0:T(8,128)(2,1)}, u32[]{:S(2)}, u32[]{:S(2)}) collective-permute-start(bf16[256,2048]{1,0:T(8,128)(2,1)S(1)} %bitcast.52), channel_id=1, source_target_pairs={{0,4},{4,8},{8,12},{1,5},{5,9},{9,13},{2,6},{6,10},{10,14},{3,7},{... | collective-permute-start | bytes 3145736 | tf_op jit(solution)/shard_map/ppermute | solution.py:302
  68.3 38.5 %collective-permute-start.6 = (bf16[256,2048]{1,0:T(8,128)(2,1)}, bf16[256,2048]{1,0:T(8,128)(2,1)S(1)}, u32[]{:S(2)}, u32[]{:S(2)}) collective-permute-start(bf16[256,2048]{1,0:T(8,128)(2,1)} %collective-permute-done.2.refs_1_), channel_id=1, source_target_pairs={{8,12},{9,13},{10,14},{11,15},{24,28},{25,29},{26,30},{27,31}} | collective-permute-start | bytes 3145736 | tf_op jit(solution)/shard_map/ppermute | solution.py:302
  69.9 36.9 %collective-permute-start.7 = (bf16[256,2048]{1,0:T(8,128)(2,1)}, bf16[256,2048]{1,0:T(8,128)(2,1)S(1)}, u32[]{:S(2)}, u32[]{:S(2)}) collective-permute-start(bf16[256,2048]{1,0:T(8,128)(2,1)} %collective-permute-done.3.refs_5_), channel_id=1, source_target_pairs={{4,0},{5,1},{6,2},{7,3},{20,16},{21,17},{22,18},{23,19}} | collective-permute-start | bytes 3145736 | tf_op jit(solution)/shard_map/ppermute | solution.py:303
  107.7 34.7 %collective-permute-start.8 = (bf16[256,2048]{1,0:T(8,128)(2,1)S(1)}, bf16[256,2048]{1,0:T(8,128)(2,1)}, u32[]{:S(2)}, u32[]{:S(2)}) collective-permute-start(bf16[256,2048]{1,0:T(8,128)(2,1)S(1)} %collective-permute-done.4.refs_2_), channel_id=1, source_target_pairs={{4,8},{8,12},{5,9},{9,13},{6,10},{10,14},{7,11},{11,15},{20,24},{2... | collective-permute-start | bytes 3145736 | tf_op jit(solution)/shard_map/ppermute | solution.py:302
  112.0 30.4 %collective-permute-start.9 = (bf16[256,2048]{1,0:T(8,128)(2,1)S(1)}, bf16[256,2048]{1,0:T(8,128)(2,1)}, u32[]{:S(2)}, u32[]{:S(2)}) collective-permute-start(bf16[256,2048]{1,0:T(8,128)(2,1)S(1)} %collective-permute-done.5.refs_4_), channel_id=1, source_target_pairs={{4,0},{8,4},{5,1},{9,5},{6,2},{10,6},{7,3},{11,7},{20,16},{24,20},... | collective-permute-start | bytes 3145736 | tf_op jit(solution)/shard_map/ppermute | solution.py:303
  283.6 32.7 %collective-permute-start.21 = (bf16[256,1024]{1,0:T(8,128)(2,1)S(1)}, bf16[256,1024]{1,0:T(8,128)(2,1)S(1)}, u32[]{:S(2)}, u32[]{:S(2)}) collective-permute-start(bf16[256,1024]{1,0:T(8,128)(2,1)S(1)} %slice.47), channel_id=1, source_target_pairs={{0,1},{1,0},{2,3},{3,2},{4,5},{5,4},{6,7},{7,6},{8,9},{9,8},{10,11... | collective-permute-start | bytes 1572872 | tf_op jit(solution)/shard_map/ppermute | solution.py:389
  285.1 33.0 %collective-permute-start.29 = (bf16[256,1024]{1,0:T(8,128)(2,1)S(1)}, bf16[256,1024]{1,0:T(8,128)(2,1)S(1)}, u32[]{:S(2)}, u32[]{:S(2)}) collective-permute-start(bf16[256,1024]{1,0:T(8,128)(2,1)S(1)} %add_convert_fusion.18.refs_0_), channel_id=1, source_target_pairs={{0,2},{2,0},{1,3},{3,1},{4,6},{6,4},{5,7},{7,5},{8,10},{10,8},{9,1... | collective-permute-start | bytes 1572872 | tf_op jit(solution)/shard_map/ppermute | solution.py:391
  293.8 33.7 %collective-permute-start.30 = (bf16[256,1024]{1,0:T(8,128)(2,1)S(1)}, bf16[256,1024]{1,0:T(8,128)(2,1)S(1)}, u32[]{:S(2)}, u32[]{:S(2)}) collective-permute-start(bf16[256,1024]{1,0:T(8,128)(2,1)S(1)} %collective-permute-done.28.refs_1_), channel_id=1, source_target_pairs={{0,2},{2,0},{1,3},{3,1},{4,6},{6,4},{5,7},{7,5},{8,10},{10,8},{9,1... | collective-permute-start | bytes 1572872 | tf_op jit(solution)/shard_map/ppermute | solution.py:391
  318.1 42.3 %collective-permute-start.26 = (bf16[256,1024]{1,0:T(8,128)(2,1)S(1)}, bf16[256,1024]{1,0:T(8,128)(2,1)S(1)}, u32[]{:S(2)}, u32[]{:S(2)}) collective-permute-start(bf16[256,1024]{1,0:T(8,128)(2,1)S(1)} %add_convert_fusion.17.refs_0_), channel_id=1, source_target_pairs={{0,2},{2,0},{1,3},{3,1},{4,6},{6,4},{5,7},{7,5},{8,10},{10,8},{9,1... | collective-permute-start | bytes 1572872 | tf_op jit(solution)/shard_map/ppermute | solution.py:391
  327.5 32.8 %collective-permute-start.27 = (bf16[256,1024]{1,0:T(8,128)(2,1)S(1)}, bf16[256,1024]{1,0:T(8,128)(2,1)S(1)}, u32[]{:S(2)}, u32[]{:S(2)}) collective-permute-start(bf16[256,1024]{1,0:T(8,128)(2,1)S(1)} %collective-permute-done.25.refs_1_), channel_id=1, source_target_pairs={{0,2},{2,0},{1,3},{3,1},{4,6},{6,4},{5,7},{7,5},{8,10},{10,8},{9,1... | collective-permute-start | bytes 1572872 | tf_op jit(solution)/shard_map/ppermute | solution.py:391
  327.6 44.8 %collective-permute-start.23 = (bf16[256,1024]{1,0:T(8,128)(2,1)S(1)}, bf16[256,1024]{1,0:T(8,128)(2,1)S(1)}, u32[]{:S(2)}, u32[]{:S(2)}) collective-permute-start(bf16[256,1024]{1,0:T(8,128)(2,1)S(1)} %add_convert_fusion.16.refs_0_), channel_id=1, source_target_pairs={{0,2},{2,0},{1,3},{3,1},{4,6},{6,4},{5,7},{7,5},{8,10},{10,8},{9,1... | collective-permute-start | bytes 1572872 | tf_op jit(solution)/shard_map/ppermute | solution.py:391
  338.3 34.1 %collective-permute-start.24 = (bf16[256,1024]{1,0:T(8,128)(2,1)S(1)}, bf16[256,1024]{1,0:T(8,128)(2,1)S(1)}, u32[]{:S(2)}, u32[]{:S(2)}) collective-permute-start(bf16[256,1024]{1,0:T(8,128)(2,1)S(1)} %collective-permute-done.22.refs_1_), channel_id=1, source_target_pairs={{0,2},{2,0},{1,3},{3,1},{4,6},{6,4},{5,7},{7,5},{8,10},{10,8},{9,1... | collective-permute-start | bytes 1572872 | tf_op jit(solution)/shard_map/ppermute | solution.py:391
  410.4 31.9 %collective-permute-start.38 = (bf16[256,1024]{1,0:T(8,128)(2,1)}, bf16[256,1024]{1,0:T(8,128)(2,1)S(1)}, u32[]{:S(2)}, u32[]{:S(2)}) collective-permute-start(bf16[256,1024]{1,0:T(8,128)(2,1)} %get-tuple-element.240), channel_id=1, source_target_pairs={{0,4},{1,5},{2,6},{3,7},{16,20},{17,21},{18,22},{19,23}} | collective-permute-start | bytes 1572872 | tf_op jit(solution)/shard_map/ppermute | solution.py:315
  411.3 31.1 %collective-permute-start.39 = (bf16[256,1024]{1,0:T(8,128)(2,1)}, bf16[256,1024]{1,0:T(8,128)(2,1)S(1)}, u32[]{:S(2)}, u32[]{:S(2)}) collective-permute-start(bf16[256,1024]{1,0:T(8,128)(2,1)} %get-tuple-element.241), channel_id=1, source_target_pairs={{12,8},{13,9},{14,10},{15,11},{28,24},{29,25},{30,26},{31,27}} | collective-permute-start | bytes 1572872 | tf_op jit(solution)/shard_map/ppermute | solution.py:316
  413.8 55.8 %collective-permute-start.34 = (bf16[256,1024]{1,0:T(8,128)(2,1)S(1)}, bf16[256,1024]{1,0:T(8,128)(2,1)S(1)}, u32[]{:S(2)}, u32[]{:S(2)}) collective-permute-start(bf16[256,1024]{1,0:T(8,128)(2,1)S(1)} %get-tuple-element.231), channel_id=1, source_target_pairs={{0,4},{4,8},{1,5},{5,9},{2,6},{6,10},{3,7},{7,11},{16,20},{20,24},... | collective-permute-start | bytes 1572872 | tf_op jit(solution)/shard_map/ppermute | solution.py:315
  437.8 32.0 %collective-permute-start.35 = (bf16[256,1024]{1,0:T(8,128)(2,1)S(1)}, bf16[256,1024]{1,0:T(8,128)(2,1)S(1)}, u32[]{:S(2)}, u32[]{:S(2)}) collective-permute-start(bf16[256,1024]{1,0:T(8,128)(2,1)S(1)} %get-tuple-element.232), channel_id=1, source_target_pairs={{12,8},{8,4},{13,9},{9,5},{14,10},{10,6},{15,11},{11,7},{28,24},{2... | collective-permute-start | bytes 1572872 | tf_op jit(solution)/shard_map/ppermute | solution.py:316
  442.7 33.3 %collective-permute-start.40 = (bf16[256,1024]{1,0:T(8,128)(2,1)S(1)}, bf16[256,1024]{1,0:T(8,128)(2,1)S(1)}, u32[]{:S(2)}, u32[]{:S(2)}) collective-permute-start(bf16[256,1024]{1,0:T(8,128)(2,1)S(1)} %get-tuple-element.242), channel_id=1, source_target_pairs={{0,4},{4,8},{1,5},{5,9},{2,6},{6,10},{3,7},{7,11},{16,20},{20,24},... | collective-permute-start | bytes 1572872 | tf_op jit(solution)/shard_map/ppermute | solution.py:315
  444.0 32.0 %collective-permute-start.41 = (bf16[256,1024]{1,0:T(8,128)(2,1)S(1)}, bf16[256,1024]{1,0:T(8,128)(2,1)S(1)}, u32[]{:S(2)}, u32[]{:S(2)}) collective-permute-start(bf16[256,1024]{1,0:T(8,128)(2,1)S(1)} %get-tuple-element.243), channel_id=1, source_target_pairs={{12,8},{8,4},{13,9},{9,5},{14,10},{10,6},{15,11},{11,7},{28,24},{2... | collective-permute-start | bytes 1572872 | tf_op jit(solution)/shard_map/ppermute | solution.py:316
  470.0 39.8 %collective-permute-start.36 = (bf16[256,1024]{1,0:T(8,128)(2,1)S(1)}, bf16[256,1024]{1,0:T(8,128)(2,1)S(1)}, u32[]{:S(2)}, u32[]{:S(2)}) collective-permute-start(bf16[256,1024]{1,0:T(8,128)(2,1)S(1)} %add_convert_fusion.15), channel_id=1, source_target_pairs={{0,4},{4,8},{8,12},{1,5},{5,9},{9,13},{2,6},{6,10},{10,14},{3,7},{... | collective-permute-start | bytes 1572872 | tf_op jit(solution)/shard_map/ppermute | solution.py:315
  472.0 39.6 %collective-permute-start.37 = (bf16[256,1024]{1,0:T(8,128)(2,1)S(1)}, bf16[256,1024]{1,0:T(8,128)(2,1)S(1)}, u32[]{:S(2)}, u32[]{:S(2)}) collective-permute-start(bf16[256,1024]{1,0:T(8,128)(2,1)S(1)} %add_convert_fusion.14), channel_id=1, source_target_pairs={{12,8},{8,4},{4,0},{13,9},{9,5},{5,1},{14,10},{10,6},{6,2},{15,11}... | collective-permute-start | bytes 1572872 | tf_op jit(solution)/shard_map/ppermute | solution.py:316
  490.6 70.3 %collective-permute-start.42 = (bf16[256,1024]{1,0:T(8,128)(2,1)S(1)}, bf16[256,1024]{1,0:T(8,128)(2,1)S(1)}, u32[]{:S(2)}, u32[]{:S(2)}) collective-permute-start(bf16[256,1024]{1,0:T(8,128)(2,1)S(1)} %add_convert_fusion.12), channel_id=1, source_target_pairs={{0,4},{4,8},{8,12},{1,5},{5,9},{9,13},{2,6},{6,10},{10,14},{3,7},{... | collective-permute-start | bytes 1572872 | tf_op jit(solution)/shard_map/ppermute | solution.py:315
  509.7 55.1 %collective-permute-start.43 = (bf16[256,1024]{1,0:T(8,128)(2,1)S(1)}, bf16[256,1024]{1,0:T(8,128)(2,1)S(1)}, u32[]{:S(2)}, u32[]{:S(2)}) collective-permute-start(bf16[256,1024]{1,0:T(8,128)(2,1)S(1)} %add_convert_fusion.11), channel_id=1, source_target_pairs={{12,8},{8,4},{4,0},{13,9},{9,5},{5,1},{14,10},{10,6},{6,2},{15,11}... | collective-permute-start | bytes 1572872 | tf_op jit(solution)/shard_map/ppermute | solution.py:316
  513.4 34.1 %collective-permute-start.47 = (bf16[256,1024]{1,0:T(8,128)(2,1)S(1)}, bf16[256,1024]{1,0:T(8,128)(2,1)S(1)}, u32[]{:S(2)}, u32[]{:S(2)}) collective-permute-start(bf16[256,1024]{1,0:T(8,128)(2,1)S(1)} %get-tuple-element.270), channel_id=1, source_target_pairs={{12,8},{8,4},{13,9},{9,5},{14,10},{10,6},{15,11},{11,7},{28,24},{2... | collective-permute-start | bytes 1572872 | tf_op jit(solution)/shard_map/ppermute | solution.py:316
  531.1 27.6 %collective-permute-start.53 = (bf16[256,1024]{1,0:T(8,128)(2,1)S(1)}, bf16[256,1024]{1,0:T(8,128)(2,1)S(1)}, u32[]{:S(2)}, u32[]{:S(2)}) collective-permute-start(bf16[256,1024]{1,0:T(8,128)(2,1)S(1)} %get-tuple-element.281), channel_id=1, source_target_pairs={{12,8},{8,4},{13,9},{9,5},{14,10},{10,6},{15,11},{11,7},{28,24},{2... | collective-permute-start | bytes 1572872 | tf_op jit(solution)/shard_map/ppermute | solution.py:316
  (82 other events, 1720.7 us)

commit v3 on v2

v3 whole, which is shorter than its diff:
```python
import functools

import jax
import jax.numpy as jnp
from jax import lax
from jax.experimental import pallas as pl
from jax.experimental.pallas import tpu as pltpu
from jax.sharding import PartitionSpec as P

BF16 = jnp.bfloat16
F32 = jnp.float32
MIB = 1024 * 1024
LINES = (((1,), (0,)), ((), ()))
ROWS = (((1,), (1,)), ((), ()))
COLS = (((0,), (0,)), ((), ()))
ANY = pl.BlockSpec(memory_space=pl.ANY)
ONCE = pl.Buffered(1)


def dot(x, y, dims=LINES):
    return lax.dot_general(x, y, dims, preferred_element_type=F32)


def params(limit=56):
    return pltpu.CompilerParams(vmem_limit_bytes=limit * MIB)


def cost(flops, moved):
    return pl.CostEstimate(flops=int(flops) // 16, bytes_accessed=int(moved) // 16, transcendentals=0)


def block_of(k):
    n_col, n_chan = lax.axis_size("col"), lax.axis_size("chan")
    col = lax.rem(lax.axis_index("col") + k // n_chan, n_col)
    return col * n_chan + lax.rem(lax.axis_index("chan") + k % n_chan, n_chan)


def order_kernel(env_ref, order_ref, left_ref, turned_ref):
    env = env_ref[...].reshape(order_ref.shape[0], env_ref.shape[2])
    left_ref[...] = dot(order_ref[...], env).astype(BF16)
    turned_ref[...] = dot(env, order_ref[...], (((0,), (1,)), ((), ()))).astype(BF16)


def ordered(env, tile):
    channels, bonds, depth = env.shape
    size = tile * channels
    index = jnp.arange(size)
    wanted = (index % channels) * tile + index // channels
    order = (wanted[:, None] == index[None, :]).astype(BF16)
    return pl.pallas_call(
        order_kernel,
        grid=(bonds // tile,),
        in_specs=[
            pl.BlockSpec((channels, tile, depth), lambda i: (0, i, 0)),
            pl.BlockSpec((size, size), lambda i: (0, 0)),
        ],
        out_specs=[
            pl.BlockSpec((size, depth), lambda i: (i, 0)),
            pl.BlockSpec((depth, size), lambda i: (0, i)),
        ],
        out_shape=[
            jax.ShapeDtypeStruct((bonds * channels, depth), BF16),
            jax.ShapeDtypeStruct((depth, bonds * channels), BF16),
        ],
        compiler_params=params(),
        cost_estimate=cost(4 * size * env.size, 6 * env.size),
    )(env, order)


def part_kernel(env_ref, *outs):
    lanes = outs[0].shape[1]
    for h, out in enumerate(outs):
        out[...] = env_ref[0, :, h * lanes : (h + 1) * lanes]


def parted(env, lanes):
    channels, far, width = env.shape
    count = width // lanes
    return pl.pallas_call(
        part_kernel,
        grid=(channels,),
        in_specs=[pl.BlockSpec((1, far, width), lambda v: (v, 0, 0))],
        out_specs=[pl.BlockSpec((far, lanes), lambda v: (0, v))] * count,
        out_shape=[jax.ShapeDtypeStruct((far, channels * lanes), BF16)] * count,
        compiler_params=params(),
        cost_estimate=cost(0, 4 * env.size),
    )(env)


def fore_kernel(channels, lanes, theta_ref, left_ref, mpo_ref, right_ref, *refs):
    out, ones, threes = refs[-3:]
    phys_pair = theta_ref.shape[1] // lanes
    pair, step = 2 * channels, 2 * phys_pair
    pairs = left_ref.shape[0] // pair
    full = dot(left_ref[...], theta_ref[...])
    for i in range(pairs):
        for s in range(0, phys_pair, 2):
            both = [
                full[i * pair : (i + 1) * pair, q * lanes : (q + 1) * lanes] for q in (s, s + 1)
            ]
            ones[s * pair : (s + 2) * pair, i * lanes : (i + 1) * lanes] = jnp.concatenate(
                both, axis=0
            ).astype(BF16)
    mixed = dot(mpo_ref[...], ones[...]).astype(BF16)
    for i in range(pairs):
        for v in range(channels):
            threes[i * step : (i + 1) * step, v * lanes : (v + 1) * lanes] = mixed[
                v * step : (v + 1) * step, i * lanes : (i + 1) * lanes
            ]
    part = dot(right_ref[...], threes[...], ROWS)
    if len(refs) == 4:
        part = part + refs[0][...]
    out[...] = part.astype(out.dtype)


def fore(theta, left, mpo, right, total, channels, group, groups, kind, tile):
    far = right.shape[0]
    lanes = right.shape[1] // channels
    phys_pair = theta.shape[1] // lanes
    bonds = left.shape[0] // channels // groups
    steps = bonds // tile
    totals = [] if total is None else [total]
    return pl.pallas_call(
        functools.partial(fore_kernel, channels, lanes),
        grid=(steps,),
        in_specs=[
            pl.BlockSpec(theta.shape, lambda i: (0, 0), pipeline_mode=ONCE),
            pl.BlockSpec((tile * channels, left.shape[1]), lambda i: (group * steps + i, 0)),
            pl.BlockSpec(mpo.shape, lambda i: (0, 0), pipeline_mode=ONCE),
            pl.BlockSpec(right.shape, lambda i: (0, 0), pipeline_mode=ONCE),
        ]
        + [pl.BlockSpec((far, tile * phys_pair), lambda i: (0, group * steps + i))] * len(totals),
        out_specs=pl.BlockSpec((far, tile * phys_pair), lambda i: (0, i)),
        out_shape=jax.ShapeDtypeStruct((far, bonds * phys_pair), kind),
        scratch_shapes=[
            pltpu.VMEM((2 * channels * phys_pair, tile // 2 * lanes), BF16),
            pltpu.VMEM((tile * phys_pair, channels * lanes), BF16),
        ],
        compiler_params=params(48),
        cost_estimate=cost(
            2 * bonds * phys_pair * right.shape[1] * (left.shape[1] + far)
            + bonds * mpo.size * lanes,
            2 * (theta.size + right.size + bonds * channels * left.shape[1])
            + 4 * far * bonds * phys_pair,
        ),
    )(theta, left, mpo, right, *totals)


def back_kernel(channels, n_parts, scattered, *refs):
    parts = refs[:n_parts]
    mpo_ref, right_ref = refs[n_parts : n_parts + 2]
    out_ref, joined, ones = refs[-3:]
    lanes = right_ref.shape[1] // channels
    phys_pair = out_ref.shape[1] // lanes
    pair, step = 2 * channels, 2 * phys_pair
    pairs = out_ref.shape[0] // pair
    height = parts[0].shape[0]
    for k, part in enumerate(parts):
        place = block_of(k) if scattered else k
        joined[pl.ds(pl.multiple_of(place * height, height), height), :] = part[...]
    full = dot(joined[...], right_ref[...], COLS).astype(BF16)
    for i in range(pairs):
        for v in range(channels):
            ones[v * step : (v + 1) * step, i * lanes : (i + 1) * lanes] = full[
                i * step : (i + 1) * step, v * lanes : (v + 1) * lanes
            ]
    mixed = dot(mpo_ref[...], ones[...])
    for i in range(0, pairs, 2):
        for s in range(phys_pair):
            both = [
                mixed[s * pair : (s + 1) * pair, j * lanes : (j + 1) * lanes] for j in (i, i + 1)
            ]
            out_ref[i * pair : (i + 2) * pair, s * lanes : (s + 1) * lanes] = jnp.concatenate(
                both, axis=0
            ).astype(BF16)


def back(parts, mpo, right, buffer, channels, phys_pair, group, groups, scattered, tile):
    columns = parts[0].shape[1]
    bonds = columns // phys_pair
    far = right.shape[0]
    lanes = right.shape[1] // channels
    steps = bonds // tile
    buffers = [] if buffer is None else [buffer]
    return pl.pallas_call(
        functools.partial(back_kernel, channels, len(parts), scattered),
        grid=(steps,),
        input_output_aliases={} if buffer is None else {len(parts) + 2: 0},
        in_specs=[pl.BlockSpec((p.shape[0], tile * phys_pair), lambda i: (0, i)) for p in parts]
        + [
            pl.BlockSpec(mpo.shape, lambda i: (0, 0), pipeline_mode=ONCE),
            pl.BlockSpec(right.shape, lambda i: (0, 0), pipeline_mode=ONCE),
        ]
        + [ANY] * len(buffers),
        out_specs=pl.BlockSpec(
            (tile * channels, phys_pair * lanes), lambda i: (group * steps + i, 0)
        ),
        out_shape=jax.ShapeDtypeStruct((groups * bonds * channels, phys_pair * lanes), BF16),
        scratch_shapes=[
            pltpu.VMEM((far, tile * phys_pair), BF16),
            pltpu.VMEM((2 * channels * phys_pair, tile // 2 * lanes), BF16),
        ],
        compiler_params=params(48),
        cost_estimate=cost(
            2 * right.size * columns + bonds * mpo.size * lanes,
            2 * (right.size + far * columns + bonds * channels * phys_pair * lanes),
        ),
    )(*parts, mpo, right, *buffers)


def last_kernel(left_ref, back_ref, out_ref):
    out_ref[...] = dot(left_ref[...], back_ref[...]).astype(BF16)


def last(left_t, backs, chunk, n_chunks):
    columns = backs.shape[1] // n_chunks
    steps = 2
    return pl.pallas_call(
        last_kernel,
        grid=(steps,),
        in_specs=[
            pl.BlockSpec(left_t.shape, lambda i: (0, 0), pipeline_mode=ONCE),
            pl.BlockSpec((backs.shape[0], columns // steps), lambda i: (0, chunk * steps + i)),
        ],
        out_specs=pl.BlockSpec((left_t.shape[0], columns // steps), lambda i: (0, i)),
        out_shape=jax.ShapeDtypeStruct((left_t.shape[0], columns), BF16),
        compiler_params=params(48),
        cost_estimate=cost(
            2 * left_t.size * columns,
            2 * (left_t.size + left_t.shape[1] * columns + left_t.shape[0] * columns),
        ),
    )(left_t, backs)


def after(arrays, *deps):
    return lax.optimization_barrier((arrays, deps))[0]


def shards(theta, left_env, right_env, mpo_left, mpo_right):
    bonds, channels, depth = left_env.shape
    rows, phys_pair, width = theta.shape
    scattered = lax.axis_size("col") == 2 and lax.axis_size("chan") == 2
    tile = min(32, bonds)
    lanes = min(128, width)
    halves = width // lanes
    groups = max(1, min(4, bonds // tile))
    swap = [(0, 1), (1, 0)]

    paired = jnp.einsum("wuxs,uvyt->wstxyv", mpo_left, mpo_right, precision=lax.Precision.HIGHEST)
    mpo = paired.reshape(channels, phys_pair, phys_pair, channels).astype(BF16)
    twice = jnp.einsum("wsxv,jk->sjwvkx", mpo, jnp.eye(2, dtype=BF16))
    size = 2 * channels * phys_pair
    mpo_back = twice.reshape(size, size)
    mpo_fore = mpo_back.T
    left, left_t = ordered(left_env.transpose(1, 0, 2), tile)
    right = parted(right_env.transpose(1, 0, 2), lanes)

    gathered = []
    for h in range(halves):
        piece = theta[:, :, h * lanes : (h + 1) * lanes].reshape(rows, phys_pair * lanes)
        if h > 0:
            piece = after(piece, gathered[-1], left, left_t, mpo_fore, mpo_back, right)
        gathered.append(lax.all_gather(piece, "row", axis=0, tiled=True))

    total = None
    for h in range(halves - 1):
        total = fore(gathered[h], left, mpo_fore, right[h], total, channels, 0, 1, F32, tile)

    def backward(h, g, parts, backs):
        return back(
            parts, mpo_back, right[h], backs, channels, phys_pair, g, groups, scattered, tile
        )

    own, everyone, backs = [], [], None
    block = gathered[-1]
    for g in range(groups):
        waits = own[g - 2 : g - 1] if g > 1 else []
        if g > 2:
            waits = waits + [everyone[g - 3][-1]]
        term = fore(
            after(block, *waits), left, mpo_fore, right[-1], total, channels, g, groups, BF16, tile
        )
        mine = lax.psum_scatter(term, ("col", "chan"), scatter_dimension=0, tiled=True)
        own.append(mine)
        if g > 1:
            backs = backward(0, g - 2, everyone[g - 2], backs)
            mine = after(mine, backs)
        if scattered:
            across = lax.ppermute(mine, "chan", swap)
            parts = [mine, across] + [lax.ppermute(p, "col", swap) for p in (mine, across)]
        else:
            parts = [lax.all_gather(mine, ("col", "chan"), axis=0, tiled=True)]
        everyone.append(parts)
    for g in range(max(groups - 2, 0), groups):
        backs = backward(0, g, everyone[g], backs)

    n_chunks = 2
    per = phys_pair // n_chunks
    products = []
    for h in range(halves):
        if h > 0:
            backs = None
            for g, parts in enumerate(everyone):
                waits = [term] if g < groups // 2 else products[-n_chunks : 1 - n_chunks]
                backs = backward(h, g, after(parts, *waits), backs)
        for c in range(n_chunks):
            if c > 0:
                backs = after(backs, term, *(products[-n_chunks : 1 - n_chunks] if h > 0 else []))
            term = last(left_t, backs, c, n_chunks)
            products.append(lax.psum_scatter(term, "row", scatter_dimension=0, tiled=True))
    products = [x.reshape(rows, per, lanes) for x in products]
    products = [
        jnp.concatenate(products[h * n_chunks : (h + 1) * n_chunks], axis=1) for h in range(halves)
    ]
    return jnp.concatenate(own, axis=1), jnp.concatenate(products, axis=2)


def solution(mesh):
    in_specs = (
        P(("grp", "row"), None, ("col", "chan")),
        P(("grp", "row"), None, None),
        P("grp", None, ("col", "chan")),
        P(),
        P(),
    )
    out_specs = (P(("grp", "col", "chan"), "row"), P(("grp", "row"), None, ("col", "chan")))
    return jax.shard_map(shards, mesh=mesh, in_specs=in_specs, out_specs=out_specs, check_vma=False)
```

time: 589 us -> 590 us (level)
  waiting for transfers between devices: 170 us -> 280 us
  starting transfers between devices: 119 us -> 14.8 us
  Pallas kernels: 254 us -> 217 us
  local copies, waits for them, and re-layouts: 18.5 us -> 45.6 us
  between operations: 2.57 us -> 14.7 us
  other arithmetic: 14.6 us -> 5.98 us
    reduce_scatter x0 -> x8, waiting for transfers between devices: none -> 150 us  [the longest x4 112 us: shards(): lax.psum_scatter(term, 'row', scatter_dimension=0, tiled=True)]
    ppermute x44 -> x0, waiting for transfers between devices: 129 us -> none  [the longest x6 50.9 us: gather_round(): up = lax.ppermute(up, 'row', [(r, r + 1) for r in range(t - 1, n_rows - 1)])]
    ppermute x44 -> x0, starting transfers between devices: 112 us -> none  [the longest x12 53.5 us: scatter_rows(): lax.ppermute(other, 'row', [(n_rows - 1 - r, n_rows - 2 - r) for r in ran...]
    all_gather x0 -> x2, waiting for transfers between devices: none -> 75 us  [shards(): gathered.append(lax.all_gather(piece, 'row', axis=0, tiled=True))]
    pallas_call x18, Pallas kernels: 242 us -> 205 us  [the longest x5 87.4 us: fore(): pl.pallas_call(functools.partial(fore_kernel, channels, lanes), grid=(ste...]
    unnamed x106 -> x98, local copies, waits for them, and re-layouts: 9.4 us -> 37.6 us
    ppermute x4, waiting for transfers between devices: 40.5 us -> 54.2 us  [shards(): across = lax.ppermute(mine, 'chan', swap)]
    reduce_scatter x0 -> x8, starting transfers between devices: none -> 11.4 us  [the longest x4 10.8 us: shards(): lax.psum_scatter(term, ('col', 'chan'), scatter_dimension=0, tiled=True)]
  transfers between devices with their start and end apart: 56 -> 22, of which waited for: 22 -> 12; matrix products, arithmetic and copies ran while one was open for 4% -> 3% of each run, Pallas kernels for 29% -> 30%
where the time goes in v3:
time: 590 us; the launch traced here: 580 us
  waiting for transfers between devices  280 us (47%)
  Pallas kernels  217 us (37%)
  local copies, waits for them, and re-layouts  45.6 us (8%)
  starting transfers between devices  14.8 us (3%)
  between operations  14.7 us (2%)
  other arithmetic  5.98 us (1%)
    reduce_scatter x4, waiting for transfers between devices, shards(): lax.psum_scatter(term, 'row', scatter_dimension=0, tiled=True)  112 us
    pallas_call x5, Pallas kernels, fore(): pl.pallas_call(functools.partial(fore_kernel, channels, lanes), grid=(ste...  87.4 us
    all_gather x2, waiting for transfers between devices, shards(): gathered.append(lax.all_gather(piece, 'row', axis=0, tiled=True))  75 us
    pallas_call x8, Pallas kernels, back(): pl.pallas_call(functools.partial(back_kernel, channels, len(parts), scatt...  63.8 us
    ppermute x4, waiting for transfers between devices, shards(): across = lax.ppermute(mine, 'chan', swap)  54.2 us
    pallas_call x4, Pallas kernels, last(): pl.pallas_call(last_kernel, grid=(steps,), in_specs=[pl.BlockSpec(left_t....  43.8 us
    unnamed x98, local copies, waits for them, and re-layouts  37.6 us
    reduce_scatter x4, waiting for transfers between devices, shards(): lax.psum_scatter(term, ('col', 'chan'), scatter_dimension=0, tiled=True)  37.3 us
  transfers between devices with their start and end apart: 22, of which 12 were waited for; matrix products, arithmetic and copies ran while one was open for 3% of the time, Pallas kernels for 30%

profile of v3, /device:TPU:16, one launch (start us, length us, event | category | flops | bytes accessed | tf_op | source)
XLA Modules:
  0.0 579.7 jit_solution(8374820719629337586)
XLA Ops:
  20.9 9.8 %shard_map.69 = (bf16[1024,1536]{1,0:T(8,128)(2,1)}, bf16[1024,1536]{1,0:T(8,128)(2,1)}) custom-call(bf16[12,1024,256]{2,1,0:T(8,128)(2,1)} %bitcast.28), custom_call_target="tpu_custom_call" | custom-call | bytes 786432 | tf_op jit(solution)/shard_map/pallas_call | solution.py:79
  31.5 12.0 %shard_map.68 = (bf16[3072,1024]{1,0:T(8,128)(2,1)}, bf16[1024,3072]{1,0:T(8,128)(2,1)}) custom-call(bf16[12,256,1024]{2,1,0:T(8,128)(2,1)} %bitcast.29, bf16[384,384]{1,0:T(8,128)(2,1)} %fusion.1.order_ref), custom_call_target="tpu_custom_call" | custom-call | flops 301989888 | bytes 1179648 | tf_op jit(solution)/shard_map/pallas_call | solution.py:50
  43.5 47.4 %all-gather.3.cloned.1.call-done.theta_ref = bf16[1024,2048]{1,0:T(8,128)(2,1)} async-done(((bf16[256,2048]{1,0:T(8,128)(2,1)}), bf16[1024,2048]{1,0:T(8,128)(2,1)}) %all-gather.3.cloned.1.call-update) | async-done | bytes 4194320 | tf_op jit(solution)/shard_map/all_gather | solution.py:263
  91.0 10.7 %reduce-scatter.9.cloned.1.call-start = ((), (), s32[]{:S(2)}) async-start(), calls=%async_computation.10 | async-start | bytes 2621440 | tf_op jit(solution)/shard_map/reduce_scatter | solution.py:283
  105.7 39.2 %shard_map.70.refs_0_ = f32[1024,4096]{1,0:T(8,128)} custom-call(bf16[1024,2048]{1,0:T(8,128)(2,1)} %all-gather.3.cloned.1.call-done.theta_ref, bf16[3072,1024]{1,0:T(8,128)(2,1)} %get-tuple-element.29.left_ref, bf16[384,384]{1,0:T(8,128)(2,1)S(1)} %copy-done.7, bf16[1024,1536]{1,0:T(8,128)(2,1)S(1)} %copy-done.3), custom_call_target="tpu_custom_call" | custom-call | flops 1912602624 | bytes 1900544 | tf_op jit(solution)/shard_map/pallas_call | solution.py:123
  144.8 27.6 %all-gather.5.cloned.1.call-done.theta_ref = bf16[1024,2048]{1,0:T(8,128)(2,1)} async-done(((bf16[256,2048]{1,0:T(8,128)(2,1)}), bf16[1024,2048]{1,0:T(8,128)(2,1)}) %all-gather.5.cloned.1.call-update) | async-done | bytes 4194320 | tf_op jit(solution)/shard_map/all_gather | solution.py:263
  173.4 12.1 %shard_map.71 = bf16[1024,1024]{1,0:T(8,128)(2,1)S(1)} custom-call(bf16[1024,2048]{1,0:T(8,128)(2,1)} %all-gather.5.cloned.1.call-done.theta_ref, bf16[3072,1024]{1,0:T(8,128)(2,1)} %get-tuple-element.29.left_ref, bf16[384,384]{1,0:T(8,128)(2,1)S(1)} %copy-done.8, bf16[1024,1536]{1,0:T(8,128)(2,1)S(1)} %copy-done.2, f32[1024,4096]{1,0:T(8,128)} %shard_map.70.refs_0_), custom_call_target="tpu_custom_call" | custom-call | flops 478150656 | bytes 819200 | tf_op jit(solution)/shard_map/pallas_call | solution.py:123
  187.8 12.1 %shard_map.72 = bf16[1024,1024]{1,0:T(8,128)(2,1)S(1)} custom-call(bf16[1024,2048]{1,0:T(8,128)(2,1)} %all-gather.5.cloned.1.call-done.theta_ref, bf16[3072,1024]{1,0:T(8,128)(2,1)} %get-tuple-element.29.left_ref, bf16[384,384]{1,0:T(8,128)(2,1)S(1)} %copy-done.9, bf16[1024,1536]{1,0:T(8,128)(2,1)S(1)} %copy-done.2, f32[1024,4096]{1,0:T(8,128)} %shard_map.70.refs_0_), custom_call_target="tpu_custom_call" | custom-call | flops 478150656 | bytes 819200 | tf_op jit(solution)/shard_map/pallas_call | solution.py:123
  201.3 17.1 %reduce-scatter.9.cloned.1.call-done.refs_0_ = bf16[256,1024]{1,0:T(8,128)(2,1)} async-done(((bf16[1024,1024]{1,0:T(8,128)(2,1)}), bf16[256,1024]{1,0:T(8,128)(2,1)}) %reduce-scatter.9.cloned.1.call-update) | async-done | bytes 524304 | tf_op jit(solution)/shard_map/reduce_scatter | solution.py:283
  219.4 12.1 %shard_map.73 = bf16[1024,1024]{1,0:T(8,128)(2,1)S(1)} custom-call(bf16[1024,2048]{1,0:T(8,128)(2,1)} %all-gather.5.cloned.1.call-done.theta_ref, bf16[3072,1024]{1,0:T(8,128)(2,1)} %get-tuple-element.29.left_ref, bf16[384,384]{1,0:T(8,128)(2,1)S(1)} %copy-done.10, bf16[1024,1536]{1,0:T(8,128)(2,1)S(1)} %copy-done.2, f32[1024,4096]{1,0:T(8,128)} %shard_map.70.refs_0_), custom_call_target="tpu_custom_call" | custom-call | flops 478150656 | bytes 819200 | tf_op jit(solution)/shard_map/pallas_call | solution.py:123
  233.5 20.6 %collective-permute-done.refs_1_ = bf16[256,1024]{1,0:T(8,128)(2,1)} collective-permute-done((bf16[256,1024]{1,0:T(8,128)(2,1)}, bf16[256,1024]{1,0:T(8,128)(2,1)}, u32[]{:S(2)}, u32[]{:S(2)}) %collective-permute-start) | collective-permute-done | bytes 524320 | tf_op jit(solution)/shard_map/ppermute | solution.py:289
  260.1 12.1 %shard_map.74 = bf16[1024,1024]{1,0:T(8,128)(2,1)S(1)} custom-call(bf16[1024,2048]{1,0:T(8,128)(2,1)} %all-gather.5.cloned.1.call-done.theta_ref, bf16[3072,1024]{1,0:T(8,128)(2,1)} %get-tuple-element.29.left_ref, bf16[384,384]{1,0:T(8,128)(2,1)S(1)} %copy-done.11, bf16[1024,1536]{1,0:T(8,128)(2,1)S(1)} %copy-done.2, f32[1024,4096]{1,0:T(8,128)} %shard_map.70.refs_0_), custom_call_target="tpu_custom_call" | custom-call | flops 478150656 | bytes 819200 | tf_op jit(solution)/shard_map/pallas_call | solution.py:123
  275.1 20.9 %collective-permute-done.2.refs_1_ = bf16[256,1024]{1,0:T(8,128)(2,1)} collective-permute-done((bf16[256,1024]{1,0:T(8,128)(2,1)}, bf16[256,1024]{1,0:T(8,128)(2,1)}, u32[]{:S(2)}, u32[]{:S(2)}) %collective-permute-start.2) | collective-permute-done | bytes 524320 | tf_op jit(solution)/shard_map/ppermute | solution.py:289
  311.7 8.3 %shard_map.76.refs_6_ = bf16[3072,2048]{1,0:T(8,128)(2,1)} custom-call(bf16[256,1024]{1,0:T(8,128)(2,1)S(1)} %copy-done.19, bf16[256,1024]{1,0:T(8,128)(2,1)} %collective-permute-done.2.refs_1_, bf16[256,1024]{1,0:T(8,128)(2,1)} %collective-permute-done.3.refs_2_, bf16[256,1024]{1,0:T(8,128)(2,1)} %collective-permute-done.4.refs_3_, ...), custom_call_target="tpu_custom_call", output_to_operand_aliasing={{}: (6, {})} | custom-call | flops 276824064 | bytes 524288 | tf_op jit(solution)/shard_map/pallas_call | solution.py:185
  320.0 15.1 %reduce-scatter.15.cloned.1.call-done.refs_0_ = bf16[256,1024]{1,0:T(8,128)(2,1)} async-done(((bf16[1024,1024]{1,0:T(8,128)(2,1)}), bf16[256,1024]{1,0:T(8,128)(2,1)}) %reduce-scatter.15.cloned.1.call-update) | async-done | bytes 524304 | tf_op jit(solution)/shard_map/reduce_scatter | solution.py:283
  336.2 12.8 %collective-permute-done.6.refs_1_ = bf16[256,1024]{1,0:T(8,128)(2,1)S(1)} collective-permute-done((bf16[256,1024]{1,0:T(8,128)(2,1)}, bf16[256,1024]{1,0:T(8,128)(2,1)S(1)}, u32[]{:S(2)}, u32[]{:S(2)}) %collective-permute-start.6) | collective-permute-done | bytes 524320 | tf_op jit(solution)/shard_map/ppermute | solution.py:289
  367.9 10.7 %shard_map.79 = bf16[1024,1024]{1,0:T(8,128)(2,1)S(1)} custom-call(bf16[1024,3072]{1,0:T(8,128)(2,1)} %get-tuple-element.30.left_ref, bf16[3072,2048]{1,0:T(8,128)(2,1)} %shard_map.78.back_ref), custom_call_target="tpu_custom_call" | custom-call | flops 402653184 | bytes 917504 | tf_op jit(solution)/shard_map/pallas_call | solution.py:218
  380.1 10.8 %shard_map.80 = bf16[1024,1024]{1,0:T(8,128)(2,1)S(1)} custom-call(bf16[1024,3072]{1,0:T(8,128)(2,1)} %get-tuple-element.30.left_ref, bf16[3072,2048]{1,0:T(8,128)(2,1)} %shard_map.78.back_ref), custom_call_target="tpu_custom_call" | custom-call | flops 402653184 | bytes 917504 | tf_op jit(solution)/shard_map/pallas_call | solution.py:218
  410.8 12.5 %reduce-scatter.17.cloned.1.call-done = bf16[256,1024]{1,0:T(8,128)(2,1)} async-done(((bf16[1024,1024]{1,0:T(8,128)(2,1)}), bf16[256,1024]{1,0:T(8,128)(2,1)}) %reduce-scatter.17.cloned.1.call-update) | async-done | bytes 524304 | tf_op jit(solution)/shard_map/reduce_scatter | solution.py:310
  442.0 10.8 %shard_map.85 = bf16[1024,1024]{1,0:T(8,128)(2,1)S(1)} custom-call(bf16[1024,3072]{1,0:T(8,128)(2,1)} %get-tuple-element.30.left_ref, bf16[3072,2048]{1,0:T(8,128)(2,1)} %shard_map.84.back_ref), custom_call_target="tpu_custom_call" | custom-call | flops 402653184 | bytes 917504 | tf_op jit(solution)/shard_map/pallas_call | solution.py:218
  454.1 15.5 %reduce-scatter.19.cloned.1.call-done = bf16[256,1024]{1,0:T(8,128)(2,1)} async-done(((bf16[1024,1024]{1,0:T(8,128)(2,1)}), bf16[256,1024]{1,0:T(8,128)(2,1)}) %reduce-scatter.19.cloned.1.call-update) | async-done | bytes 524304 | tf_op jit(solution)/shard_map/reduce_scatter | solution.py:310
  469.6 11.6 %shard_map.86 = bf16[1024,1024]{1,0:T(8,128)(2,1)} custom-call(bf16[1024,3072]{1,0:T(8,128)(2,1)} %get-tuple-element.30.left_ref, bf16[3072,2048]{1,0:T(8,128)(2,1)} %shard_map.84.back_ref), custom_call_target="tpu_custom_call" | custom-call | flops 402653184 | bytes 917504 | tf_op jit(solution)/shard_map/pallas_call | solution.py:218
  484.3 40.2 %reduce-scatter.23.cloned.1.call-done = bf16[256,1024]{1,0:T(8,128)(2,1)} async-done(((bf16[1024,1024]{1,0:T(8,128)(2,1)}), bf16[256,1024]{1,0:T(8,128)(2,1)}) %reduce-scatter.23.cloned.1.call-update) | async-done | bytes 524304 | tf_op jit(solution)/shard_map/reduce_scatter | solution.py:310
  525.7 44.3 %reduce-scatter.21.cloned.1.call-done = bf16[256,1024]{1,0:T(8,128)(2,1)} async-done(((bf16[1024,1024]{1,0:T(8,128)(2,1)}), bf16[256,1024]{1,0:T(8,128)(2,1)}) %reduce-scatter.21.cloned.1.call-update) | async-done | bytes 524304 | tf_op jit(solution)/shard_map/reduce_scatter | solution.py:310
  (159 shorter events, 118.9 us)
Async XLA Ops:
  7.2 83.8 %all-gather.3.cloned.1.call-start = ((), (), s32[]{:S(2)}) async-start(), calls=%async_computation.8 | async-start | bytes 5242880 | tf_op jit(solution)/shard_map/all_gather | solution.py:263
  10.4 162.0 %all-gather.5.cloned.1.call-start = ((), (), s32[]{:S(2)}) async-start(), calls=%async_computation.9 | async-start | bytes 5242880 | tf_op jit(solution)/shard_map/all_gather | solution.py:263
  91.0 127.4 %reduce-scatter.9.cloned.1.call-start = ((), (), s32[]{:S(2)}) async-start(), calls=%async_computation.10 | async-start | bytes 2621440 | tf_op jit(solution)/shard_map/reduce_scatter | solution.py:283
  105.7 66.8 %copy-start.2 = (bf16[1024,1536]{1,0:T(8,128)(2,1)S(1)}, bf16[1024,1536]{1,0:T(8,128)(2,1)}, u32[]{:S(2)}) copy-start(bf16[1024,1536]{1,0:T(8,128)(2,1)} %get-tuple-element.32.right_ref.refs_5_) | copy-start | bytes 9437188
  186.8 72.3 %reduce-scatter.11.cloned.1.call-start = ((), (), s32[]{:S(2)}) async-start(), calls=%async_computation.11 | async-start | bytes 2621440 | tf_op jit(solution)/shard_map/reduce_scatter | solution.py:283
  201.3 106.6 %reduce-scatter.13.cloned.1.call-start = ((), (), s32[]{:S(2)}) async-start(), calls=%async_computation.12 | async-start | bytes 2621440 | tf_op jit(solution)/shard_map/reduce_scatter | solution.py:283
  232.8 102.3 %reduce-scatter.15.cloned.1.call-start = ((), (), s32[]{:S(2)}) async-start(), calls=%async_computation.13 | async-start | bytes 2621440 | tf_op jit(solution)/shard_map/reduce_scatter | solution.py:283
  232.8 21.2 %collective-permute-start = (bf16[256,1024]{1,0:T(8,128)(2,1)}, bf16[256,1024]{1,0:T(8,128)(2,1)}, u32[]{:S(2)}, u32[]{:S(2)}) collective-permute-start(bf16[256,1024]{1,0:T(8,128)(2,1)} %reduce-scatter.9.cloned.1.call-done.refs_0_), channel_id=1, source_target_pairs={{0,1},{1,0},{2,3},{3,2},{4,5},{5,4},{6,7},{7,6},{8,9},{9,8},{10,11... | collective-permute-start | bytes 1572872 | tf_op jit(solution)/shard_map/ppermute | solution.py:289
  254.0 5.1 collective-permute-start.1
  273.5 149.8 %reduce-scatter.17.cloned.1.call-start = ((), (), s32[]{:S(2)}) async-start(), calls=%async_computation.14 | async-start | bytes 2621440 | tf_op jit(solution)/shard_map/reduce_scatter | solution.py:310
  274.0 22.0 %collective-permute-start.2 = (bf16[256,1024]{1,0:T(8,128)(2,1)}, bf16[256,1024]{1,0:T(8,128)(2,1)}, u32[]{:S(2)}, u32[]{:S(2)}) collective-permute-start(bf16[256,1024]{1,0:T(8,128)(2,1)} %reduce-scatter.11.cloned.1.call-done.refs_0_), channel_id=1, source_target_pairs={{0,1},{1,0},{2,3},{3,2},{4,5},{5,4},{6,7},{7,6},{8,9},{9,8},{10,11... | collective-permute-start | bytes 1572872 | tf_op jit(solution)/shard_map/ppermute | solution.py:289
  274.6 21.4 %collective-permute-start.5 = (bf16[256,1024]{1,0:T(8,128)(2,1)}, bf16[256,1024]{1,0:T(8,128)(2,1)S(1)}, u32[]{:S(2)}, u32[]{:S(2)}) collective-permute-start(bf16[256,1024]{1,0:T(8,128)(2,1)} %reduce-scatter.9.cloned.1.call-done.refs_0_), channel_id=1, source_target_pairs={{0,2},{2,0},{1,3},{3,1},{4,6},{6,4},{5,7},{7,5},{8,10},{10,8},{9,1... | collective-permute-start | bytes 1572872 | tf_op jit(solution)/shard_map/ppermute | solution.py:290
  274.6 33.7 %collective-permute-start.3 = (bf16[256,1024]{1,0:T(8,128)(2,1)}, bf16[256,1024]{1,0:T(8,128)(2,1)}, u32[]{:S(2)}, u32[]{:S(2)}) collective-permute-start(bf16[256,1024]{1,0:T(8,128)(2,1)} %reduce-scatter.11.cloned.1.call-done.refs_0_), channel_id=1, source_target_pairs={{0,2},{2,0},{1,3},{3,1},{4,6},{6,4},{5,7},{7,5},{8,10},{10,8},{9,1... | collective-permute-start | bytes 1572872 | tf_op jit(solution)/shard_map/ppermute | solution.py:290
  296.0 12.4 %collective-permute-start.4 = (bf16[256,1024]{1,0:T(8,128)(2,1)}, bf16[256,1024]{1,0:T(8,128)(2,1)}, u32[]{:S(2)}, u32[]{:S(2)}) collective-permute-start(bf16[256,1024]{1,0:T(8,128)(2,1)} %collective-permute-done.2.refs_1_), channel_id=1, source_target_pairs={{0,2},{2,0},{1,3},{3,1},{4,6},{6,4},{5,7},{7,5},{8,10},{10,8},{9,1... | collective-permute-start | bytes 1572872 | tf_op jit(solution)/shard_map/ppermute | solution.py:290
  307.8 27.9 %collective-permute-start.9 = (bf16[256,1024]{1,0:T(8,128)(2,1)}, bf16[256,1024]{1,0:T(8,128)(2,1)}, u32[]{:S(2)}, u32[]{:S(2)}) collective-permute-start(bf16[256,1024]{1,0:T(8,128)(2,1)} %reduce-scatter.13.cloned.1.call-done.refs_0_), channel_id=1, source_target_pairs={{0,1},{1,0},{2,3},{3,2},{4,5},{5,4},{6,7},{7,6},{8,9},{9,8},{10,11... | collective-permute-start | bytes 1572872 | tf_op jit(solution)/shard_map/ppermute | solution.py:289
  335.1 13.9 %collective-permute-start.6 = (bf16[256,1024]{1,0:T(8,128)(2,1)}, bf16[256,1024]{1,0:T(8,128)(2,1)S(1)}, u32[]{:S(2)}, u32[]{:S(2)}) collective-permute-start(bf16[256,1024]{1,0:T(8,128)(2,1)} %reduce-scatter.15.cloned.1.call-done.refs_0_), channel_id=1, source_target_pairs={{0,1},{1,0},{2,3},{3,2},{4,5},{5,4},{6,7},{7,6},{8,9},{9,8},{10,11... | collective-permute-start | bytes 1572872 | tf_op jit(solution)/shard_map/ppermute | solution.py:289
  335.7 13.3 %collective-permute-start.10 = (bf16[256,1024]{1,0:T(8,128)(2,1)}, bf16[256,1024]{1,0:T(8,128)(2,1)S(1)}, u32[]{:S(2)}, u32[]{:S(2)}) collective-permute-start(bf16[256,1024]{1,0:T(8,128)(2,1)} %reduce-scatter.13.cloned.1.call-done.refs_0_), channel_id=1, source_target_pairs={{0,2},{2,0},{1,3},{3,1},{4,6},{6,4},{5,7},{7,5},{8,10},{10,8},{9,1... | collective-permute-start | bytes 1572872 | tf_op jit(solution)/shard_map/ppermute | solution.py:290
  335.7 13.3 %collective-permute-start.11 = (bf16[256,1024]{1,0:T(8,128)(2,1)}, bf16[256,1024]{1,0:T(8,128)(2,1)S(1)}, u32[]{:S(2)}, u32[]{:S(2)}) collective-permute-start(bf16[256,1024]{1,0:T(8,128)(2,1)} %collective-permute-done.9.refs_1_), channel_id=1, source_target_pairs={{0,2},{2,0},{1,3},{3,1},{4,6},{6,4},{5,7},{7,5},{8,10},{10,8},{9,1... | collective-permute-start | bytes 1572872 | tf_op jit(solution)/shard_map/ppermute | solution.py:290
  336.2 24.3 %collective-permute-start.7 = (bf16[256,1024]{1,0:T(8,128)(2,1)}, bf16[256,1024]{1,0:T(8,128)(2,1)S(1)}, u32[]{:S(2)}, u32[]{:S(2)}) collective-permute-start(bf16[256,1024]{1,0:T(8,128)(2,1)} %reduce-scatter.15.cloned.1.call-done.refs_0_), channel_id=1, source_target_pairs={{0,2},{2,0},{1,3},{3,1},{4,6},{6,4},{5,7},{7,5},{8,10},{10,8},{9,1... | collective-permute-start | bytes 1572872 | tf_op jit(solution)/shard_map/ppermute | solution.py:290
  349.0 11.6 %collective-permute-start.8 = (bf16[256,1024]{1,0:T(8,128)(2,1)S(1)}, bf16[256,1024]{1,0:T(8,128)(2,1)S(1)}, u32[]{:S(2)}, u32[]{:S(2)}) collective-permute-start(bf16[256,1024]{1,0:T(8,128)(2,1)S(1)} %collective-permute-done.6.refs_1_), channel_id=1, source_target_pairs={{0,2},{2,0},{1,3},{3,1},{4,6},{6,4},{5,7},{7,5},{8,10},{10,8},{9,1... | collective-permute-start | bytes 1572872 | tf_op jit(solution)/shard_map/ppermute | solution.py:290
  380.0 89.5 %reduce-scatter.19.cloned.1.call-start = ((), (), s32[]{:S(2)}) async-start(), calls=%async_computation.15 | async-start | bytes 2621440 | tf_op jit(solution)/shard_map/reduce_scatter | solution.py:310
  392.2 132.3 %reduce-scatter.23.cloned.1.call-start = ((), (), s32[]{:S(2)}) async-start(), calls=%async_computation.17 | async-start | bytes 2621440 | tf_op jit(solution)/shard_map/reduce_scatter | solution.py:310
  481.2 88.8 %reduce-scatter.21.cloned.1.call-start = ((), (), s32[]{:S(2)}) async-start(), calls=%async_computation.16 | async-start | bytes 2621440 | tf_op jit(solution)/shard_map/reduce_scatter | solution.py:310
  484.1 88.5 %copy-start.1 = (f32[12,12,4,4]{1,3,2,0:T(4,128)S(1)}, f32[12,12,4,4]{1,3,2,0:T(4,128)}, u32[]{:S(2)}) copy-start(f32[12,12,4,4]{1,3,2,0:T(4,128)} %param.8) | copy-start | bytes 27652
  (44 other events, 147.4 us)
Sparse Core Ops, SparseCore 0:
  10.6 80.3 all-gather.2
  93.1 79.2 all-gather.4
  186.9 31.4 reduce-scatter.8
  221.5 37.5 reduce-scatter.10
  262.1 38.3 reduce-scatter.12
  303.6 31.4 reduce-scatter.14
  380.1 43.1 reduce-scatter.16
  426.3 43.2 reduce-scatter.18
  481.3 43.1 reduce-scatter.22
  526.8 43.1 reduce-scatter.20

commit v4 on v3

--- a/solution.py
+++ b/solution.py
@@ -113,7 +113,7 @@
     out[...] = part.astype(out.dtype)
 
 
-def fore(theta, left, mpo, right, total, channels, group, groups, kind, tile):
+def fore(theta, left, mpo, right, total, channels, group, groups, kind, tile, place=0):
     far = right.shape[0]
     lanes = right.shape[1] // channels
     phys_pair = theta.shape[1] // lanes
@@ -129,7 +129,7 @@
             pl.BlockSpec(mpo.shape, lambda i: (0, 0), pipeline_mode=ONCE),
             pl.BlockSpec(right.shape, lambda i: (0, 0), pipeline_mode=ONCE),
         ]
-        + [pl.BlockSpec((far, tile * phys_pair), lambda i: (0, group * steps + i))] * len(totals),
+        + [pl.BlockSpec((far, tile * phys_pair), lambda i: (0, place * steps + i))] * len(totals),
         out_specs=pl.BlockSpec((far, tile * phys_pair), lambda i: (0, i)),
         out_shape=jax.ShapeDtypeStruct((far, bonds * phys_pair), kind),
         scratch_shapes=[
@@ -232,19 +232,90 @@
     )(left_t, backs)
 
 
+def join_kernel(n_rows, n_parts, *refs):
+    blocks, out, sems = refs[:-2], refs[-2], refs[-1]
+    depth, columns = blocks[0].shape
+    reach = 2 * n_rows - 1
+    for phase in ("start", "wait"):
+        for k, block in enumerate(blocks):
+            source = lax.axis_index("row") + (k % reach - (n_rows - 1))
+
+            @pl.when((source >= 0) & (source < n_rows))
+            def _():
+                target = out.at[
+                    pl.ds(pl.multiple_of(source * depth, depth), depth),
+                    pl.ds(k // reach * columns, columns),
+                ]
+                getattr(pltpu.make_async_copy(block, target, sems.at[k]), phase)()
+
+
+def join(parts, n_rows):
+    blocks = [block for part in parts for block in part]
+    depth, columns = blocks[0].shape
+    return pl.pallas_call(
+        functools.partial(join_kernel, n_rows, len(parts)),
+        in_specs=[ANY] * len(blocks),
+        out_specs=ANY,
+        out_shape=jax.ShapeDtypeStruct((depth * n_rows, columns * len(parts)), BF16),
+        scratch_shapes=[pltpu.SemaphoreType.DMA((len(blocks),))],
+        cost_estimate=cost(0, 4 * depth * n_rows * columns * len(parts)),
+    )(*blocks)
+
+
 def after(arrays, *deps):
     return lax.optimization_barrier((arrays, deps))[0]
+
+
+def gather_round(pair, t, n_rows):
+    up = lax.ppermute(pair[0], "row", [(r, r + 1) for r in range(t - 1, n_rows - 1)])
+    down = lax.ppermute(pair[1], "row", [(r, r - 1) for r in range(1, n_rows - t + 1)])
+    return up, down
+
+
+def row_block(term, distance, n_rows):
+    height = term.shape[0] // n_rows
+    block = lax.rem(lax.axis_index("row") + distance, n_rows)
+    return lax.dynamic_slice_in_dim(term, block * height, height)
+
+
+def scatter_inputs(term, pair, t, n_rows):
+    up, down = row_block(term, n_rows - t, n_rows), row_block(term, t, n_rows)
+    if pair is not None:
+        up, down = add(up, pair[0]), add(down, pair[1])
+    return lax.optimization_barrier((up, down))
+
+
+def scatter_round(pair, t, n_rows):
+    up = lax.ppermute(pair[0], "row", [(r, r + 1) for r in range(t)])
+    down = lax.ppermute(pair[1], "row", [(n_rows - 1 - r, n_rows - 2 - r) for r in range(t)])
+    return up, down
+
+
+def add(x, y):
+    return (x.astype(F32) + y.astype(F32)).astype(BF16)
+
+
+def halved(term, axis):
+    height = term.shape[0] // 2
+    index = lax.axis_index(axis)
+    return [lax.dynamic_slice_in_dim(term, k * height, height) for k in (index, 1 - index)]
+
+
+def swapped(block, axis):
+    return lax.ppermute(block, axis, [(0, 1), (1, 0)])
 
 
 def shards(theta, left_env, right_env, mpo_left, mpo_right):
     bonds, channels, depth = left_env.shape
     rows, phys_pair, width = theta.shape
+    n_rows = lax.axis_size("row")
     scattered = lax.axis_size("col") == 2 and lax.axis_size("chan") == 2
     tile = min(32, bonds)
     lanes = min(128, width)
     halves = width // lanes
     groups = max(1, min(4, bonds // tile))
-    swap = [(0, 1), (1, 0)]
+    n_chunks = 2
+    per = phys_pair // n_chunks
 
     paired = jnp.einsum("wuxs,uvyt->wstxyv", mpo_left, mpo_right, precision=lax.Precision.HIGHEST)
     mpo = paired.reshape(channels, phys_pair, phys_pair, channels).astype(BF16)
@@ -255,60 +326,128 @@
     left, left_t = ordered(left_env.transpose(1, 0, 2), tile)
     right = parted(right_env.transpose(1, 0, 2), lanes)
 
-    gathered = []
+    theta_all, total, last_round = None, [None], [()] * n_chunks
+    cuts = 2 if groups % 2 == 0 and n_rows > 2 else 1
     for h in range(halves):
-        piece = theta[:, :, h * lanes : (h + 1) * lanes].reshape(rows, phys_pair * lanes)
-        if h > 0:
-            piece = after(piece, gathered[-1], left, left_t, mpo_fore, mpo_back, right)
-        gathered.append(lax.all_gather(piece, "row", axis=0, tiled=True))
-
-    total = None
-    for h in range(halves - 1):
-        total = fore(gathered[h], left, mpo_fore, right[h], total, channels, 0, 1, F32, tile)
-
-    def backward(h, g, parts, backs):
+        cut = theta[:, :, h * lanes : (h + 1) * lanes]
+        pairs, blocks, fresh = [], [], []
+        for c in range(n_chunks):
+            piece = cut[:, c * per : (c + 1) * per].reshape(rows, per * lanes)
+            pairs.append(after((piece, piece), *last_round[c]))
+            blocks.append([piece])
+        for t in range(1, n_rows):
+            if h == 0 and t > 1:
+                waits = [left, left_t] if t == 2 else [mpo_fore, mpo_back, right]
+                pairs[0] = after(pairs[0], *waits)
+            if h > 0 and t > 1 and len(fresh) < cuts:
+                held = theta_all if t == 2 else after(theta_all, *pairs)
+                fresh += [
+                    fore(held, left, mpo_fore, right[h - 1], total[0], channels, len(fresh), cuts,
+                         F32, tile)
+                ]
+                pairs = [after(pair, fresh[-1]) for pair in pairs]
+            for c in range(n_chunks):
+                pairs[c] = gather_round(pairs[c], t, n_rows)
+                blocks[c] = [pairs[c][0]] + blocks[c] + [pairs[c][1]]
+        while h > 0 and len(fresh) < cuts:
+            fresh += [
+                fore(theta_all, left, mpo_fore, right[h - 1], total[0], channels, len(fresh), cuts,
+                     F32, tile)
+            ]
+        total = fresh or total
+        last_round = pairs
+        theta_all = join(blocks, n_rows)
+
+    def forward(g, *deps):
+        here = g * len(total) // groups
+        return fore(
+            after(theta_all, *deps), left, mpo_fore, right[-1], total[here], channels, g, groups,
+            BF16, tile, g % (groups // len(total)),
+        )
+
+    def backward(h, g, parts, backs, *deps):
+        parts = after(parts, *deps)
         return back(
             parts, mpo_back, right[h], backs, channels, phys_pair, g, groups, scattered, tile
         )
 
-    own, everyone, backs = [], [], None
-    block = gathered[-1]
-    for g in range(groups):
-        waits = own[g - 2 : g - 1] if g > 1 else []
-        if g > 2:
-            waits = waits + [everyone[g - 3][-1]]
-        term = fore(
-            after(block, *waits), left, mpo_fore, right[-1], total, channels, g, groups, BF16, tile
-        )
-        mine = lax.psum_scatter(term, ("col", "chan"), scatter_dimension=0, tiled=True)
-        own.append(mine)
-        if g > 1:
-            backs = backward(0, g - 2, everyone[g - 2], backs)
-            mine = after(mine, backs)
+    terms, near, own, far, everyone, backs = [], [], [], [], [], None
+    step = 0
+    while len(everyone) < groups or step < 2 * groups:
+        g = step - groups
+        waits = []
         if scattered:
-            across = lax.ppermute(mine, "chan", swap)
-            parts = [mine, across] + [lax.ppermute(p, "col", swap) for p in (mine, across)]
-        else:
-            parts = [lax.all_gather(mine, ("col", "chan"), axis=0, tiled=True)]
-        everyone.append(parts)
-    for g in range(max(groups - 2, 0), groups):
+            for lag, done in ((2, near), (3, own), (4, far)):
+                waits += done[step - lag : step - lag + 1] if step >= lag else []
+        if step < groups:
+            terms.append(forward(step, *waits))
+            out = terms[-1]
+        elif 0 <= g < len(everyone):
+            backs = backward(0, g, everyone[g], backs, *waits)
+            out = backs
+        step += 1
+        if not scattered:
+            if step <= groups:
+                own.append(lax.psum_scatter(out, ("col", "chan"), scatter_dimension=0, tiled=True))
+                everyone.append([lax.all_gather(own[-1], ("col", "chan"), axis=0, tiled=True)])
+            continue
+        if len(everyone) < len(far):
+            across = after(far[len(everyone)], out)
+            pair = [own[len(everyone)], across]
+            everyone.append(pair + [swapped(x, "col") for x in pair])
+        if len(far) < len(own):
+            far.append(swapped(after(own[len(far)], out), "chan"))
+        if len(own) < len(near):
+            mine, other = halved(after(near[len(own)], out), "chan")
+            own.append(add(mine, swapped(other, "chan")))
+        if len(near) < len(terms):
+            mine, other = halved(terms[len(near)], "col")
+            near.append(add(mine, swapped(other, "col")))
+    for g in range(step - groups, groups):
         backs = backward(0, g, everyone[g], backs)
 
-    n_chunks = 2
-    per = phys_pair // n_chunks
+    terms, rounds = [], []
+
+    def advance(i, *deps):
+        t = len(rounds[i]) + 1
+        if t < n_rows:
+            pair = after(rounds[i][-1], *deps) if t > 1 else None
+            ready = scatter_inputs(terms[i], pair, t, n_rows)
+            rounds[i].append(scatter_round(ready, t, n_rows))
+            return list(ready)
+
+    def come(i, t):
+        return list(rounds[i][min(t, len(rounds[i])) - 1])
+
+    for h in range(halves):
+        first = len(terms)
+        if h > 0:
+            one, two, backs = first - n_chunks, first - 1, None
+            for g, parts in enumerate(everyone):
+                waits = [terms[-1]] + come(one, 1) if g == 0 else []
+                if g == 1:
+                    waits = come(one, 2) + come(two, 1)
+                    advance(one, backs)
+                    advance(two, backs)
+                elif g > 1 and g == groups - 1:
+                    waits = come(one, 3) + come(two, 2)
+                    advance(two, backs)
+                backs = backward(h, g, parts, backs, *waits)
+        for c in range(n_chunks):
+            waits = come(first - 1, 3) if h > 0 and c > 0 else []
+            waits += sent + terms[first:] if c > 0 else []
+            terms.append(last(left_t, after(backs, *waits), c, n_chunks))
+            rounds.append([])
+            for i in range(first, len(terms)):
+                sent = advance(i, terms[-1])
     products = []
-    for h in range(halves):
-        if h > 0:
-            backs = None
-            for g, parts in enumerate(everyone):
-                waits = [term] if g < groups // 2 else products[-n_chunks : 1 - n_chunks]
-                backs = backward(h, g, after(parts, *waits), backs)
-        for c in range(n_chunks):
-            if c > 0:
-                backs = after(backs, term, *(products[-n_chunks : 1 - n_chunks] if h > 0 else []))
-            term = last(left_t, backs, c, n_chunks)
-            products.append(lax.psum_scatter(term, "row", scatter_dimension=0, tiled=True))
-    products = [x.reshape(rows, per, lanes) for x in products]
+    for i in range(len(terms)):
+        while len(rounds[i]) < n_rows - 1:
+            advance(i)
+        total = row_block(terms[i], 0, n_rows).astype(F32)
+        for x in rounds[i][-1]:
+            total = total + x.astype(F32)
+        products.append(total.astype(BF16).reshape(rows, per, lanes))
     products = [
         jnp.concatenate(products[h * n_chunks : (h + 1) * n_chunks], axis=1) for h in range(halves)
     ]

time: 590 us -> 790 us (1.34)
  Pallas kernels: 217 us -> 474 us
  waiting for transfers between devices: 280 us -> 109 us
  starting transfers between devices: 14.8 us -> 130 us
  other arithmetic: 5.98 us -> 29 us
  between operations: 14.7 us -> 2.29 us
  local copies, waits for them, and re-layouts: 45.6 us -> 33.6 us
    pallas_call x0 -> x2, Pallas kernels: none -> 257 us  [join(): pl.pallas_call(functools.partial(join_kernel, n_rows, len(parts)), in_spe...]
    reduce_scatter x8 -> x0, waiting for transfers between devices: 150 us -> none  [the longest x4 112 us: shards(): lax.psum_scatter(term, 'row', scatter_dimension=0, tiled=True)]
    ppermute x12 -> x68, starting transfers between devices: 3.35 us -> 130 us  [the longest x12 40.7 us: scatter_round(): lax.ppermute(pair[1], 'row', [(n_rows - 1 - r, n_rows - 2 - r) for r in r...]
    all_gather x2 -> x0, waiting for transfers between devices: 75 us -> none  [shards(): gathered.append(lax.all_gather(piece, 'row', axis=0, tiled=True))]
    ppermute x12 -> x68, waiting for transfers between devices: 54.2 us -> 109 us  [the longest x20 39.1 us: swapped(): return lax.ppermute(block, axis, [(0, 1), (1, 0)])]
    unnamed x98 -> x130, local copies, waits for them, and re-layouts: 37.6 us -> 18.3 us
    convert_element_type x0 -> x18, other arithmetic: none -> 18.5 us  [add(): return (x.astype(F32) + y.astype(F32)).astype(BF16)]
    reduce_scatter x8 -> x0, starting transfers between devices: 11.4 us -> none  [the longest x4 10.8 us: shards(): lax.psum_scatter(term, ('col', 'chan'), scatter_dimension=0, tiled=True)]
  transfers between devices with their start and end apart: 22 -> 68, of which waited for: 12 -> 22; matrix products, arithmetic and copies ran while one was open for 3% -> 5% of each run, Pallas kernels for 30% -> 38%
where the time goes in v4:
time: 790 us; the launch traced here: 779 us
  Pallas kernels  474 us (60%)
  starting transfers between devices  130 us (16%)
  waiting for transfers between devices  109 us (14%)
  local copies, waits for them, and re-layouts  33.6 us (4%)
  other arithmetic  29 us (4%)
    pallas_call x2, Pallas kernels, join(): pl.pallas_call(functools.partial(join_kernel, n_rows, len(parts)), in_spe...  257 us
    pallas_call x6, Pallas kernels, fore(): pl.pallas_call(functools.partial(fore_kernel, channels, lanes), grid=(ste...  91.4 us
    pallas_call x8, Pallas kernels, back(): pl.pallas_call(functools.partial(back_kernel, channels, len(parts), scatt...  60.8 us
    pallas_call x4, Pallas kernels, last(): pl.pallas_call(last_kernel, grid=(steps,), in_specs=[pl.BlockSpec(left_t....  43 us
    ppermute x12, starting transfers between devices, scatter_round(): lax.ppermute(pair[1], 'row', [(n_rows - 1 - r, n_rows - 2 - r) for r in r...  40.7 us
    ppermute x20, waiting for transfers between devices, swapped(): return lax.ppermute(block, axis, [(0, 1), (1, 0)])  39.1 us
    ppermute x12, starting transfers between devices, gather_round(): lax.ppermute(pair[0], 'row', [(r, r + 1) for r in range(t - 1, n_rows - 1)])  34.8 us
    ppermute x12, waiting for transfers between devices, scatter_round(): lax.ppermute(pair[1], 'row', [(n_rows - 1 - r, n_rows - 2 - r) for r in r...  33.8 us
  transfers between devices with their start and end apart: 68, of which 22 were waited for; matrix products, arithmetic and copies ran while one was open for 5% of the time, Pallas kernels for 38%

profile of v4, /device:TPU:16, one launch (start us, length us, event | category | flops | bytes accessed | tf_op | source)
XLA Modules:
  0.0 779.1 jit_solution(6174396398437770407)
XLA Ops:
  22.7 12.1 %shard_map.68 = (bf16[3072,1024]{1,0:T(8,128)(2,1)}, bf16[1024,3072]{1,0:T(8,128)(2,1)}) custom-call(bf16[12,256,1024]{2,1,0:T(8,128)(2,1)} %bitcast.40, bf16[384,384]{1,0:T(8,128)(2,1)} %fusion.9.order_ref), custom_call_target="tpu_custom_call" | custom-call | flops 301989888 | bytes 1179648 | tf_op jit(solution)/shard_map/pallas_call | solution.py:50
  53.4 9.8 %shard_map.69 = (bf16[1024,1536]{1,0:T(8,128)(2,1)}, bf16[1024,1536]{1,0:T(8,128)(2,1)}) custom-call(bf16[12,1024,256]{2,1,0:T(8,128)(2,1)} %bitcast.41), custom_call_target="tpu_custom_call" | custom-call | bytes 786432 | tf_op jit(solution)/shard_map/pallas_call | solution.py:79
  69.2 8.1 %collective-permute-done.4.refs_0_ = bf16[256,1024]{1,0:T(8,128)(2,1)S(1)} collective-permute-done((bf16[256,1024]{1,0:T(8,128)(2,1)}, bf16[256,1024]{1,0:T(8,128)(2,1)S(1)}, u32[]{:S(2)}, u32[]{:S(2)}) %collective-permute-start.4) | collective-permute-done | bytes 524320 | tf_op jit(solution)/shard_map/ppermute | solution.py:270
  96.0 128.3 %shard_map.70.theta_ref = bf16[1024,2048]{1,0:T(8,128)(2,1)} custom-call(bf16[256,1024]{1,0:T(8,128)(2,1)} %copy-done.53, bf16[256,1024]{1,0:T(8,128)(2,1)} %collective-permute-done.2.refs_1_, bf16[256,1024]{1,0:T(8,128)(2,1)} %collective-permute-done.refs_2_, bf16[256,1024]{1,0:T(8,128)(2,1)} %bitcast.45, bf16[256,1024]{1,0:T(8,128)(2,1)} %collective-permute-done.1.refs_4_, ...), custom_call_target="tpu_custom_call" | custom-call | bytes 524288 | tf_op jit(solution)/shard_map/pallas_call | solution.py:255
  225.2 21.4 %shard_map.71.refs_0_ = f32[1024,2048]{1,0:T(8,128)} custom-call(bf16[1024,2048]{1,0:T(8,128)(2,1)} %shard_map.70.theta_ref, bf16[3072,1024]{1,0:T(8,128)(2,1)} %get-tuple-element.117.left_ref, bf16[384,384]{1,0:T(8,128)(2,1)S(1)} %copy-done.6, bf16[1024,1536]{1,0:T(8,128)(2,1)S(1)} %copy-done.3), custom_call_target="tpu_custom_call" | custom-call | flops 956301312 | bytes 1179648 | tf_op jit(solution)/shard_map/pallas_call | solution.py:123
  271.2 21.5 %shard_map.72.refs_0_ = f32[1024,2048]{1,0:T(8,128)} custom-call(bf16[1024,2048]{1,0:T(8,128)(2,1)} %shard_map.70.theta_ref, bf16[3072,1024]{1,0:T(8,128)(2,1)} %get-tuple-element.117.left_ref, bf16[384,384]{1,0:T(8,128)(2,1)S(1)} %copy-done.6, bf16[1024,1536]{1,0:T(8,128)(2,1)S(1)} %copy-done.3), custom_call_target="tpu_custom_call" | custom-call | flops 956301312 | bytes 1179648 | tf_op jit(solution)/shard_map/pallas_call | solution.py:123
  298.0 7.7 collective-permute-done.22.refs_7_
  312.1 128.3 %shard_map.73.theta_ref = bf16[1024,2048]{1,0:T(8,128)(2,1)} custom-call(bf16[256,1024]{1,0:T(8,128)(2,1)} %copy-done.59, bf16[256,1024]{1,0:T(8,128)(2,1)} %collective-permute-done.14.refs_1_, bf16[256,1024]{1,0:T(8,128)(2,1)} %collective-permute-done.6.refs_2_, bf16[256,1024]{1,0:T(8,128)(2,1)} %bitcast.37.refs_3_, ...), custom_call_target="tpu_custom_call" | custom-call | bytes 524288 | tf_op jit(solution)/shard_map/pallas_call | solution.py:255
  441.4 12.1 %shard_map.74 = bf16[1024,1024]{1,0:T(8,128)(2,1)S(1)} custom-call(bf16[1024,2048]{1,0:T(8,128)(2,1)} %shard_map.73.theta_ref, bf16[3072,1024]{1,0:T(8,128)(2,1)} %get-tuple-element.117.left_ref, bf16[384,384]{1,0:T(8,128)(2,1)S(1)} %copy-done.7, bf16[1024,1536]{1,0:T(8,128)(2,1)S(1)} %copy-done.2, f32[1024,2048]{1,0:T(8,128)} %shard_map.71.refs_0_), custom_call_target="tpu_custom_call" | custom-call | flops 478150656 | bytes 819200 | tf_op jit(solution)/shard_map/pallas_call | solution.py:123
  455.1 12.1 %shard_map.75 = bf16[1024,1024]{1,0:T(8,128)(2,1)S(1)} custom-call(bf16[1024,2048]{1,0:T(8,128)(2,1)} %shard_map.73.theta_ref, bf16[3072,1024]{1,0:T(8,128)(2,1)} %get-tuple-element.117.left_ref, bf16[384,384]{1,0:T(8,128)(2,1)S(1)} %copy-done.7, bf16[1024,1536]{1,0:T(8,128)(2,1)S(1)} %copy-done.2, f32[1024,2048]{1,0:T(8,128)} %shard_map.71.refs_0_), custom_call_target="tpu_custom_call" | custom-call | flops 478150656 | bytes 819200 | tf_op jit(solution)/shard_map/pallas_call | solution.py:123
  474.7 12.1 %shard_map.76 = bf16[1024,1024]{1,0:T(8,128)(2,1)S(1)} custom-call(bf16[1024,2048]{1,0:T(8,128)(2,1)} %shard_map.73.theta_ref, bf16[3072,1024]{1,0:T(8,128)(2,1)} %get-tuple-element.117.left_ref, bf16[384,384]{1,0:T(8,128)(2,1)S(1)} %copy-done.8, bf16[1024,1536]{1,0:T(8,128)(2,1)S(1)} %copy-done.2, f32[1024,2048]{1,0:T(8,128)} %shard_map.72.refs_0_), custom_call_target="tpu_custom_call" | custom-call | flops 478150656 | bytes 819200 | tf_op jit(solution)/shard_map/pallas_call | solution.py:123
  496.9 12.2 %shard_map.77 = bf16[1024,1024]{1,0:T(8,128)(2,1)S(1)} custom-call(bf16[1024,2048]{1,0:T(8,128)(2,1)} %shard_map.73.theta_ref, bf16[3072,1024]{1,0:T(8,128)(2,1)} %get-tuple-element.117.left_ref, bf16[384,384]{1,0:T(8,128)(2,1)S(1)} %copy-done.9, bf16[1024,1536]{1,0:T(8,128)(2,1)S(1)} %copy-done.2, f32[1024,2048]{1,0:T(8,128)} %shard_map.72.refs_0_), custom_call_target="tpu_custom_call" | custom-call | flops 478150656 | bytes 819200 | tf_op jit(solution)/shard_map/pallas_call | solution.py:123
  529.8 10.0 %collective-permute-done.29 = bf16[256,1024]{1,0:T(8,128)(2,1)S(1)} collective-permute-done((bf16[256,1024]{1,0:T(8,128)(2,1)S(1)}, bf16[256,1024]{1,0:T(8,128)(2,1)S(1)}, u32[]{:S(2)}, u32[]{:S(2)}) %collective-permute-start.29) | collective-permute-done | bytes 524320 | tf_op jit(solution)/shard_map/ppermute | solution.py:305
  555.4 9.0 %collective-permute-done.34 = bf16[256,1024]{1,0:T(8,128)(2,1)S(1)} collective-permute-done((bf16[256,1024]{1,0:T(8,128)(2,1)S(1)}, bf16[256,1024]{1,0:T(8,128)(2,1)S(1)}, u32[]{:S(2)}, u32[]{:S(2)}) %collective-permute-start.34) | collective-permute-done | bytes 524320 | tf_op jit(solution)/shard_map/ppermute | solution.py:305
  566.0 7.5 shard_map.80.refs_6_
  581.7 8.3 %shard_map.81.back_ref = bf16[3072,2048]{1,0:T(8,128)(2,1)} custom-call(bf16[256,1024]{1,0:T(8,128)(2,1)} %add_convert_fusion.16.refs_0_, bf16[256,1024]{1,0:T(8,128)(2,1)} %collective-permute-done.38.refs_1_, bf16[256,1024]{1,0:T(8,128)(2,1)} %collective-permute-done.42.refs_2_, ...), custom_call_target="tpu_custom_call", output_to_operand_aliasing={{}: (6, {})} | custom-call | flops 276824064 | bytes 524288 | tf_op jit(solution)/shard_map/pallas_call | solution.py:185
  589.9 10.7 %shard_map.82 = bf16[1024,1024]{1,0:T(8,128)(2,1)S(1)} custom-call(bf16[1024,3072]{1,0:T(8,128)(2,1)} %get-tuple-element.118.left_ref, bf16[3072,2048]{1,0:T(8,128)(2,1)} %shard_map.81.back_ref), custom_call_target="tpu_custom_call" | custom-call | flops 402653184 | bytes 917504 | tf_op jit(solution)/shard_map/pallas_call | solution.py:218
  605.8 10.8 %shard_map.83 = bf16[1024,1024]{1,0:T(8,128)(2,1)S(1)} custom-call(bf16[1024,3072]{1,0:T(8,128)(2,1)} %get-tuple-element.118.left_ref, bf16[3072,2048]{1,0:T(8,128)(2,1)} %shard_map.81.back_ref), custom_call_target="tpu_custom_call" | custom-call | flops 402653184 | bytes 917504 | tf_op jit(solution)/shard_map/pallas_call | solution.py:218
  659.5 7.7 shard_map.85.refs_6_
  682.9 8.3 %shard_map.87.back_ref = bf16[3072,2048]{1,0:T(8,128)(2,1)} custom-call(bf16[256,1024]{1,0:T(8,128)(2,1)} %add_convert_fusion.16.refs_0_, bf16[256,1024]{1,0:T(8,128)(2,1)} %collective-permute-done.38.refs_1_, bf16[256,1024]{1,0:T(8,128)(2,1)} %collective-permute-done.42.refs_2_, ...), custom_call_target="tpu_custom_call", output_to_operand_aliasing={{}: (6, {})} | custom-call | flops 276824064 | bytes 524288 | tf_op jit(solution)/shard_map/pallas_call | solution.py:185
  691.1 10.7 %shard_map.88 = bf16[1024,1024]{1,0:T(8,128)(2,1)S(1)} custom-call(bf16[1024,3072]{1,0:T(8,128)(2,1)} %get-tuple-element.118.left_ref, bf16[3072,2048]{1,0:T(8,128)(2,1)} %shard_map.87.back_ref), custom_call_target="tpu_custom_call" | custom-call | flops 402653184 | bytes 917504 | tf_op jit(solution)/shard_map/pallas_call | solution.py:218
  706.7 10.8 %shard_map.89 = bf16[1024,1024]{1,0:T(8,128)(2,1)S(1)} custom-call(bf16[1024,3072]{1,0:T(8,128)(2,1)} %get-tuple-element.118.left_ref, bf16[3072,2048]{1,0:T(8,128)(2,1)} %shard_map.87.back_ref), custom_call_target="tpu_custom_call" | custom-call | flops 402653184 | bytes 917504 | tf_op jit(solution)/shard_map/pallas_call | solution.py:218
  727.7 7.3 collective-permute-done.63
  769.1 7.9 %collective-permute-done.67 = bf16[256,1024]{1,0:T(8,128)(2,1)S(1)} collective-permute-done((bf16[256,1024]{1,0:T(8,128)(2,1)S(1)}, bf16[256,1024]{1,0:T(8,128)(2,1)S(1)}, u32[]{:S(2)}, u32[]{:S(2)}) %collective-permute-start.67) | collective-permute-done | bytes 524320 | tf_op jit(solution)/shard_map/ppermute | solution.py:290
  (310 shorter events, 282.4 us)
Async XLA Ops:
  3.5 31.4 %collective-permute-start = (bf16[256,1024]{1,0:T(8,128)(2,1)S(1)}, bf16[256,1024]{1,0:T(8,128)(2,1)}, u32[]{:S(2)}, u32[]{:S(2)}) collective-permute-start(bf16[256,1024]{1,0:T(8,128)(2,1)S(1)} %bitcast.43), channel_id=1, source_target_pairs={{0,4},{4,8},{8,12},{1,5},{5,9},{9,13},{2,6},{6,10},{10,14},{3,7},{... | collective-permute-start | bytes 1572872 | tf_op jit(solution)/shard_map/ppermute | solution.py:270
  7.0 27.9 %collective-permute-start.1 = (bf16[256,1024]{1,0:T(8,128)(2,1)S(1)}, bf16[256,1024]{1,0:T(8,128)(2,1)}, u32[]{:S(2)}, u32[]{:S(2)}) collective-permute-start(bf16[256,1024]{1,0:T(8,128)(2,1)S(1)} %bitcast.44), channel_id=1, source_target_pairs={{4,0},{8,4},{12,8},{5,1},{9,5},{13,9},{6,2},{10,6},{14,10},{7,3},{... | collective-permute-start | bytes 1572872 | tf_op jit(solution)/shard_map/ppermute | solution.py:271
  10.2 32.1 %collective-permute-start.8 = (bf16[256,1024]{1,0:T(8,128)(2,1)}, bf16[256,1024]{1,0:T(8,128)(2,1)}, u32[]{:S(2)}, u32[]{:S(2)}) collective-permute-start(bf16[256,1024]{1,0:T(8,128)(2,1)} %bitcast.35.refs_10_), channel_id=1, source_target_pairs={{0,4},{4,8},{8,12},{1,5},{5,9},{9,13},{2,6},{6,10},{10,14},{3,7},{... | collective-permute-start | bytes 1572872 | tf_op jit(solution)/shard_map/ppermute | solution.py:270
  14.5 29.7 %collective-permute-start.11 = (bf16[256,1024]{1,0:T(8,128)(2,1)}, bf16[256,1024]{1,0:T(8,128)(2,1)}, u32[]{:S(2)}, u32[]{:S(2)}) collective-permute-start(bf16[256,1024]{1,0:T(8,128)(2,1)} %bitcast.35.refs_10_), channel_id=1, source_target_pairs={{4,0},{8,4},{12,8},{5,1},{9,5},{13,9},{6,2},{10,6},{14,10},{7,3},{... | collective-permute-start | bytes 1572872 | tf_op jit(solution)/shard_map/ppermute | solution.py:271
  34.8 28.5 %collective-permute-start.2 = (bf16[256,1024]{1,0:T(8,128)(2,1)}, bf16[256,1024]{1,0:T(8,128)(2,1)}, u32[]{:S(2)}, u32[]{:S(2)}) collective-permute-start(bf16[256,1024]{1,0:T(8,128)(2,1)} %collective-permute-done.refs_2_), channel_id=1, source_target_pairs={{4,8},{8,12},{5,9},{9,13},{6,10},{10,14},{7,11},{11,15},{20,24},{2... | collective-permute-start | bytes 1572872 | tf_op jit(solution)/shard_map/ppermute | solution.py:270
  39.5 23.8 %collective-permute-start.3 = (bf16[256,1024]{1,0:T(8,128)(2,1)}, bf16[256,1024]{1,0:T(8,128)(2,1)}, u32[]{:S(2)}, u32[]{:S(2)}) collective-permute-start(bf16[256,1024]{1,0:T(8,128)(2,1)} %collective-permute-done.1.refs_4_), channel_id=1, source_target_pairs={{4,0},{8,4},{5,1},{9,5},{6,2},{10,6},{7,3},{11,7},{20,16},{24,20},... | collective-permute-start | bytes 1572872 | tf_op jit(solution)/shard_map/ppermute | solution.py:271
  65.3 23.2 %collective-permute-start.10 = (bf16[256,1024]{1,0:T(8,128)(2,1)}, bf16[256,1024]{1,0:T(8,128)(2,1)S(1)}, u32[]{:S(2)}, u32[]{:S(2)}) collective-permute-start(bf16[256,1024]{1,0:T(8,128)(2,1)} %collective-permute-done.9.refs_8_), channel_id=1, source_target_pairs={{8,12},{9,13},{10,14},{11,15},{24,28},{25,29},{26,30},{27,31}} | collective-permute-start | bytes 1572872 | tf_op jit(solution)/shard_map/ppermute | solution.py:270
  77.3 169.4 %collective-permute-start.6 = (bf16[256,1024]{1,0:T(8,128)(2,1)}, bf16[256,1024]{1,0:T(8,128)(2,1)}, u32[]{:S(2)}, u32[]{:S(2)}) collective-permute-start(bf16[256,1024]{1,0:T(8,128)(2,1)} %bitcast.37.refs_3_), channel_id=1, source_target_pairs={{0,4},{4,8},{8,12},{1,5},{5,9},{9,13},{2,6},{6,10},{10,14},{3,7},{... | collective-permute-start | bytes 1572872 | tf_op jit(solution)/shard_map/ppermute | solution.py:270
  81.6 165.1 %collective-permute-start.7 = (bf16[256,1024]{1,0:T(8,128)(2,1)}, bf16[256,1024]{1,0:T(8,128)(2,1)}, u32[]{:S(2)}, u32[]{:S(2)}) collective-permute-start(bf16[256,1024]{1,0:T(8,128)(2,1)} %bitcast.37.refs_3_), channel_id=1, source_target_pairs={{4,0},{8,4},{12,8},{5,1},{9,5},{13,9},{6,2},{10,6},{14,10},{7,3},{... | collective-permute-start | bytes 1572872 | tf_op jit(solution)/shard_map/ppermute | solution.py:271
  88.5 165.6 %collective-permute-start.16 = (bf16[256,1024]{1,0:T(8,128)(2,1)}, bf16[256,1024]{1,0:T(8,128)(2,1)}, u32[]{:S(2)}, u32[]{:S(2)}) collective-permute-start(bf16[256,1024]{1,0:T(8,128)(2,1)} %bitcast.34.refs_10_), channel_id=1, source_target_pairs={{0,4},{4,8},{8,12},{1,5},{5,9},{9,13},{2,6},{6,10},{10,14},{3,7},{... | collective-permute-start | bytes 1572872 | tf_op jit(solution)/shard_map/ppermute | solution.py:270
  92.8 161.3 %collective-permute-start.17 = (bf16[256,1024]{1,0:T(8,128)(2,1)}, bf16[256,1024]{1,0:T(8,128)(2,1)}, u32[]{:S(2)}, u32[]{:S(2)}) collective-permute-start(bf16[256,1024]{1,0:T(8,128)(2,1)} %bitcast.34.refs_10_), channel_id=1, source_target_pairs={{4,0},{8,4},{12,8},{5,1},{9,5},{13,9},{6,2},{10,6},{14,10},{7,3},{... | collective-permute-start | bytes 1572872 | tf_op jit(solution)/shard_map/ppermute | solution.py:271
  487.9 30.7 %collective-permute-start.28 = (bf16[512,1024]{1,0:T(8,128)(2,1)}, bf16[512,1024]{1,0:T(8,128)(2,1)}, u32[]{:S(2)}, u32[]{:S(2)}) collective-permute-start(bf16[512,1024]{1,0:T(8,128)(2,1)} %constant_dynamic-slice_fusion.11), channel_id=1, source_target_pairs={{0,2},{2,0},{1,3},{3,1},{4,6},{6,4},{5,7},{7,5},{8,10},{10,8},{9,1... | collective-permute-start | bytes 3145736 | tf_op jit(solution)/shard_map/ppermute | solution.py:305
  494.4 24.2 %collective-permute-start.31 = (bf16[256,1024]{1,0:T(8,128)(2,1)S(1)}, bf16[256,1024]{1,0:T(8,128)(2,1)S(1)}, u32[]{:S(2)}, u32[]{:S(2)}) collective-permute-start(bf16[256,1024]{1,0:T(8,128)(2,1)S(1)} %add_convert_fusion.19.refs_0_), channel_id=1, source_target_pairs={{0,1},{1,0},{2,3},{3,2},{4,5},{5,4},{6,7},{7,6},{8,9},{9,8},{10,11... | collective-permute-start | bytes 1572872 | tf_op jit(solution)/shard_map/ppermute | solution.py:305
  495.9 25.2 %collective-permute-start.32 = (bf16[256,1024]{1,0:T(8,128)(2,1)S(1)}, bf16[256,1024]{1,0:T(8,128)(2,1)S(1)}, u32[]{:S(2)}, u32[]{:S(2)}) collective-permute-start(bf16[256,1024]{1,0:T(8,128)(2,1)S(1)} %add_convert_fusion.19.refs_0_), channel_id=1, source_target_pairs={{0,2},{2,0},{1,3},{3,1},{4,6},{6,4},{5,7},{7,5},{8,10},{10,8},{9,1... | collective-permute-start | bytes 1572872 | tf_op jit(solution)/shard_map/ppermute | solution.py:305
  511.3 28.8 %collective-permute-start.30 = (bf16[512,1024]{1,0:T(8,128)(2,1)S(1)}, bf16[512,1024]{1,0:T(8,128)(2,1)S(1)}, u32[]{:S(2)}, u32[]{:S(2)}) collective-permute-start(bf16[512,1024]{1,0:T(8,128)(2,1)S(1)} %constant_dynamic-slice_fusion.9), channel_id=1, source_target_pairs={{0,2},{2,0},{1,3},{3,1},{4,6},{6,4},{5,7},{7,5},{8,10},{10,8},{9,1... | collective-permute-start | bytes 3145736 | tf_op jit(solution)/shard_map/ppermute | solution.py:305
  541.1 23.3 %collective-permute-start.34 = (bf16[256,1024]{1,0:T(8,128)(2,1)S(1)}, bf16[256,1024]{1,0:T(8,128)(2,1)S(1)}, u32[]{:S(2)}, u32[]{:S(2)}) collective-permute-start(bf16[256,1024]{1,0:T(8,128)(2,1)S(1)} %constant_dynamic-slice_fusion.8), channel_id=1, source_target_pairs={{0,1},{1,0},{2,3},{3,2},{4,5},{5,4},{6,7},{7,6},{8,9},{9,8},{10,11... | collective-permute-start | bytes 1572872 | tf_op jit(solution)/shard_map/ppermute | solution.py:305
  542.6 23.3 %collective-permute-start.40 = (bf16[256,1024]{1,0:T(8,128)(2,1)S(1)}, bf16[256,1024]{1,0:T(8,128)(2,1)S(1)}, u32[]{:S(2)}, u32[]{:S(2)}) collective-permute-start(bf16[256,1024]{1,0:T(8,128)(2,1)S(1)} %add_convert_fusion.17.refs_0_), channel_id=1, source_target_pairs={{0,2},{2,0},{1,3},{3,1},{4,6},{6,4},{5,7},{7,5},{8,10},{10,8},{9,1... | collective-permute-start | bytes 1572872 | tf_op jit(solution)/shard_map/ppermute | solution.py:305
  636.9 37.7 %collective-permute-start.52 = (bf16[256,1024]{1,0:T(8,128)(2,1)}, bf16[256,1024]{1,0:T(8,128)(2,1)}, u32[]{:S(2)}, u32[]{:S(2)}) collective-permute-start(bf16[256,1024]{1,0:T(8,128)(2,1)} %get-tuple-element.189), channel_id=1, source_target_pairs={{0,4},{4,8},{1,5},{5,9},{2,6},{6,10},{3,7},{7,11},{16,20},{20,24},... | collective-permute-start | bytes 1572872 | tf_op jit(solution)/shard_map/ppermute | solution.py:289
  638.2 36.4 %collective-permute-start.53 = (bf16[256,1024]{1,0:T(8,128)(2,1)}, bf16[256,1024]{1,0:T(8,128)(2,1)}, u32[]{:S(2)}, u32[]{:S(2)}) collective-permute-start(bf16[256,1024]{1,0:T(8,128)(2,1)} %get-tuple-element.190), channel_id=1, source_target_pairs={{12,8},{8,4},{13,9},{9,5},{14,10},{10,6},{15,11},{11,7},{28,24},{2... | collective-permute-start | bytes 1572872 | tf_op jit(solution)/shard_map/ppermute | solution.py:290
  649.0 33.9 %collective-permute-start.48 = (bf16[256,1024]{1,0:T(8,128)(2,1)}, bf16[256,1024]{1,0:T(8,128)(2,1)}, u32[]{:S(2)}, u32[]{:S(2)}) collective-permute-start(bf16[256,1024]{1,0:T(8,128)(2,1)} %get-tuple-element.183), channel_id=1, source_target_pairs={{0,4},{4,8},{8,12},{1,5},{5,9},{9,13},{2,6},{6,10},{10,14},{3,7},{... | collective-permute-start | bytes 1572872 | tf_op jit(solution)/shard_map/ppermute | solution.py:289
  650.9 32.0 %collective-permute-start.49 = (bf16[256,1024]{1,0:T(8,128)(2,1)}, bf16[256,1024]{1,0:T(8,128)(2,1)}, u32[]{:S(2)}, u32[]{:S(2)}) collective-permute-start(bf16[256,1024]{1,0:T(8,128)(2,1)} %get-tuple-element.184), channel_id=1, source_target_pairs={{12,8},{8,4},{4,0},{13,9},{9,5},{5,1},{14,10},{10,6},{6,2},{15,11}... | collective-permute-start | bytes 1572872 | tf_op jit(solution)/shard_map/ppermute | solution.py:290
  676.2 30.5 %collective-permute-start.54 = (bf16[256,1024]{1,0:T(8,128)(2,1)S(1)}, bf16[256,1024]{1,0:T(8,128)(2,1)S(1)}, u32[]{:S(2)}, u32[]{:S(2)}) collective-permute-start(bf16[256,1024]{1,0:T(8,128)(2,1)S(1)} %get-tuple-element.201), channel_id=1, source_target_pairs={{0,4},{4,8},{8,12},{1,5},{5,9},{9,13},{2,6},{6,10},{10,14},{3,7},{... | collective-permute-start | bytes 1572872 | tf_op jit(solution)/shard_map/ppermute | solution.py:289
  678.4 28.3 %collective-permute-start.55 = (bf16[256,1024]{1,0:T(8,128)(2,1)S(1)}, bf16[256,1024]{1,0:T(8,128)(2,1)S(1)}, u32[]{:S(2)}, u32[]{:S(2)}) collective-permute-start(bf16[256,1024]{1,0:T(8,128)(2,1)S(1)} %get-tuple-element.202), channel_id=1, source_target_pairs={{12,8},{8,4},{4,0},{13,9},{9,5},{5,1},{14,10},{10,6},{6,2},{15,11}... | collective-permute-start | bytes 1572872 | tf_op jit(solution)/shard_map/ppermute | solution.py:290
  721.2 25.1 %collective-permute-start.59 = (bf16[256,1024]{1,0:T(8,128)(2,1)S(1)}, bf16[256,1024]{1,0:T(8,128)(2,1)S(1)}, u32[]{:S(2)}, u32[]{:S(2)}) collective-permute-start(bf16[256,1024]{1,0:T(8,128)(2,1)S(1)} %get-tuple-element.213), channel_id=1, source_target_pairs={{12,8},{8,4},{13,9},{9,5},{14,10},{10,6},{15,11},{11,7},{28,24},{2... | collective-permute-start | bytes 1572872 | tf_op jit(solution)/shard_map/ppermute | solution.py:290
  (105 other events, 1481.7 us)

commit v5 on v4

--- a/solution.py
+++ b/solution.py
@@ -146,66 +146,69 @@
     )(theta, left, mpo, right, *totals)
 
 
-def back_kernel(channels, n_parts, scattered, *refs):
+def back_kernel(channels, n_parts, n_halves, scattered, *refs):
     parts = refs[:n_parts]
-    mpo_ref, right_ref = refs[n_parts : n_parts + 2]
-    out_ref, joined, ones = refs[-3:]
-    lanes = right_ref.shape[1] // channels
-    phys_pair = out_ref.shape[1] // lanes
+    mpo_ref, rights = refs[n_parts], refs[n_parts + 1 : n_parts + 1 + n_halves]
+    outs, joined, ones = refs[-2 - n_halves : -2], refs[-2], refs[-1]
+    lanes = rights[0].shape[1] // channels
+    phys_pair = outs[0].shape[1] // lanes
     pair, step = 2 * channels, 2 * phys_pair
-    pairs = out_ref.shape[0] // pair
+    pairs = outs[0].shape[0] // pair
     height = parts[0].shape[0]
     for k, part in enumerate(parts):
         place = block_of(k) if scattered else k
         joined[pl.ds(pl.multiple_of(place * height, height), height), :] = part[...]
-    full = dot(joined[...], right_ref[...], COLS).astype(BF16)
-    for i in range(pairs):
-        for v in range(channels):
-            ones[v * step : (v + 1) * step, i * lanes : (i + 1) * lanes] = full[
-                i * step : (i + 1) * step, v * lanes : (v + 1) * lanes
-            ]
-    mixed = dot(mpo_ref[...], ones[...])
-    for i in range(0, pairs, 2):
-        for s in range(phys_pair):
-            both = [
-                mixed[s * pair : (s + 1) * pair, j * lanes : (j + 1) * lanes] for j in (i, i + 1)
-            ]
-            out_ref[i * pair : (i + 2) * pair, s * lanes : (s + 1) * lanes] = jnp.concatenate(
-                both, axis=0
-            ).astype(BF16)
-
-
-def back(parts, mpo, right, buffer, channels, phys_pair, group, groups, scattered, tile):
+    for right_ref, out_ref in zip(rights, outs):
+        full = dot(joined[...], right_ref[...], COLS).astype(BF16)
+        for i in range(pairs):
+            for v in range(channels):
+                ones[v * step : (v + 1) * step, i * lanes : (i + 1) * lanes] = full[
+                    i * step : (i + 1) * step, v * lanes : (v + 1) * lanes
+                ]
+        mixed = dot(mpo_ref[...], ones[...])
+        for i in range(0, pairs, 2):
+            for s in range(phys_pair):
+                both = [
+                    mixed[s * pair : (s + 1) * pair, j * lanes : (j + 1) * lanes]
+                    for j in (i, i + 1)
+                ]
+                out_ref[i * pair : (i + 2) * pair, s * lanes : (s + 1) * lanes] = jnp.concatenate(
+                    both, axis=0
+                ).astype(BF16)
+
+
+def back(parts, mpo, rights, buffers, channels, phys_pair, group, groups, scattered, tile):
     columns = parts[0].shape[1]
     bonds = columns // phys_pair
-    far = right.shape[0]
-    lanes = right.shape[1] // channels
+    far, width = rights[0].shape
+    lanes = width // channels
     steps = bonds // tile
-    buffers = [] if buffer is None else [buffer]
-    return pl.pallas_call(
-        functools.partial(back_kernel, channels, len(parts), scattered),
+    count = len(rights)
+    before = len(parts) + 1 + count
+    return pl.pallas_call(
+        functools.partial(back_kernel, channels, len(parts), count, scattered),
         grid=(steps,),
-        input_output_aliases={} if buffer is None else {len(parts) + 2: 0},
+        input_output_aliases={before + k: k for k in range(len(buffers))},
         in_specs=[pl.BlockSpec((p.shape[0], tile * phys_pair), lambda i: (0, i)) for p in parts]
-        + [
-            pl.BlockSpec(mpo.shape, lambda i: (0, 0), pipeline_mode=ONCE),
-            pl.BlockSpec(right.shape, lambda i: (0, 0), pipeline_mode=ONCE),
+        + [pl.BlockSpec(mpo.shape, lambda i: (0, 0), pipeline_mode=ONCE)]
+        + [pl.BlockSpec((far, width), lambda i: (0, 0), pipeline_mode=ONCE)] * count
+        + [ANY] * len(buffers),
+        out_specs=[
+            pl.BlockSpec((tile * channels, phys_pair * lanes), lambda i: (group * steps + i, 0))
         ]
-        + [ANY] * len(buffers),
-        out_specs=pl.BlockSpec(
-            (tile * channels, phys_pair * lanes), lambda i: (group * steps + i, 0)
-        ),
-        out_shape=jax.ShapeDtypeStruct((groups * bonds * channels, phys_pair * lanes), BF16),
+        * count,
+        out_shape=[jax.ShapeDtypeStruct((groups * bonds * channels, phys_pair * lanes), BF16)]
+        * count,
         scratch_shapes=[
             pltpu.VMEM((far, tile * phys_pair), BF16),
             pltpu.VMEM((2 * channels * phys_pair, tile // 2 * lanes), BF16),
         ],
         compiler_params=params(48),
         cost_estimate=cost(
-            2 * right.size * columns + bonds * mpo.size * lanes,
-            2 * (right.size + far * columns + bonds * channels * phys_pair * lanes),
+            count * (2 * far * width * columns + bonds * mpo.size * lanes),
+            2 * count * (far * width + bonds * channels * phys_pair * lanes) + 2 * far * columns,
         ),
-    )(*parts, mpo, right, *buffers)
+    )(*parts, mpo, *rights, *buffers)
 
 
 def last_kernel(left_ref, back_ref, out_ref):
@@ -255,9 +258,10 @@
     return pl.pallas_call(
         functools.partial(join_kernel, n_rows, len(parts)),
         in_specs=[ANY] * len(blocks),
-        out_specs=ANY,
+        out_specs=pl.BlockSpec(memory_space=pltpu.VMEM),
         out_shape=jax.ShapeDtypeStruct((depth * n_rows, columns * len(parts)), BF16),
         scratch_shapes=[pltpu.SemaphoreType.DMA((len(blocks),))],
+        compiler_params=params(16),
         cost_estimate=cost(0, 4 * depth * n_rows * columns * len(parts)),
     )(*blocks)
 
@@ -336,16 +340,18 @@
             pairs.append(after((piece, piece), *last_round[c]))
             blocks.append([piece])
         for t in range(1, n_rows):
-            if h == 0 and t > 1:
-                waits = [left, left_t] if t == 2 else [mpo_fore, mpo_back, right]
-                pairs[0] = after(pairs[0], *waits)
+            if (h, t) == (0, 2):
+                pairs[0] = after(pairs[0], left, left_t)
+            if (h, t) == (1, 1):
+                pairs[0] = after(pairs[0], mpo_fore, mpo_back, right)
             if h > 0 and t > 1 and len(fresh) < cuts:
-                held = theta_all if t == 2 else after(theta_all, *pairs)
+                held = theta_all if t == 2 else after(theta_all, *sent)
                 fresh += [
                     fore(held, left, mpo_fore, right[h - 1], total[0], channels, len(fresh), cuts,
                          F32, tile)
                 ]
                 pairs = [after(pair, fresh[-1]) for pair in pairs]
+            sent = list(pairs)
             for c in range(n_chunks):
                 pairs[c] = gather_round(pairs[c], t, n_rows)
                 blocks[c] = [pairs[c][0]] + blocks[c] + [pairs[c][1]]
@@ -365,13 +371,11 @@
             BF16, tile, g % (groups // len(total)),
         )
 
-    def backward(h, g, parts, backs, *deps):
-        parts = after(parts, *deps)
-        return back(
-            parts, mpo_back, right[h], backs, channels, phys_pair, g, groups, scattered, tile
-        )
-
-    terms, near, own, far, everyone, backs = [], [], [], [], [], None
+    def backward(g, backs, *deps):
+        parts = after(everyone[g], *deps)
+        return back(parts, mpo_back, right, backs, channels, phys_pair, g, groups, scattered, tile)
+
+    terms, near, own, far, everyone, backs = [], [], [], [], [], []
     step = 0
     while len(everyone) < groups or step < 2 * groups:
         g = step - groups
@@ -383,8 +387,8 @@
             terms.append(forward(step, *waits))
             out = terms[-1]
         elif 0 <= g < len(everyone):
-            backs = backward(0, g, everyone[g], backs, *waits)
-            out = backs
+            backs = backward(g, backs, *waits)
+            out = backs[-1]
         step += 1
         if not scattered:
             if step <= groups:
@@ -404,7 +408,7 @@
             mine, other = halved(terms[len(near)], "col")
             near.append(add(mine, swapped(other, "col")))
     for g in range(step - groups, groups):
-        backs = backward(0, g, everyone[g], backs)
+        backs = backward(g, backs)
 
     terms, rounds = [], []
 
@@ -419,27 +423,14 @@
     def come(i, t):
         return list(rounds[i][min(t, len(rounds[i])) - 1])
 
-    for h in range(halves):
-        first = len(terms)
-        if h > 0:
-            one, two, backs = first - n_chunks, first - 1, None
-            for g, parts in enumerate(everyone):
-                waits = [terms[-1]] + come(one, 1) if g == 0 else []
-                if g == 1:
-                    waits = come(one, 2) + come(two, 1)
-                    advance(one, backs)
-                    advance(two, backs)
-                elif g > 1 and g == groups - 1:
-                    waits = come(one, 3) + come(two, 2)
-                    advance(two, backs)
-                backs = backward(h, g, parts, backs, *waits)
-        for c in range(n_chunks):
-            waits = come(first - 1, 3) if h > 0 and c > 0 else []
-            waits += sent + terms[first:] if c > 0 else []
-            terms.append(last(left_t, after(backs, *waits), c, n_chunks))
-            rounds.append([])
-            for i in range(first, len(terms)):
-                sent = advance(i, terms[-1])
+    for i in range(halves * n_chunks):
+        waits = sent + terms[-1:] if i > 0 else []
+        waits += come(i - 2, 1) if i > 1 else []
+        waits += come(i - 3, 2) if i > 2 else []
+        terms.append(last(left_t, after(backs[i // n_chunks], *waits), i % n_chunks, n_chunks))
+        rounds.append([])
+        for j in range(i + 1):
+            sent = advance(j, terms[-1])
     products = []
     for i in range(len(terms)):
         while len(rounds[i]) < n_rows - 1:

time: 790 us -> 515 us (0.65)
  Pallas kernels: 474 us -> 218 us
  waiting for transfers between devices: 109 us -> 56.9 us
  starting transfers between devices: 130 us -> 151 us
  local copies, waits for them, and re-layouts: 33.6 us -> 47.5 us
    pallas_call x2, Pallas kernels: 257 us -> 3.31 us  [join(): pl.pallas_call(functools.partial(join_kernel, n_rows, len(parts)), in_spe...]
    ppermute x12, waiting for transfers between devices: 32.2 us -> 7.04 us  [gather_round(): lax.ppermute(pair[0], 'row', [(r, r + 1) for r in range(t - 1, n_rows - 1)])]
    ppermute x20, waiting for transfers between devices: 39.1 us -> 20.7 us  [swapped(): return lax.ppermute(block, axis, [(0, 1), (1, 0)])]
    ppermute x12, starting transfers between devices: 40.7 us -> 52.8 us  [scatter_round(): lax.ppermute(pair[1], 'row', [(n_rows - 1 - r, n_rows - 2 - r) for r in r...]
    ppermute x12, starting transfers between devices: 28.9 us -> 38.1 us  [gather_round(): lax.ppermute(pair[1], 'row', [(r, r - 1) for r in range(1, n_rows - t + 1)])]
    ppermute x12, waiting for transfers between devices: 33.8 us -> 25.7 us  [scatter_round(): lax.ppermute(pair[1], 'row', [(n_rows - 1 - r, n_rows - 2 - r) for r in r...]
    unnamed x130 -> x102, local copies, waits for them, and re-layouts: 18.3 us -> 23.2 us
    pallas_call x8 -> x4, Pallas kernels: 60.8 us -> 57.8 us  [back(): pl.pallas_call(functools.partial(back_kernel, channels, len(parts), count...]
  transfers between devices with their start and end apart: 68 -> 68, of which waited for: 22 -> 12; matrix products, arithmetic and copies ran while one was open for 5% -> 10% of each run, Pallas kernels for 38% -> 35%
where the time goes in v5:
time: 515 us; the launch traced here: 506 us
  Pallas kernels  218 us (42%)
  starting transfers between devices  151 us (29%)
  waiting for transfers between devices  56.9 us (11%)
  local copies, waits for them, and re-layouts  47.5 us (9%)
  other arithmetic  28 us (5%)
    pallas_call x6, Pallas kernels, fore(): pl.pallas_call(functools.partial(fore_kernel, channels, lanes), grid=(ste...  91.6 us
    pallas_call x4, Pallas kernels, back(): pl.pallas_call(functools.partial(back_kernel, channels, len(parts), count...  57.8 us
    ppermute x12, starting transfers between devices, scatter_round(): lax.ppermute(pair[1], 'row', [(n_rows - 1 - r, n_rows - 2 - r) for r in r...  52.8 us
    pallas_call x4, Pallas kernels, last(): pl.pallas_call(last_kernel, grid=(steps,), in_specs=[pl.BlockSpec(left_t....  43.2 us
    ppermute x12, starting transfers between devices, gather_round(): lax.ppermute(pair[1], 'row', [(r, r - 1) for r in range(1, n_rows - t + 1)])  38.1 us
    ppermute x12, starting transfers between devices, gather_round(): lax.ppermute(pair[0], 'row', [(r, r + 1) for r in range(t - 1, n_rows - 1)])  28.1 us
    ppermute x12, waiting for transfers between devices, scatter_round(): lax.ppermute(pair[1], 'row', [(n_rows - 1 - r, n_rows - 2 - r) for r in r...  25.7 us
    unnamed x102, local copies, waits for them, and re-layouts  23.2 us
  transfers between devices with their start and end apart: 68, of which 12 were waited for; matrix products, arithmetic and copies ran while one was open for 10% of the time, Pallas kernels for 35%

profile of v5, /device:TPU:16, one launch (start us, length us, event | category | flops | bytes accessed | tf_op | source)
XLA Modules:
  0.0 506.0 jit_solution(14098106980681161631)
XLA Ops:
  16.2 12.0 %shard_map.68 = (bf16[3072,1024]{1,0:T(8,128)(2,1)}, bf16[1024,3072]{1,0:T(8,128)(2,1)}) custom-call(bf16[12,256,1024]{2,1,0:T(8,128)(2,1)} %bitcast.52, bf16[384,384]{1,0:T(8,128)(2,1)} %fusion.9.order_ref), custom_call_target="tpu_custom_call" | custom-call | flops 301989888 | bytes 1179648 | tf_op jit(solution)/shard_map/pallas_call | solution.py:50
  65.1 7.4 %reshape.54.refs_4_ = bf16[384,384]{1,0:T(8,128)(2,1)S(1)} reshape(bf16[16,2,12,12,2,16]{5,4,3,2,1,0:T(2,128)(2,1)} %multiply_bitcast_fusion) | data formatting | bytes 589824 | tf_op jit(solution)/shard_map/reshape | solution.py:328
  72.5 9.9 %shard_map.69 = (bf16[1024,1536]{1,0:T(8,128)(2,1)}, bf16[1024,1536]{1,0:T(8,128)(2,1)}) custom-call(bf16[12,1024,256]{2,1,0:T(8,128)(2,1)} %bitcast.53), custom_call_target="tpu_custom_call" | custom-call | bytes 786432 | tf_op jit(solution)/shard_map/pallas_call | solution.py:79
  103.6 21.5 %shard_map.71.refs_0_ = f32[1024,2048]{1,0:T(8,128)} custom-call(bf16[1024,2048]{1,0:T(8,128)(2,1)} %copy-done.6, bf16[3072,1024]{1,0:T(8,128)(2,1)} %get-tuple-element.110.left_ref, bf16[384,384]{1,0:T(8,128)(2,1)S(1)} %copy.25.mpo_ref, bf16[1024,1536]{1,0:T(8,128)(2,1)S(1)} %copy-done.3), custom_call_target="tpu_custom_call" | custom-call | flops 956301312 | bytes 1179648 | tf_op jit(solution)/shard_map/pallas_call | solution.py:123
  137.2 21.5 %shard_map.72.refs_0_ = f32[1024,2048]{1,0:T(8,128)} custom-call(bf16[1024,2048]{1,0:T(8,128)(2,1)} %copy-done.6, bf16[3072,1024]{1,0:T(8,128)(2,1)} %get-tuple-element.110.left_ref, bf16[384,384]{1,0:T(8,128)(2,1)S(1)} %copy.25.mpo_ref, bf16[1024,1536]{1,0:T(8,128)(2,1)S(1)} %copy-done.3), custom_call_target="tpu_custom_call" | custom-call | flops 956301312 | bytes 1179648 | tf_op jit(solution)/shard_map/pallas_call | solution.py:123
  187.3 12.1 %shard_map.74 = bf16[1024,1024]{1,0:T(8,128)(2,1)S(1)} custom-call(bf16[1024,2048]{1,0:T(8,128)(2,1)} %copy-done.5, bf16[3072,1024]{1,0:T(8,128)(2,1)} %get-tuple-element.110.left_ref, bf16[384,384]{1,0:T(8,128)(2,1)S(1)} %copy.25.mpo_ref, bf16[1024,1536]{1,0:T(8,128)(2,1)S(1)} %copy-done.2, f32[1024,2048]{1,0:T(8,128)} %shard_map.71.refs_0_), custom_call_target="tpu_custom_call" | custom-call | flops 478150656 | bytes 819200 | tf_op jit(solution)/shard_map/pallas_call | solution.py:123
  201.0 12.1 %shard_map.75 = bf16[1024,1024]{1,0:T(8,128)(2,1)S(1)} custom-call(bf16[1024,2048]{1,0:T(8,128)(2,1)} %copy-done.5, bf16[3072,1024]{1,0:T(8,128)(2,1)} %get-tuple-element.110.left_ref, bf16[384,384]{1,0:T(8,128)(2,1)S(1)} %copy.25.mpo_ref, bf16[1024,1536]{1,0:T(8,128)(2,1)S(1)} %copy-done.2, f32[1024,2048]{1,0:T(8,128)} %shard_map.71.refs_0_), custom_call_target="tpu_custom_call" | custom-call | flops 478150656 | bytes 819200 | tf_op jit(solution)/shard_map/pallas_call | solution.py:123
  220.6 12.1 %shard_map.76 = bf16[1024,1024]{1,0:T(8,128)(2,1)S(1)} custom-call(bf16[1024,2048]{1,0:T(8,128)(2,1)} %copy-done.5, bf16[3072,1024]{1,0:T(8,128)(2,1)} %get-tuple-element.110.left_ref, bf16[384,384]{1,0:T(8,128)(2,1)S(1)} %copy.25.mpo_ref, bf16[1024,1536]{1,0:T(8,128)(2,1)S(1)} %copy-done.2, f32[1024,2048]{1,0:T(8,128)} %shard_map.72.refs_0_), custom_call_target="tpu_custom_call" | custom-call | flops 478150656 | bytes 819200 | tf_op jit(solution)/shard_map/pallas_call | solution.py:123
  241.7 12.5 %shard_map.77 = bf16[1024,1024]{1,0:T(8,128)(2,1)S(1)} custom-call(bf16[1024,2048]{1,0:T(8,128)(2,1)} %copy-done.5, bf16[3072,1024]{1,0:T(8,128)(2,1)} %get-tuple-element.110.left_ref, bf16[384,384]{1,0:T(8,128)(2,1)S(1)} %copy.25.mpo_ref, bf16[1024,1536]{1,0:T(8,128)(2,1)S(1)} %copy-done.2, f32[1024,2048]{1,0:T(8,128)} %shard_map.72.refs_0_), custom_call_target="tpu_custom_call" | custom-call | flops 478150656 | bytes 819200 | tf_op jit(solution)/shard_map/pallas_call | solution.py:123
  256.6 7.9 %collective-permute-done.31.refs_1_ = bf16[256,1024]{1,0:T(8,128)(2,1)S(1)} collective-permute-done((bf16[256,1024]{1,0:T(8,128)(2,1)S(1)}, bf16[256,1024]{1,0:T(8,128)(2,1)S(1)}, u32[]{:S(2)}, u32[]{:S(2)}) %collective-permute-start.31) | collective-permute-done | bytes 524320 | tf_op jit(solution)/shard_map/ppermute | solution.py:309
  267.0 14.3 %shard_map.78 = (bf16[3072,2048]{1,0:T(8,128)(2,1)}, bf16[3072,2048]{1,0:T(8,128)(2,1)}) custom-call(bf16[256,1024]{1,0:T(8,128)(2,1)S(1)} %add_convert_fusion.19.refs_0_, bf16[256,1024]{1,0:T(8,128)(2,1)S(1)} %collective-permute-done.31.refs_1_, bf16[256,1024]{1,0:T(8,128)(2,1)S(1)} %collective-permute-done.32.refs_2_, ...), custom_call_target="tpu_custom_call" | custom-call | flops 553648128 | bytes 917504 | tf_op jit(solution)/shard_map/pallas_call | solution.py:188
  288.5 14.4 %shard_map.79 = (bf16[3072,2048]{1,0:T(8,128)(2,1)}, bf16[3072,2048]{1,0:T(8,128)(2,1)}) custom-call(bf16[256,1024]{1,0:T(8,128)(2,1)S(1)} %add_convert_fusion.18.refs_0_, bf16[256,1024]{1,0:T(8,128)(2,1)S(1)} %collective-permute-done.35.refs_1_, ...), custom_call_target="tpu_custom_call", output_to_operand_aliasing={{0}: (7, {}), {1}: (8, {})} | custom-call | flops 553648128 | bytes 917504 | tf_op jit(solution)/shard_map/pallas_call | solution.py:188
  311.8 14.3 %shard_map.80 = (bf16[3072,2048]{1,0:T(8,128)(2,1)}, bf16[3072,2048]{1,0:T(8,128)(2,1)}) custom-call(bf16[256,1024]{1,0:T(8,128)(2,1)S(1)} %add_convert_fusion.17.refs_0_, bf16[256,1024]{1,0:T(8,128)(2,1)S(1)} %collective-permute-done.39.refs_1_, ...), custom_call_target="tpu_custom_call", output_to_operand_aliasing={{0}: (7, {}), {1}: (8, {})} | custom-call | flops 553648128 | bytes 917504 | tf_op jit(solution)/shard_map/pallas_call | solution.py:188
  328.5 14.8 %shard_map.81 = (bf16[3072,2048]{1,0:T(8,128)(2,1)}, bf16[3072,2048]{1,0:T(8,128)(2,1)}) custom-call(bf16[256,1024]{1,0:T(8,128)(2,1)} %add_convert_fusion.16.refs_0_, bf16[256,1024]{1,0:T(8,128)(2,1)} %collective-permute-done.38.refs_1_, bf16[256,1024]{1,0:T(8,128)(2,1)} %collective-permute-done.42.refs_2_, ...), custom_call_target="tpu_custom_call", output_to_operand_aliasing={{0}: (7, {}), {1}: (8, {})} | custom-call | flops 553648128 | bytes 917504 | tf_op jit(solution)/shard_map/pallas_call | solution.py:188
  343.3 10.7 %shard_map.82 = bf16[1024,1024]{1,0:T(8,128)(2,1)S(1)} custom-call(bf16[1024,3072]{1,0:T(8,128)(2,1)} %get-tuple-element.111.left_ref, bf16[3072,2048]{1,0:T(8,128)(2,1)} %get-tuple-element.172.back_ref), custom_call_target="tpu_custom_call" | custom-call | flops 402653184 | bytes 917504 | tf_op jit(solution)/shard_map/pallas_call | solution.py:221
  358.0 10.8 %shard_map.83 = bf16[1024,1024]{1,0:T(8,128)(2,1)S(1)} custom-call(bf16[1024,3072]{1,0:T(8,128)(2,1)} %get-tuple-element.111.left_ref, bf16[3072,2048]{1,0:T(8,128)(2,1)} %get-tuple-element.172.back_ref), custom_call_target="tpu_custom_call" | custom-call | flops 402653184 | bytes 917504 | tf_op jit(solution)/shard_map/pallas_call | solution.py:221
  380.7 10.7 %shard_map.84 = bf16[1024,1024]{1,0:T(8,128)(2,1)S(1)} custom-call(bf16[1024,3072]{1,0:T(8,128)(2,1)} %get-tuple-element.111.left_ref, bf16[3072,2048]{1,0:T(8,128)(2,1)} %get-tuple-element.191.back_ref), custom_call_target="tpu_custom_call" | custom-call | flops 402653184 | bytes 917504 | tf_op jit(solution)/shard_map/pallas_call | solution.py:221
  409.8 11.0 %shard_map.85 = bf16[1024,1024]{1,0:T(8,128)(2,1)S(1)} custom-call(bf16[1024,3072]{1,0:T(8,128)(2,1)} %get-tuple-element.111.left_ref, bf16[3072,2048]{1,0:T(8,128)(2,1)} %get-tuple-element.191.back_ref), custom_call_target="tpu_custom_call" | custom-call | flops 402653184 | bytes 917504 | tf_op jit(solution)/shard_map/pallas_call | solution.py:221
  431.0 7.5 %collective-permute-done.63 = bf16[256,1024]{1,0:T(8,128)(2,1)S(1)} collective-permute-done((bf16[256,1024]{1,0:T(8,128)(2,1)S(1)}, bf16[256,1024]{1,0:T(8,128)(2,1)S(1)}, u32[]{:S(2)}, u32[]{:S(2)}) %collective-permute-start.63) | collective-permute-done | bytes 524320 | tf_op jit(solution)/shard_map/ppermute | solution.py:294
  438.4 9.6 %collective-permute-start.59 = (bf16[256,1024]{1,0:T(8,128)(2,1)S(1)}, bf16[256,1024]{1,0:T(8,128)(2,1)S(1)}, u32[]{:S(2)}, u32[]{:S(2)}) collective-permute-start(bf16[256,1024]{1,0:T(8,128)(2,1)S(1)} %get-tuple-element.199), channel_id=1, source_target_pairs={{12,8},{8,4},{13,9},{9,5},{14,10},{10,6},{15,11},{11,7},{28,24},{2... | collective-permute-start | bytes 1572872 | tf_op jit(solution)/shard_map/ppermute | solution.py:294
  458.9 9.7 %collective-permute-start.55 = (bf16[256,1024]{1,0:T(8,128)(2,1)S(1)}, bf16[256,1024]{1,0:T(8,128)(2,1)S(1)}, u32[]{:S(2)}, u32[]{:S(2)}) collective-permute-start(bf16[256,1024]{1,0:T(8,128)(2,1)S(1)} %get-tuple-element.195), channel_id=1, source_target_pairs={{12,8},{8,4},{4,0},{13,9},{9,5},{5,1},{14,10},{10,6},{6,2},{15,11}... | collective-permute-start | bytes 1572872 | tf_op jit(solution)/shard_map/ppermute | solution.py:294
  470.9 8.9 %collective-permute-start.61 = (bf16[256,1024]{1,0:T(8,128)(2,1)S(1)}, bf16[256,1024]{1,0:T(8,128)(2,1)S(1)}, u32[]{:S(2)}, u32[]{:S(2)}) collective-permute-start(bf16[256,1024]{1,0:T(8,128)(2,1)S(1)} %get-tuple-element.203), channel_id=1, source_target_pairs={{12,8},{8,4},{4,0},{13,9},{9,5},{5,1},{14,10},{10,6},{6,2},{15,11}... | collective-permute-start | bytes 1572872 | tf_op jit(solution)/shard_map/ppermute | solution.py:294
  486.5 8.1 %collective-permute-done.61 = bf16[256,1024]{1,0:T(8,128)(2,1)S(1)} collective-permute-done((bf16[256,1024]{1,0:T(8,128)(2,1)S(1)}, bf16[256,1024]{1,0:T(8,128)(2,1)S(1)}, u32[]{:S(2)}, u32[]{:S(2)}) %collective-permute-start.61) | collective-permute-done | bytes 524320 | tf_op jit(solution)/shard_map/ppermute | solution.py:294
  495.2 8.6 %collective-permute-done.67 = bf16[256,1024]{1,0:T(8,128)(2,1)S(1)} collective-permute-done((bf16[256,1024]{1,0:T(8,128)(2,1)S(1)}, bf16[256,1024]{1,0:T(8,128)(2,1)S(1)}, u32[]{:S(2)}, u32[]{:S(2)}) %collective-permute-start.67) | collective-permute-done | bytes 524320 | tf_op jit(solution)/shard_map/ppermute | solution.py:294
  (276 shorter events, 221.6 us)
Async XLA Ops:
  9.5 26.2 %collective-permute-start.8 = (bf16[256,1024]{1,0:T(8,128)(2,1)S(1)}, bf16[256,1024]{1,0:T(8,128)(2,1)S(1)}, u32[]{:S(2)}, u32[]{:S(2)}) collective-permute-start(bf16[256,1024]{1,0:T(8,128)(2,1)S(1)} %bitcast.49), channel_id=1, source_target_pairs={{0,4},{4,8},{8,12},{1,5},{5,9},{9,13},{2,6},{6,10},{10,14},{3,7},{... | collective-permute-start | bytes 1572872 | tf_op jit(solution)/shard_map/ppermute | solution.py:274
  53.2 29.4 %collective-permute-start.3 = (bf16[256,1024]{1,0:T(8,128)(2,1)}, bf16[256,1024]{1,0:T(8,128)(2,1)}, u32[]{:S(2)}, u32[]{:S(2)}) collective-permute-start(bf16[256,1024]{1,0:T(8,128)(2,1)} %collective-permute-done.2.refs_1_), channel_id=1, source_target_pairs={{8,12},{9,13},{10,14},{11,15},{24,28},{25,29},{26,30},{27,31}} | collective-permute-start | bytes 1572872 | tf_op jit(solution)/shard_map/ppermute | solution.py:274
  55.3 27.4 %collective-permute-start.5 = (bf16[256,1024]{1,0:T(8,128)(2,1)}, bf16[256,1024]{1,0:T(8,128)(2,1)}, u32[]{:S(2)}, u32[]{:S(2)}) collective-permute-start(bf16[256,1024]{1,0:T(8,128)(2,1)} %collective-permute-done.4.refs_5_), channel_id=1, source_target_pairs={{4,0},{5,1},{6,2},{7,3},{20,16},{21,17},{22,18},{23,19}} | collective-permute-start | bytes 1572872 | tf_op jit(solution)/shard_map/ppermute | solution.py:275
  82.7 42.3 %collective-permute-start.16 = (bf16[256,1024]{1,0:T(8,128)(2,1)S(1)}, bf16[256,1024]{1,0:T(8,128)(2,1)}, u32[]{:S(2)}, u32[]{:S(2)}) collective-permute-start(bf16[256,1024]{1,0:T(8,128)(2,1)S(1)} %bitcast.43), channel_id=1, source_target_pairs={{0,4},{4,8},{8,12},{1,5},{5,9},{9,13},{2,6},{6,10},{10,14},{3,7},{... | collective-permute-start | bytes 1572872 | tf_op jit(solution)/shard_map/ppermute | solution.py:274
  84.6 40.4 %collective-permute-start.17 = (bf16[256,1024]{1,0:T(8,128)(2,1)S(1)}, bf16[256,1024]{1,0:T(8,128)(2,1)}, u32[]{:S(2)}, u32[]{:S(2)}) collective-permute-start(bf16[256,1024]{1,0:T(8,128)(2,1)S(1)} %bitcast.44), channel_id=1, source_target_pairs={{4,0},{8,4},{12,8},{5,1},{9,5},{13,9},{6,2},{10,6},{14,10},{7,3},{... | collective-permute-start | bytes 1572872 | tf_op jit(solution)/shard_map/ppermute | solution.py:275
  90.0 41.2 %collective-permute-start.6 = (bf16[256,1024]{1,0:T(8,128)(2,1)S(1)}, bf16[256,1024]{1,0:T(8,128)(2,1)}, u32[]{:S(2)}, u32[]{:S(2)}) collective-permute-start(bf16[256,1024]{1,0:T(8,128)(2,1)S(1)} %bitcast.40), channel_id=1, source_target_pairs={{0,4},{4,8},{8,12},{1,5},{5,9},{9,13},{2,6},{6,10},{10,14},{3,7},{... | collective-permute-start | bytes 1572872 | tf_op jit(solution)/shard_map/ppermute | solution.py:274
  91.9 39.3 %collective-permute-start.7 = (bf16[256,1024]{1,0:T(8,128)(2,1)S(1)}, bf16[256,1024]{1,0:T(8,128)(2,1)}, u32[]{:S(2)}, u32[]{:S(2)}) collective-permute-start(bf16[256,1024]{1,0:T(8,128)(2,1)S(1)} %bitcast.41), channel_id=1, source_target_pairs={{4,0},{8,4},{12,8},{5,1},{9,5},{13,9},{6,2},{10,6},{14,10},{7,3},{... | collective-permute-start | bytes 1572872 | tf_op jit(solution)/shard_map/ppermute | solution.py:275
  125.0 33.7 %collective-permute-start.20 = (bf16[256,1024]{1,0:T(8,128)(2,1)}, bf16[256,1024]{1,0:T(8,128)(2,1)S(1)}, u32[]{:S(2)}, u32[]{:S(2)}) collective-permute-start(bf16[256,1024]{1,0:T(8,128)(2,1)} %collective-permute-done.16.refs_9_), channel_id=1, source_target_pairs={{4,8},{8,12},{5,9},{9,13},{6,10},{10,14},{7,11},{11,15},{20,24},{2... | collective-permute-start | bytes 1572872 | tf_op jit(solution)/shard_map/ppermute | solution.py:274
  127.3 31.4 %collective-permute-start.21 = (bf16[256,1024]{1,0:T(8,128)(2,1)}, bf16[256,1024]{1,0:T(8,128)(2,1)S(1)}, u32[]{:S(2)}, u32[]{:S(2)}) collective-permute-start(bf16[256,1024]{1,0:T(8,128)(2,1)} %collective-permute-done.17.refs_11_), channel_id=1, source_target_pairs={{4,0},{8,4},{5,1},{9,5},{6,2},{10,6},{7,3},{11,7},{20,16},{24,20},... | collective-permute-start | bytes 1572872 | tf_op jit(solution)/shard_map/ppermute | solution.py:275
  131.3 31.8 %collective-permute-start.14 = (bf16[256,1024]{1,0:T(8,128)(2,1)}, bf16[256,1024]{1,0:T(8,128)(2,1)S(1)}, u32[]{:S(2)}, u32[]{:S(2)}) collective-permute-start(bf16[256,1024]{1,0:T(8,128)(2,1)} %collective-permute-done.6.refs_2_), channel_id=1, source_target_pairs={{4,8},{8,12},{5,9},{9,13},{6,10},{10,14},{7,11},{11,15},{20,24},{2... | collective-permute-start | bytes 1572872 | tf_op jit(solution)/shard_map/ppermute | solution.py:274
  133.2 29.9 %collective-permute-start.15 = (bf16[256,1024]{1,0:T(8,128)(2,1)}, bf16[256,1024]{1,0:T(8,128)(2,1)S(1)}, u32[]{:S(2)}, u32[]{:S(2)}) collective-permute-start(bf16[256,1024]{1,0:T(8,128)(2,1)} %collective-permute-done.7.refs_4_), channel_id=1, source_target_pairs={{4,0},{8,4},{5,1},{9,5},{6,2},{10,6},{7,3},{11,7},{20,16},{24,20},... | collective-permute-start | bytes 1572872 | tf_op jit(solution)/shard_map/ppermute | solution.py:275
  233.8 30.7 %collective-permute-start.28 = (bf16[512,1024]{1,0:T(8,128)(2,1)}, bf16[512,1024]{1,0:T(8,128)(2,1)}, u32[]{:S(2)}, u32[]{:S(2)}) collective-permute-start(bf16[512,1024]{1,0:T(8,128)(2,1)} %constant_dynamic-slice_fusion.11), channel_id=1, source_target_pairs={{0,2},{2,0},{1,3},{3,1},{4,6},{6,4},{5,7},{7,5},{8,10},{10,8},{9,1... | collective-permute-start | bytes 3145736 | tf_op jit(solution)/shard_map/ppermute | solution.py:309
  256.3 29.6 %collective-permute-start.30 = (bf16[512,1024]{1,0:T(8,128)(2,1)S(1)}, bf16[512,1024]{1,0:T(8,128)(2,1)S(1)}, u32[]{:S(2)}, u32[]{:S(2)}) collective-permute-start(bf16[512,1024]{1,0:T(8,128)(2,1)S(1)} %constant_dynamic-slice_fusion.9), channel_id=1, source_target_pairs={{0,2},{2,0},{1,3},{3,1},{4,6},{6,4},{5,7},{7,5},{8,10},{10,8},{9,1... | collective-permute-start | bytes 3145736 | tf_op jit(solution)/shard_map/ppermute | solution.py:309
  374.8 27.5 %collective-permute-start.46 = (bf16[256,1024]{1,0:T(8,128)(2,1)S(1)}, bf16[256,1024]{1,0:T(8,128)(2,1)S(1)}, u32[]{:S(2)}, u32[]{:S(2)}) collective-permute-start(bf16[256,1024]{1,0:T(8,128)(2,1)S(1)} %get-tuple-element.175), channel_id=1, source_target_pairs={{0,4},{4,8},{1,5},{5,9},{2,6},{6,10},{3,7},{7,11},{16,20},{20,24},... | collective-permute-start | bytes 1572872 | tf_op jit(solution)/shard_map/ppermute | solution.py:293
  376.1 27.5 %collective-permute-start.47 = (bf16[256,1024]{1,0:T(8,128)(2,1)S(1)}, bf16[256,1024]{1,0:T(8,128)(2,1)S(1)}, u32[]{:S(2)}, u32[]{:S(2)}) collective-permute-start(bf16[256,1024]{1,0:T(8,128)(2,1)S(1)} %get-tuple-element.176), channel_id=1, source_target_pairs={{12,8},{8,4},{13,9},{9,5},{14,10},{10,6},{15,11},{11,7},{28,24},{2... | collective-permute-start | bytes 1572872 | tf_op jit(solution)/shard_map/ppermute | solution.py:294
  393.1 27.8 %collective-permute-start.52 = (bf16[256,1024]{1,0:T(8,128)(2,1)S(1)}, bf16[256,1024]{1,0:T(8,128)(2,1)S(1)}, u32[]{:S(2)}, u32[]{:S(2)}) collective-permute-start(bf16[256,1024]{1,0:T(8,128)(2,1)S(1)} %get-tuple-element.187), channel_id=1, source_target_pairs={{0,4},{4,8},{1,5},{5,9},{2,6},{6,10},{3,7},{7,11},{16,20},{20,24},... | collective-permute-start | bytes 1572872 | tf_op jit(solution)/shard_map/ppermute | solution.py:293
  394.4 26.5 %collective-permute-start.53 = (bf16[256,1024]{1,0:T(8,128)(2,1)S(1)}, bf16[256,1024]{1,0:T(8,128)(2,1)S(1)}, u32[]{:S(2)}, u32[]{:S(2)}) collective-permute-start(bf16[256,1024]{1,0:T(8,128)(2,1)S(1)} %get-tuple-element.188), channel_id=1, source_target_pairs={{12,8},{8,4},{13,9},{9,5},{14,10},{10,6},{15,11},{11,7},{28,24},{2... | collective-permute-start | bytes 1572872 | tf_op jit(solution)/shard_map/ppermute | solution.py:294
  405.3 43.1 %collective-permute-start.48 = (bf16[256,1024]{1,0:T(8,128)(2,1)S(1)}, bf16[256,1024]{1,0:T(8,128)(2,1)S(1)}, u32[]{:S(2)}, u32[]{:S(2)}) collective-permute-start(bf16[256,1024]{1,0:T(8,128)(2,1)S(1)} %get-tuple-element.183), channel_id=1, source_target_pairs={{0,4},{4,8},{8,12},{1,5},{5,9},{9,13},{2,6},{6,10},{10,14},{3,7},{... | collective-permute-start | bytes 1572872 | tf_op jit(solution)/shard_map/ppermute | solution.py:293
  423.4 26.3 %collective-permute-start.49 = (bf16[256,1024]{1,0:T(8,128)(2,1)S(1)}, bf16[256,1024]{1,0:T(8,128)(2,1)S(1)}, u32[]{:S(2)}, u32[]{:S(2)}) collective-permute-start(bf16[256,1024]{1,0:T(8,128)(2,1)S(1)} %get-tuple-element.184), channel_id=1, source_target_pairs={{12,8},{8,4},{4,0},{13,9},{9,5},{5,1},{14,10},{10,6},{6,2},{15,11}... | collective-permute-start | bytes 1572872 | tf_op jit(solution)/shard_map/ppermute | solution.py:294
  425.3 56.8 %collective-permute-start.54 = (bf16[256,1024]{1,0:T(8,128)(2,1)S(1)}, bf16[256,1024]{1,0:T(8,128)(2,1)S(1)}, u32[]{:S(2)}, u32[]{:S(2)}) collective-permute-start(bf16[256,1024]{1,0:T(8,128)(2,1)S(1)} %get-tuple-element.194), channel_id=1, source_target_pairs={{0,4},{4,8},{8,12},{1,5},{5,9},{9,13},{2,6},{6,10},{10,14},{3,7},{... | collective-permute-start | bytes 1572872 | tf_op jit(solution)/shard_map/ppermute | solution.py:293
  429.7 29.2 %collective-permute-start.58 = (bf16[256,1024]{1,0:T(8,128)(2,1)S(1)}, bf16[256,1024]{1,0:T(8,128)(2,1)S(1)}, u32[]{:S(2)}, u32[]{:S(2)}) collective-permute-start(bf16[256,1024]{1,0:T(8,128)(2,1)S(1)} %get-tuple-element.198), channel_id=1, source_target_pairs={{0,4},{4,8},{1,5},{5,9},{2,6},{6,10},{3,7},{7,11},{16,20},{20,24},... | collective-permute-start | bytes 1572872 | tf_op jit(solution)/shard_map/ppermute | solution.py:293
  438.4 30.2 %collective-permute-start.59 = (bf16[256,1024]{1,0:T(8,128)(2,1)S(1)}, bf16[256,1024]{1,0:T(8,128)(2,1)S(1)}, u32[]{:S(2)}, u32[]{:S(2)}) collective-permute-start(bf16[256,1024]{1,0:T(8,128)(2,1)S(1)} %get-tuple-element.199), channel_id=1, source_target_pairs={{12,8},{8,4},{13,9},{9,5},{14,10},{10,6},{15,11},{11,7},{28,24},{2... | collective-permute-start | bytes 1572872 | tf_op jit(solution)/shard_map/ppermute | solution.py:294
  449.7 30.1 %collective-permute-start.65 = (bf16[256,1024]{1,0:T(8,128)(2,1)S(1)}, bf16[256,1024]{1,0:T(8,128)(2,1)S(1)}, u32[]{:S(2)}, u32[]{:S(2)}) collective-permute-start(bf16[256,1024]{1,0:T(8,128)(2,1)S(1)} %get-tuple-element.209), channel_id=1, source_target_pairs={{12,8},{8,4},{13,9},{9,5},{14,10},{10,6},{15,11},{11,7},{28,24},{2... | collective-permute-start | bytes 1572872 | tf_op jit(solution)/shard_map/ppermute | solution.py:294
  458.9 27.2 %collective-permute-start.55 = (bf16[256,1024]{1,0:T(8,128)(2,1)S(1)}, bf16[256,1024]{1,0:T(8,128)(2,1)S(1)}, u32[]{:S(2)}, u32[]{:S(2)}) collective-permute-start(bf16[256,1024]{1,0:T(8,128)(2,1)S(1)} %get-tuple-element.195), channel_id=1, source_target_pairs={{12,8},{8,4},{4,0},{13,9},{9,5},{5,1},{14,10},{10,6},{6,2},{15,11}... | collective-permute-start | bytes 1572872 | tf_op jit(solution)/shard_map/ppermute | solution.py:294
  (91 other events, 1220.5 us)

commit v6 on v5

--- a/solution.py
+++ b/solution.py
@@ -261,7 +261,7 @@
         out_specs=pl.BlockSpec(memory_space=pltpu.VMEM),
         out_shape=jax.ShapeDtypeStruct((depth * n_rows, columns * len(parts)), BF16),
         scratch_shapes=[pltpu.SemaphoreType.DMA((len(blocks),))],
-        compiler_params=params(16),
+        compiler_params=params(),
         cost_estimate=cost(0, 4 * depth * n_rows * columns * len(parts)),
     )(*blocks)
 
@@ -321,48 +321,57 @@
     n_chunks = 2
     per = phys_pair // n_chunks
 
-    paired = jnp.einsum("wuxs,uvyt->wstxyv", mpo_left, mpo_right, precision=lax.Precision.HIGHEST)
-    mpo = paired.reshape(channels, phys_pair, phys_pair, channels).astype(BF16)
-    twice = jnp.einsum("wsxv,jk->sjwvkx", mpo, jnp.eye(2, dtype=BF16))
-    size = 2 * channels * phys_pair
-    mpo_back = twice.reshape(size, size)
-    mpo_fore = mpo_back.T
+    def environments(*deps):
+        own_left, own_right, far_env = after((mpo_left, mpo_right, right_env), *deps)
+        paired = jnp.einsum("wuxs,uvyt->wstxyv", own_left, own_right, precision=lax.Precision.HIGHEST)
+        mpo = paired.reshape(channels, phys_pair, phys_pair, channels).astype(BF16)
+        twice = jnp.einsum("wsxv,jk->sjwvkx", mpo, jnp.eye(2, dtype=BF16))
+        size = 2 * channels * phys_pair
+        mpo_back = twice.reshape(size, size)
+        return mpo_back.T, mpo_back, parted(far_env.transpose(1, 0, 2), lanes)
+
     left, left_t = ordered(left_env.transpose(1, 0, 2), tile)
-    right = parted(right_env.transpose(1, 0, 2), lanes)
+    if halves == 1:
+        mpo_fore, mpo_back, right = environments()
 
     theta_all, total, last_round = None, [None], [()] * n_chunks
     cuts = 2 if groups % 2 == 0 and n_rows > 2 else 1
     for h in range(halves):
         cut = theta[:, :, h * lanes : (h + 1) * lanes]
         pairs, blocks, fresh = [], [], []
+
+        def ahead(*deps):
+            return [
+                fore(
+                    after(theta_all, *deps, *fresh), left, mpo_fore, right[h - 1], total[0], channels,
+                    len(fresh), cuts, F32, tile,
+                )
+            ]
+
         for c in range(n_chunks):
             piece = cut[:, c * per : (c + 1) * per].reshape(rows, per * lanes)
             pairs.append(after((piece, piece), *last_round[c]))
             blocks.append([piece])
         for t in range(1, n_rows):
+            came = list(pairs)
             if (h, t) == (0, 2):
                 pairs[0] = after(pairs[0], left, left_t)
-            if (h, t) == (1, 1):
-                pairs[0] = after(pairs[0], mpo_fore, mpo_back, right)
-            if h > 0 and t > 1 and len(fresh) < cuts:
-                held = theta_all if t == 2 else after(theta_all, *sent)
-                fresh += [
-                    fore(held, left, mpo_fore, right[h - 1], total[0], channels, len(fresh), cuts,
-                         F32, tile)
-                ]
+            if (h, t) == (1, 2):
+                pairs = [after(pair, mpo_fore, mpo_back, right) for pair in pairs]
+            if h > 0 and t > 2 and len(fresh) < cuts:
+                fresh += ahead(*sent)
                 pairs = [after(pair, fresh[-1]) for pair in pairs]
-            sent = list(pairs)
+            sent = came
             for c in range(n_chunks):
                 pairs[c] = gather_round(pairs[c], t, n_rows)
                 blocks[c] = [pairs[c][0]] + blocks[c] + [pairs[c][1]]
         while h > 0 and len(fresh) < cuts:
-            fresh += [
-                fore(theta_all, left, mpo_fore, right[h - 1], total[0], channels, len(fresh), cuts,
-                     F32, tile)
-            ]
+            fresh += ahead(*sent)
         total = fresh or total
         last_round = pairs
-        theta_all = join(blocks, n_rows)
+        if h == 0 and halves > 1:
+            mpo_fore, mpo_back, right = environments(*pairs)
+        theta_all = join(after(blocks, *fresh), n_rows)
 
     def forward(g, *deps):
         here = g * len(total) // groups

time: 515 us -> 507 us (0.984)
  local copies, waits for them, and re-layouts: 47.5 us -> 21.1 us
  waiting for transfers between devices: 56.9 us -> 71 us
    unnamed x102 -> x82, local copies, waits for them, and re-layouts: 23.2 us -> 6.32 us
    ppermute x12, waiting for transfers between devices: 7.04 us -> 20.1 us  [gather_round(): lax.ppermute(pair[0], 'row', [(r, r + 1) for r in range(t - 1, n_rows - 1)])]
    ppermute x12, starting transfers between devices: 28.1 us -> 40.2 us  [gather_round(): lax.ppermute(pair[0], 'row', [(r, r + 1) for r in range(t - 1, n_rows - 1)])]
    ppermute x12, starting transfers between devices: 38.1 us -> 27.6 us  [gather_round(): lax.ppermute(pair[1], 'row', [(r, r - 1) for r in range(1, n_rows - t + 1)])]
    reshape x1, local copies, waits for them, and re-layouts: 7.42 us -> 1.6 us  [environments(): mpo_back = twice.reshape(size, size)]
    pallas_call x2, Pallas kernels: 3.31 us -> 8.97 us  [join(): pl.pallas_call(functools.partial(join_kernel, n_rows, len(parts)), in_spe...]
  transfers between devices with their start and end apart: 68 -> 68, of which waited for: 12 -> 14; matrix products, arithmetic and copies ran while one was open for 10% -> 8% of each run, Pallas kernels for 35% -> 37%
where the time goes in v6:
time: 507 us; the launch traced here: 497 us
  Pallas kernels  223 us (44%)
  starting transfers between devices  151 us (30%)
  waiting for transfers between devices  71 us (14%)
  other arithmetic  26.6 us (5%)
  local copies, waits for them, and re-layouts  21.1 us (4%)
    pallas_call x6, Pallas kernels, fore(): pl.pallas_call(functools.partial(fore_kernel, channels, lanes), grid=(ste...  91.7 us
    pallas_call x4, Pallas kernels, back(): pl.pallas_call(functools.partial(back_kernel, channels, len(parts), count...  57.8 us
    ppermute x12, starting transfers between devices, scatter_round(): lax.ppermute(pair[1], 'row', [(n_rows - 1 - r, n_rows - 2 - r) for r in r...  51.1 us
    pallas_call x4, Pallas kernels, last(): pl.pallas_call(last_kernel, grid=(steps,), in_specs=[pl.BlockSpec(left_t....  43 us
    ppermute x12, starting transfers between devices, gather_round(): lax.ppermute(pair[0], 'row', [(r, r + 1) for r in range(t - 1, n_rows - 1)])  40.2 us
    ppermute x12, starting transfers between devices, gather_round(): lax.ppermute(pair[1], 'row', [(r, r - 1) for r in range(1, n_rows - t + 1)])  27.6 us
    ppermute x12, waiting for transfers between devices, scatter_round(): lax.ppermute(pair[1], 'row', [(n_rows - 1 - r, n_rows - 2 - r) for r in r...  26.5 us
    ppermute x12, starting transfers between devices, scatter_round(): up = lax.ppermute(pair[0], 'row', [(r, r + 1) for r in range(t)])  21.9 us
  transfers between devices with their start and end apart: 68, of which 14 were waited for; matrix products, arithmetic and copies ran while one was open for 8% of the time, Pallas kernels for 37%

profile of v6, /device:TPU:16, one launch (start us, length us, event | category | flops | bytes accessed | tf_op | source)
XLA Modules:
  0.0 497.0 jit_solution(4356805532119435725)
XLA Ops:
  15.2 12.0 %shard_map.68 = (bf16[3072,1024]{1,0:T(8,128)(2,1)}, bf16[1024,3072]{1,0:T(8,128)(2,1)}) custom-call(bf16[12,256,1024]{2,1,0:T(8,128)(2,1)} %bitcast.40, bf16[384,384]{1,0:T(8,128)(2,1)} %fusion.9.order_ref), custom_call_target="tpu_custom_call" | custom-call | flops 301989888 | bytes 1179648 | tf_op jit(solution)/shard_map/pallas_call | solution.py:50
  94.6 9.9 %shard_map.69 = (bf16[1024,1536]{1,0:T(8,128)(2,1)}, bf16[1024,1536]{1,0:T(8,128)(2,1)}) custom-call(bf16[12,1024,256]{2,1,0:T(8,128)(2,1)} %bitcast.41), custom_call_target="tpu_custom_call" | custom-call | bytes 786432 | tf_op jit(solution)/shard_map/pallas_call | solution.py:79
  124.3 21.5 %shard_map.71.refs_0_ = f32[1024,2048]{1,0:T(8,128)} custom-call(bf16[1024,2048]{1,0:T(8,128)(2,1)} %shard_map.70.theta_ref, bf16[3072,1024]{1,0:T(8,128)(2,1)} %get-tuple-element.140.left_ref, bf16[384,384]{1,0:T(8,128)(2,1)S(1)} %copy.25.mpo_ref, bf16[1024,1536]{1,0:T(8,128)(2,1)S(1)} %copy-done.3), custom_call_target="tpu_custom_call" | custom-call | flops 956301312 | bytes 1179648 | tf_op jit(solution)/shard_map/pallas_call | solution.py:123
  152.9 21.5 %shard_map.72.refs_0_ = f32[1024,2048]{1,0:T(8,128)} custom-call(bf16[1024,2048]{1,0:T(8,128)(2,1)} %shard_map.70.theta_ref, bf16[3072,1024]{1,0:T(8,128)(2,1)} %get-tuple-element.140.left_ref, bf16[384,384]{1,0:T(8,128)(2,1)S(1)} %copy.25.mpo_ref, bf16[1024,1536]{1,0:T(8,128)(2,1)S(1)} %copy-done.3), custom_call_target="tpu_custom_call" | custom-call | flops 956301312 | bytes 1179648 | tf_op jit(solution)/shard_map/pallas_call | solution.py:123
  179.0 12.1 %shard_map.74 = bf16[1024,1024]{1,0:T(8,128)(2,1)S(1)} custom-call(bf16[1024,2048]{1,0:T(8,128)(2,1)} %shard_map.73.theta_ref, bf16[3072,1024]{1,0:T(8,128)(2,1)} %get-tuple-element.140.left_ref, bf16[384,384]{1,0:T(8,128)(2,1)S(1)} %copy.25.mpo_ref, bf16[1024,1536]{1,0:T(8,128)(2,1)S(1)} %copy-done.2, f32[1024,2048]{1,0:T(8,128)} %shard_map.71.refs_0_), custom_call_target="tpu_custom_call" | custom-call | flops 478150656 | bytes 819200 | tf_op jit(solution)/shard_map/pallas_call | solution.py:123
  192.8 12.1 %shard_map.75 = bf16[1024,1024]{1,0:T(8,128)(2,1)S(1)} custom-call(bf16[1024,2048]{1,0:T(8,128)(2,1)} %shard_map.73.theta_ref, bf16[3072,1024]{1,0:T(8,128)(2,1)} %get-tuple-element.140.left_ref, bf16[384,384]{1,0:T(8,128)(2,1)S(1)} %copy.25.mpo_ref, bf16[1024,1536]{1,0:T(8,128)(2,1)S(1)} %copy-done.2, f32[1024,2048]{1,0:T(8,128)} %shard_map.71.refs_0_), custom_call_target="tpu_custom_call" | custom-call | flops 478150656 | bytes 819200 | tf_op jit(solution)/shard_map/pallas_call | solution.py:123
  212.3 12.5 %shard_map.76 = bf16[1024,1024]{1,0:T(8,128)(2,1)S(1)} custom-call(bf16[1024,2048]{1,0:T(8,128)(2,1)} %shard_map.73.theta_ref, bf16[3072,1024]{1,0:T(8,128)(2,1)} %get-tuple-element.140.left_ref, bf16[384,384]{1,0:T(8,128)(2,1)S(1)} %copy.25.mpo_ref, bf16[1024,1536]{1,0:T(8,128)(2,1)S(1)} %copy-done.2, f32[1024,2048]{1,0:T(8,128)} %shard_map.72.refs_0_), custom_call_target="tpu_custom_call" | custom-call | flops 478150656 | bytes 819200 | tf_op jit(solution)/shard_map/pallas_call | solution.py:123
  233.8 12.1 %shard_map.77 = bf16[1024,1024]{1,0:T(8,128)(2,1)S(1)} custom-call(bf16[1024,2048]{1,0:T(8,128)(2,1)} %shard_map.73.theta_ref, bf16[3072,1024]{1,0:T(8,128)(2,1)} %get-tuple-element.140.left_ref, bf16[384,384]{1,0:T(8,128)(2,1)S(1)} %copy.25.mpo_ref, bf16[1024,1536]{1,0:T(8,128)(2,1)S(1)} %copy-done.2, f32[1024,2048]{1,0:T(8,128)} %shard_map.72.refs_0_), custom_call_target="tpu_custom_call" | custom-call | flops 478150656 | bytes 819200 | tf_op jit(solution)/shard_map/pallas_call | solution.py:123
  248.3 8.3 %collective-permute-done.31.refs_1_ = bf16[256,1024]{1,0:T(8,128)(2,1)S(1)} collective-permute-done((bf16[256,1024]{1,0:T(8,128)(2,1)S(1)}, bf16[256,1024]{1,0:T(8,128)(2,1)S(1)}, u32[]{:S(2)}, u32[]{:S(2)}) %collective-permute-start.31) | collective-permute-done | bytes 524320 | tf_op jit(solution)/shard_map/ppermute | solution.py:309
  259.1 14.4 %shard_map.78 = (bf16[3072,2048]{1,0:T(8,128)(2,1)}, bf16[3072,2048]{1,0:T(8,128)(2,1)}) custom-call(bf16[256,1024]{1,0:T(8,128)(2,1)S(1)} %add_convert_fusion.19.refs_0_, bf16[256,1024]{1,0:T(8,128)(2,1)S(1)} %collective-permute-done.31.refs_1_, bf16[256,1024]{1,0:T(8,128)(2,1)S(1)} %collective-permute-done.32.refs_2_, ...), custom_call_target="tpu_custom_call" | custom-call | flops 553648128 | bytes 917504 | tf_op jit(solution)/shard_map/pallas_call | solution.py:188
  280.6 14.3 %shard_map.79 = (bf16[3072,2048]{1,0:T(8,128)(2,1)}, bf16[3072,2048]{1,0:T(8,128)(2,1)}) custom-call(bf16[256,1024]{1,0:T(8,128)(2,1)S(1)} %add_convert_fusion.18.refs_0_, bf16[256,1024]{1,0:T(8,128)(2,1)S(1)} %collective-permute-done.35.refs_1_, ...), custom_call_target="tpu_custom_call", output_to_operand_aliasing={{0}: (7, {}), {1}: (8, {})} | custom-call | flops 553648128 | bytes 917504 | tf_op jit(solution)/shard_map/pallas_call | solution.py:188
  295.4 7.0 %collective-permute-done.34 = bf16[256,1024]{1,0:T(8,128)(2,1)S(1)} collective-permute-done((bf16[256,1024]{1,0:T(8,128)(2,1)S(1)}, bf16[256,1024]{1,0:T(8,128)(2,1)S(1)}, u32[]{:S(2)}, u32[]{:S(2)}) %collective-permute-start.34) | collective-permute-done | bytes 524320 | tf_op jit(solution)/shard_map/ppermute | solution.py:309
  303.9 14.5 %shard_map.80 = (bf16[3072,2048]{1,0:T(8,128)(2,1)}, bf16[3072,2048]{1,0:T(8,128)(2,1)}) custom-call(bf16[256,1024]{1,0:T(8,128)(2,1)S(1)} %add_convert_fusion.17.refs_0_, bf16[256,1024]{1,0:T(8,128)(2,1)S(1)} %collective-permute-done.39.refs_1_, ...), custom_call_target="tpu_custom_call", output_to_operand_aliasing={{0}: (7, {}), {1}: (8, {})} | custom-call | flops 553648128 | bytes 917504 | tf_op jit(solution)/shard_map/pallas_call | solution.py:188
  320.8 14.6 %shard_map.81 = (bf16[3072,2048]{1,0:T(8,128)(2,1)}, bf16[3072,2048]{1,0:T(8,128)(2,1)}) custom-call(bf16[256,1024]{1,0:T(8,128)(2,1)} %add_convert_fusion.16.refs_0_, bf16[256,1024]{1,0:T(8,128)(2,1)} %collective-permute-done.38.refs_1_, bf16[256,1024]{1,0:T(8,128)(2,1)} %collective-permute-done.42.refs_2_, ...), custom_call_target="tpu_custom_call", output_to_operand_aliasing={{0}: (7, {}), {1}: (8, {})} | custom-call | flops 553648128 | bytes 917504 | tf_op jit(solution)/shard_map/pallas_call | solution.py:188
  335.4 10.7 %shard_map.82 = bf16[1024,1024]{1,0:T(8,128)(2,1)S(1)} custom-call(bf16[1024,3072]{1,0:T(8,128)(2,1)} %get-tuple-element.141.left_ref, bf16[3072,2048]{1,0:T(8,128)(2,1)} %get-tuple-element.232.back_ref), custom_call_target="tpu_custom_call" | custom-call | flops 402653184 | bytes 917504 | tf_op jit(solution)/shard_map/pallas_call | solution.py:221
  350.1 10.8 %shard_map.83 = bf16[1024,1024]{1,0:T(8,128)(2,1)S(1)} custom-call(bf16[1024,3072]{1,0:T(8,128)(2,1)} %get-tuple-element.141.left_ref, bf16[3072,2048]{1,0:T(8,128)(2,1)} %get-tuple-element.232.back_ref), custom_call_target="tpu_custom_call" | custom-call | flops 402653184 | bytes 917504 | tf_op jit(solution)/shard_map/pallas_call | solution.py:221
  372.8 10.7 %shard_map.84 = bf16[1024,1024]{1,0:T(8,128)(2,1)S(1)} custom-call(bf16[1024,3072]{1,0:T(8,128)(2,1)} %get-tuple-element.141.left_ref, bf16[3072,2048]{1,0:T(8,128)(2,1)} %get-tuple-element.251.back_ref), custom_call_target="tpu_custom_call" | custom-call | flops 402653184 | bytes 917504 | tf_op jit(solution)/shard_map/pallas_call | solution.py:221
  402.0 10.8 %shard_map.85 = bf16[1024,1024]{1,0:T(8,128)(2,1)S(1)} custom-call(bf16[1024,3072]{1,0:T(8,128)(2,1)} %get-tuple-element.141.left_ref, bf16[3072,2048]{1,0:T(8,128)(2,1)} %get-tuple-element.251.back_ref), custom_call_target="tpu_custom_call" | custom-call | flops 402653184 | bytes 917504 | tf_op jit(solution)/shard_map/pallas_call | solution.py:221
  422.9 7.5 %collective-permute-done.63 = bf16[256,1024]{1,0:T(8,128)(2,1)S(1)} collective-permute-done((bf16[256,1024]{1,0:T(8,128)(2,1)S(1)}, bf16[256,1024]{1,0:T(8,128)(2,1)S(1)}, u32[]{:S(2)}, u32[]{:S(2)}) %collective-permute-start.63) | collective-permute-done | bytes 524320 | tf_op jit(solution)/shard_map/ppermute | solution.py:294
  430.3 8.6 %collective-permute-start.59 = (bf16[256,1024]{1,0:T(8,128)(2,1)S(1)}, bf16[256,1024]{1,0:T(8,128)(2,1)S(1)}, u32[]{:S(2)}, u32[]{:S(2)}) collective-permute-start(bf16[256,1024]{1,0:T(8,128)(2,1)S(1)} %get-tuple-element.259), channel_id=1, source_target_pairs={{12,8},{8,4},{13,9},{9,5},{14,10},{10,6},{15,11},{11,7},{28,24},{2... | collective-permute-start | bytes 1572872 | tf_op jit(solution)/shard_map/ppermute | solution.py:294
  449.8 9.6 %collective-permute-start.55 = (bf16[256,1024]{1,0:T(8,128)(2,1)S(1)}, bf16[256,1024]{1,0:T(8,128)(2,1)S(1)}, u32[]{:S(2)}, u32[]{:S(2)}) collective-permute-start(bf16[256,1024]{1,0:T(8,128)(2,1)S(1)} %get-tuple-element.255), channel_id=1, source_target_pairs={{12,8},{8,4},{4,0},{13,9},{9,5},{5,1},{14,10},{10,6},{6,2},{15,11}... | collective-permute-start | bytes 1572872 | tf_op jit(solution)/shard_map/ppermute | solution.py:294
  461.8 8.9 %collective-permute-start.61 = (bf16[256,1024]{1,0:T(8,128)(2,1)S(1)}, bf16[256,1024]{1,0:T(8,128)(2,1)S(1)}, u32[]{:S(2)}, u32[]{:S(2)}) collective-permute-start(bf16[256,1024]{1,0:T(8,128)(2,1)S(1)} %get-tuple-element.263), channel_id=1, source_target_pairs={{12,8},{8,4},{4,0},{13,9},{9,5},{5,1},{14,10},{10,6},{6,2},{15,11}... | collective-permute-start | bytes 1572872 | tf_op jit(solution)/shard_map/ppermute | solution.py:294
  477.4 9.1 %collective-permute-done.61 = bf16[256,1024]{1,0:T(8,128)(2,1)S(1)} collective-permute-done((bf16[256,1024]{1,0:T(8,128)(2,1)S(1)}, bf16[256,1024]{1,0:T(8,128)(2,1)S(1)}, u32[]{:S(2)}, u32[]{:S(2)}) %collective-permute-start.61) | collective-permute-done | bytes 524320 | tf_op jit(solution)/shard_map/ppermute | solution.py:294
  486.9 7.7 %collective-permute-done.67 = bf16[256,1024]{1,0:T(8,128)(2,1)S(1)} collective-permute-done((bf16[256,1024]{1,0:T(8,128)(2,1)S(1)}, bf16[256,1024]{1,0:T(8,128)(2,1)S(1)}, u32[]{:S(2)}, u32[]{:S(2)}) %collective-permute-start.67) | collective-permute-done | bytes 524320 | tf_op jit(solution)/shard_map/ppermute | solution.py:294
  (256 shorter events, 213.5 us)
Async XLA Ops:
  65.7 46.2 %collective-permute-start.6 = (bf16[256,1024]{1,0:T(8,128)(2,1)}, bf16[256,1024]{1,0:T(8,128)(2,1)}, u32[]{:S(2)}, u32[]{:S(2)}) collective-permute-start(bf16[256,1024]{1,0:T(8,128)(2,1)} %bitcast.37.refs_3_), channel_id=1, source_target_pairs={{0,4},{4,8},{8,12},{1,5},{5,9},{9,13},{2,6},{6,10},{10,14},{3,7},{... | collective-permute-start | bytes 1572872 | tf_op jit(solution)/shard_map/ppermute | solution.py:274
  70.1 41.8 %collective-permute-start.7 = (bf16[256,1024]{1,0:T(8,128)(2,1)}, bf16[256,1024]{1,0:T(8,128)(2,1)}, u32[]{:S(2)}, u32[]{:S(2)}) collective-permute-start(bf16[256,1024]{1,0:T(8,128)(2,1)} %bitcast.37.refs_3_), channel_id=1, source_target_pairs={{4,0},{8,4},{12,8},{5,1},{9,5},{13,9},{6,2},{10,6},{14,10},{7,3},{... | collective-permute-start | bytes 1572872 | tf_op jit(solution)/shard_map/ppermute | solution.py:275
  77.0 27.5 %collective-permute-start.16 = (bf16[256,1024]{1,0:T(8,128)(2,1)}, bf16[256,1024]{1,0:T(8,128)(2,1)}, u32[]{:S(2)}, u32[]{:S(2)}) collective-permute-start(bf16[256,1024]{1,0:T(8,128)(2,1)} %bitcast.34.refs_10_), channel_id=1, source_target_pairs={{0,4},{4,8},{8,12},{1,5},{5,9},{9,13},{2,6},{6,10},{10,14},{3,7},{... | collective-permute-start | bytes 1572872 | tf_op jit(solution)/shard_map/ppermute | solution.py:274
  104.5 41.3 %collective-permute-start.20 = (bf16[256,1024]{1,0:T(8,128)(2,1)}, bf16[256,1024]{1,0:T(8,128)(2,1)}, u32[]{:S(2)}, u32[]{:S(2)}) collective-permute-start(bf16[256,1024]{1,0:T(8,128)(2,1)} %collective-permute-done.16.refs_9_), channel_id=1, source_target_pairs={{4,8},{8,12},{5,9},{9,13},{6,10},{10,14},{7,11},{11,15},{20,24},{2... | collective-permute-start | bytes 1572872 | tf_op jit(solution)/shard_map/ppermute | solution.py:274
  109.2 36.6 %collective-permute-start.21 = (bf16[256,1024]{1,0:T(8,128)(2,1)}, bf16[256,1024]{1,0:T(8,128)(2,1)}, u32[]{:S(2)}, u32[]{:S(2)}) collective-permute-start(bf16[256,1024]{1,0:T(8,128)(2,1)} %collective-permute-done.17.refs_11_), channel_id=1, source_target_pairs={{4,0},{8,4},{5,1},{9,5},{6,2},{10,6},{7,3},{11,7},{20,16},{24,20},... | collective-permute-start | bytes 1572872 | tf_op jit(solution)/shard_map/ppermute | solution.py:275
  112.0 37.4 %collective-permute-start.14 = (bf16[256,1024]{1,0:T(8,128)(2,1)}, bf16[256,1024]{1,0:T(8,128)(2,1)}, u32[]{:S(2)}, u32[]{:S(2)}) collective-permute-start(bf16[256,1024]{1,0:T(8,128)(2,1)} %collective-permute-done.6.refs_2_), channel_id=1, source_target_pairs={{4,8},{8,12},{5,9},{9,13},{6,10},{10,14},{7,11},{11,15},{20,24},{2... | collective-permute-start | bytes 1572872 | tf_op jit(solution)/shard_map/ppermute | solution.py:274
  113.9 35.5 %collective-permute-start.15 = (bf16[256,1024]{1,0:T(8,128)(2,1)}, bf16[256,1024]{1,0:T(8,128)(2,1)}, u32[]{:S(2)}, u32[]{:S(2)}) collective-permute-start(bf16[256,1024]{1,0:T(8,128)(2,1)} %collective-permute-done.7.refs_4_), channel_id=1, source_target_pairs={{4,0},{8,4},{5,1},{9,5},{6,2},{10,6},{7,3},{11,7},{20,16},{24,20},... | collective-permute-start | bytes 1572872 | tf_op jit(solution)/shard_map/ppermute | solution.py:275
  145.8 28.7 %collective-permute-start.22 = (bf16[256,1024]{1,0:T(8,128)(2,1)}, bf16[256,1024]{1,0:T(8,128)(2,1)}, u32[]{:S(2)}, u32[]{:S(2)}) collective-permute-start(bf16[256,1024]{1,0:T(8,128)(2,1)} %collective-permute-done.20.refs_8_), channel_id=1, source_target_pairs={{8,12},{9,13},{10,14},{11,15},{24,28},{25,29},{26,30},{27,31}} | collective-permute-start | bytes 1572872 | tf_op jit(solution)/shard_map/ppermute | solution.py:274
  147.9 26.6 %collective-permute-start.23 = (bf16[256,1024]{1,0:T(8,128)(2,1)}, bf16[256,1024]{1,0:T(8,128)(2,1)}, u32[]{:S(2)}, u32[]{:S(2)}) collective-permute-start(bf16[256,1024]{1,0:T(8,128)(2,1)} %collective-permute-done.21.refs_12_), channel_id=1, source_target_pairs={{4,0},{5,1},{6,2},{7,3},{20,16},{21,17},{22,18},{23,19}} | collective-permute-start | bytes 1572872 | tf_op jit(solution)/shard_map/ppermute | solution.py:275
  149.4 25.1 %collective-permute-start.18 = (bf16[256,1024]{1,0:T(8,128)(2,1)}, bf16[256,1024]{1,0:T(8,128)(2,1)}, u32[]{:S(2)}, u32[]{:S(2)}) collective-permute-start(bf16[256,1024]{1,0:T(8,128)(2,1)} %collective-permute-done.14.refs_1_), channel_id=1, source_target_pairs={{8,12},{9,13},{10,14},{11,15},{24,28},{25,29},{26,30},{27,31}} | collective-permute-start | bytes 1572872 | tf_op jit(solution)/shard_map/ppermute | solution.py:274
  225.9 30.6 %collective-permute-start.28 = (bf16[512,1024]{1,0:T(8,128)(2,1)}, bf16[512,1024]{1,0:T(8,128)(2,1)}, u32[]{:S(2)}, u32[]{:S(2)}) collective-permute-start(bf16[512,1024]{1,0:T(8,128)(2,1)} %constant_dynamic-slice_fusion.11), channel_id=1, source_target_pairs={{0,2},{2,0},{1,3},{3,1},{4,6},{6,4},{5,7},{7,5},{8,10},{10,8},{9,1... | collective-permute-start | bytes 3145736 | tf_op jit(solution)/shard_map/ppermute | solution.py:309
  247.3 26.2 %collective-permute-start.35 = (bf16[256,1024]{1,0:T(8,128)(2,1)S(1)}, bf16[256,1024]{1,0:T(8,128)(2,1)S(1)}, u32[]{:S(2)}, u32[]{:S(2)}) collective-permute-start(bf16[256,1024]{1,0:T(8,128)(2,1)S(1)} %add_convert_fusion.18.refs_0_), channel_id=1, source_target_pairs={{0,1},{1,0},{2,3},{3,2},{4,5},{5,4},{6,7},{7,6},{8,9},{9,8},{10,11... | collective-permute-start | bytes 1572872 | tf_op jit(solution)/shard_map/ppermute | solution.py:309
  248.0 30.0 %collective-permute-start.30 = (bf16[512,1024]{1,0:T(8,128)(2,1)S(1)}, bf16[512,1024]{1,0:T(8,128)(2,1)S(1)}, u32[]{:S(2)}, u32[]{:S(2)}) collective-permute-start(bf16[512,1024]{1,0:T(8,128)(2,1)S(1)} %constant_dynamic-slice_fusion.9), channel_id=1, source_target_pairs={{0,2},{2,0},{1,3},{3,1},{4,6},{6,4},{5,7},{7,5},{8,10},{10,8},{9,1... | collective-permute-start | bytes 3145736 | tf_op jit(solution)/shard_map/ppermute | solution.py:309
  367.0 27.5 %collective-permute-start.46 = (bf16[256,1024]{1,0:T(8,128)(2,1)S(1)}, bf16[256,1024]{1,0:T(8,128)(2,1)S(1)}, u32[]{:S(2)}, u32[]{:S(2)}) collective-permute-start(bf16[256,1024]{1,0:T(8,128)(2,1)S(1)} %get-tuple-element.235), channel_id=1, source_target_pairs={{0,4},{4,8},{1,5},{5,9},{2,6},{6,10},{3,7},{7,11},{16,20},{20,24},... | collective-permute-start | bytes 1572872 | tf_op jit(solution)/shard_map/ppermute | solution.py:293
  368.3 27.5 %collective-permute-start.47 = (bf16[256,1024]{1,0:T(8,128)(2,1)S(1)}, bf16[256,1024]{1,0:T(8,128)(2,1)S(1)}, u32[]{:S(2)}, u32[]{:S(2)}) collective-permute-start(bf16[256,1024]{1,0:T(8,128)(2,1)S(1)} %get-tuple-element.236), channel_id=1, source_target_pairs={{12,8},{8,4},{13,9},{9,5},{14,10},{10,6},{15,11},{11,7},{28,24},{2... | collective-permute-start | bytes 1572872 | tf_op jit(solution)/shard_map/ppermute | solution.py:294
  385.3 27.5 %collective-permute-start.52 = (bf16[256,1024]{1,0:T(8,128)(2,1)S(1)}, bf16[256,1024]{1,0:T(8,128)(2,1)S(1)}, u32[]{:S(2)}, u32[]{:S(2)}) collective-permute-start(bf16[256,1024]{1,0:T(8,128)(2,1)S(1)} %get-tuple-element.247), channel_id=1, source_target_pairs={{0,4},{4,8},{1,5},{5,9},{2,6},{6,10},{3,7},{7,11},{16,20},{20,24},... | collective-permute-start | bytes 1572872 | tf_op jit(solution)/shard_map/ppermute | solution.py:293
  386.6 26.2 %collective-permute-start.53 = (bf16[256,1024]{1,0:T(8,128)(2,1)S(1)}, bf16[256,1024]{1,0:T(8,128)(2,1)S(1)}, u32[]{:S(2)}, u32[]{:S(2)}) collective-permute-start(bf16[256,1024]{1,0:T(8,128)(2,1)S(1)} %get-tuple-element.248), channel_id=1, source_target_pairs={{12,8},{8,4},{13,9},{9,5},{14,10},{10,6},{15,11},{11,7},{28,24},{2... | collective-permute-start | bytes 1572872 | tf_op jit(solution)/shard_map/ppermute | solution.py:294
  397.4 41.9 %collective-permute-start.48 = (bf16[256,1024]{1,0:T(8,128)(2,1)S(1)}, bf16[256,1024]{1,0:T(8,128)(2,1)S(1)}, u32[]{:S(2)}, u32[]{:S(2)}) collective-permute-start(bf16[256,1024]{1,0:T(8,128)(2,1)S(1)} %get-tuple-element.243), channel_id=1, source_target_pairs={{0,4},{4,8},{8,12},{1,5},{5,9},{9,13},{2,6},{6,10},{10,14},{3,7},{... | collective-permute-start | bytes 1572872 | tf_op jit(solution)/shard_map/ppermute | solution.py:293
  415.3 26.3 %collective-permute-start.49 = (bf16[256,1024]{1,0:T(8,128)(2,1)S(1)}, bf16[256,1024]{1,0:T(8,128)(2,1)S(1)}, u32[]{:S(2)}, u32[]{:S(2)}) collective-permute-start(bf16[256,1024]{1,0:T(8,128)(2,1)S(1)} %get-tuple-element.244), channel_id=1, source_target_pairs={{12,8},{8,4},{4,0},{13,9},{9,5},{5,1},{14,10},{10,6},{6,2},{15,11}... | collective-permute-start | bytes 1572872 | tf_op jit(solution)/shard_map/ppermute | solution.py:294
  417.2 55.8 %collective-permute-start.54 = (bf16[256,1024]{1,0:T(8,128)(2,1)S(1)}, bf16[256,1024]{1,0:T(8,128)(2,1)S(1)}, u32[]{:S(2)}, u32[]{:S(2)}) collective-permute-start(bf16[256,1024]{1,0:T(8,128)(2,1)S(1)} %get-tuple-element.254), channel_id=1, source_target_pairs={{0,4},{4,8},{8,12},{1,5},{5,9},{9,13},{2,6},{6,10},{10,14},{3,7},{... | collective-permute-start | bytes 1572872 | tf_op jit(solution)/shard_map/ppermute | solution.py:293
  421.6 28.3 %collective-permute-start.58 = (bf16[256,1024]{1,0:T(8,128)(2,1)S(1)}, bf16[256,1024]{1,0:T(8,128)(2,1)S(1)}, u32[]{:S(2)}, u32[]{:S(2)}) collective-permute-start(bf16[256,1024]{1,0:T(8,128)(2,1)S(1)} %get-tuple-element.258), channel_id=1, source_target_pairs={{0,4},{4,8},{1,5},{5,9},{2,6},{6,10},{3,7},{7,11},{16,20},{20,24},... | collective-permute-start | bytes 1572872 | tf_op jit(solution)/shard_map/ppermute | solution.py:293
  430.3 29.2 %collective-permute-start.59 = (bf16[256,1024]{1,0:T(8,128)(2,1)S(1)}, bf16[256,1024]{1,0:T(8,128)(2,1)S(1)}, u32[]{:S(2)}, u32[]{:S(2)}) collective-permute-start(bf16[256,1024]{1,0:T(8,128)(2,1)S(1)} %get-tuple-element.259), channel_id=1, source_target_pairs={{12,8},{8,4},{13,9},{9,5},{14,10},{10,6},{15,11},{11,7},{28,24},{2... | collective-permute-start | bytes 1572872 | tf_op jit(solution)/shard_map/ppermute | solution.py:294
  441.6 29.2 %collective-permute-start.65 = (bf16[256,1024]{1,0:T(8,128)(2,1)S(1)}, bf16[256,1024]{1,0:T(8,128)(2,1)S(1)}, u32[]{:S(2)}, u32[]{:S(2)}) collective-permute-start(bf16[256,1024]{1,0:T(8,128)(2,1)S(1)} %get-tuple-element.269), channel_id=1, source_target_pairs={{12,8},{8,4},{13,9},{9,5},{14,10},{10,6},{15,11},{11,7},{28,24},{2... | collective-permute-start | bytes 1572872 | tf_op jit(solution)/shard_map/ppermute | solution.py:294
  449.8 27.2 %collective-permute-start.55 = (bf16[256,1024]{1,0:T(8,128)(2,1)S(1)}, bf16[256,1024]{1,0:T(8,128)(2,1)S(1)}, u32[]{:S(2)}, u32[]{:S(2)}) collective-permute-start(bf16[256,1024]{1,0:T(8,128)(2,1)S(1)} %get-tuple-element.255), channel_id=1, source_target_pairs={{12,8},{8,4},{4,0},{13,9},{9,5},{5,1},{14,10},{10,6},{6,2},{15,11}... | collective-permute-start | bytes 1572872 | tf_op jit(solution)/shard_map/ppermute | solution.py:294
  (81 other events, 1608.7 us)

commit v7 on v6

--- a/solution.py
+++ b/solution.py
@@ -67,17 +67,22 @@
     )(env, order)
 
 
-def part_kernel(env_ref, *outs):
-    lanes = outs[0].shape[1]
-    for h, out in enumerate(outs):
-        out[...] = env_ref[0, :, h * lanes : (h + 1) * lanes]
-
-
-def parted(env, lanes):
+def part_kernel(scattered, env_ref, *outs):
+    far, lanes = outs[0].shape
+    count = lax.axis_size("col") * lax.axis_size("chan") if scattered else 1
+    height = far // count
+    for k in range(count):
+        place = block_of(k) if scattered else k
+        rows = pl.ds(pl.multiple_of(place * height, height), height)
+        for h, out in enumerate(outs):
+            out[k * height : (k + 1) * height] = env_ref[0, rows, h * lanes : (h + 1) * lanes]
+
+
+def parted(env, lanes, scattered):
     channels, far, width = env.shape
     count = width // lanes
     return pl.pallas_call(
-        part_kernel,
+        functools.partial(part_kernel, scattered),
         grid=(channels,),
         in_specs=[pl.BlockSpec((1, far, width), lambda v: (v, 0, 0))],
         out_specs=[pl.BlockSpec((far, lanes), lambda v: (0, v))] * count,
@@ -87,8 +92,8 @@
     )(env)
 
 
-def fore_kernel(channels, lanes, theta_ref, left_ref, mpo_ref, right_ref, *refs):
-    out, ones, threes = refs[-3:]
+def fore_kernel(channels, lanes, n_outs, theta_ref, left_ref, mpo_ref, right_ref, *refs):
+    outs, ones, threes = refs[-2 - n_outs : -2], refs[-2], refs[-1]
     phys_pair = theta_ref.shape[1] // lanes
     pair, step = 2 * channels, 2 * phys_pair
     pairs = left_ref.shape[0] // pair
@@ -108,12 +113,14 @@
                 v * step : (v + 1) * step, i * lanes : (i + 1) * lanes
             ]
     part = dot(right_ref[...], threes[...], ROWS)
-    if len(refs) == 4:
+    if len(refs) > 2 + n_outs:
         part = part + refs[0][...]
-    out[...] = part.astype(out.dtype)
-
-
-def fore(theta, left, mpo, right, total, channels, group, groups, kind, tile, place=0):
+    height = outs[0].shape[0]
+    for k, out in enumerate(outs):
+        out[...] = part[k * height : (k + 1) * height].astype(out.dtype)
+
+
+def fore(theta, left, mpo, right, total, channels, group, groups, kind, tile, place=0, n_outs=1):
     far = right.shape[0]
     lanes = right.shape[1] // channels
     phys_pair = theta.shape[1] // lanes
@@ -121,7 +128,7 @@
     steps = bonds // tile
     totals = [] if total is None else [total]
     return pl.pallas_call(
-        functools.partial(fore_kernel, channels, lanes),
+        functools.partial(fore_kernel, channels, lanes, n_outs),
         grid=(steps,),
         in_specs=[
             pl.BlockSpec(theta.shape, lambda i: (0, 0), pipeline_mode=ONCE),
@@ -130,8 +137,8 @@
             pl.BlockSpec(right.shape, lambda i: (0, 0), pipeline_mode=ONCE),
         ]
         + [pl.BlockSpec((far, tile * phys_pair), lambda i: (0, place * steps + i))] * len(totals),
-        out_specs=pl.BlockSpec((far, tile * phys_pair), lambda i: (0, i)),
-        out_shape=jax.ShapeDtypeStruct((far, bonds * phys_pair), kind),
+        out_specs=[pl.BlockSpec((far // n_outs, tile * phys_pair), lambda i: (0, i))] * n_outs,
+        out_shape=[jax.ShapeDtypeStruct((far // n_outs, bonds * phys_pair), kind)] * n_outs,
         scratch_shapes=[
             pltpu.VMEM((2 * channels * phys_pair, tile // 2 * lanes), BF16),
             pltpu.VMEM((tile * phys_pair, channels * lanes), BF16),
@@ -146,7 +153,7 @@
     )(theta, left, mpo, right, *totals)
 
 
-def back_kernel(channels, n_parts, n_halves, scattered, *refs):
+def back_kernel(channels, n_parts, n_halves, *refs):
     parts = refs[:n_parts]
     mpo_ref, rights = refs[n_parts], refs[n_parts + 1 : n_parts + 1 + n_halves]
     outs, joined, ones = refs[-2 - n_halves : -2], refs[-2], refs[-1]
@@ -156,8 +163,7 @@
     pairs = outs[0].shape[0] // pair
     height = parts[0].shape[0]
     for k, part in enumerate(parts):
-        place = block_of(k) if scattered else k
-        joined[pl.ds(pl.multiple_of(place * height, height), height), :] = part[...]
+        joined[k * height : (k + 1) * height] = part[...]
     for right_ref, out_ref in zip(rights, outs):
         full = dot(joined[...], right_ref[...], COLS).astype(BF16)
         for i in range(pairs):
@@ -177,7 +183,7 @@
                 ).astype(BF16)
 
 
-def back(parts, mpo, rights, buffers, channels, phys_pair, group, groups, scattered, tile):
+def back(parts, mpo, rights, buffers, channels, phys_pair, group, groups, tile):
     columns = parts[0].shape[1]
     bonds = columns // phys_pair
     far, width = rights[0].shape
@@ -186,7 +192,7 @@
     count = len(rights)
     before = len(parts) + 1 + count
     return pl.pallas_call(
-        functools.partial(back_kernel, channels, len(parts), count, scattered),
+        functools.partial(back_kernel, channels, len(parts), count),
         grid=(steps,),
         input_output_aliases={before + k: k for k in range(len(buffers))},
         in_specs=[pl.BlockSpec((p.shape[0], tile * phys_pair), lambda i: (0, i)) for p in parts]
@@ -299,12 +305,6 @@
     return (x.astype(F32) + y.astype(F32)).astype(BF16)
 
 
-def halved(term, axis):
-    height = term.shape[0] // 2
-    index = lax.axis_index(axis)
-    return [lax.dynamic_slice_in_dim(term, k * height, height) for k in (index, 1 - index)]
-
-
 def swapped(block, axis):
     return lax.ppermute(block, axis, [(0, 1), (1, 0)])
 
@@ -321,18 +321,22 @@
     n_chunks = 2
     per = phys_pair // n_chunks
 
-    def environments(*deps):
-        own_left, own_right, far_env = after((mpo_left, mpo_right, right_env), *deps)
-        paired = jnp.einsum("wuxs,uvyt->wstxyv", own_left, own_right, precision=lax.Precision.HIGHEST)
+    def mpo_pairs(*deps):
+        one, two = after((mpo_left, mpo_right), *deps)
+        paired = jnp.einsum("wuxs,uvyt->wstxyv", one, two, precision=lax.Precision.HIGHEST)
         mpo = paired.reshape(channels, phys_pair, phys_pair, channels).astype(BF16)
         twice = jnp.einsum("wsxv,jk->sjwvkx", mpo, jnp.eye(2, dtype=BF16))
         size = 2 * channels * phys_pair
         mpo_back = twice.reshape(size, size)
-        return mpo_back.T, mpo_back, parted(far_env.transpose(1, 0, 2), lanes)
+        return mpo_back.T, mpo_back
+
+    def far_parts(*deps):
+        return parted(after(right_env, *deps).transpose(1, 0, 2), lanes, scattered)
 
     left, left_t = ordered(left_env.transpose(1, 0, 2), tile)
-    if halves == 1:
-        mpo_fore, mpo_back, right = environments()
+    if halves == 1 or n_rows == 2:
+        mpo_fore, mpo_back = mpo_pairs()
+    right = far_parts() if halves == 1 else None
 
     theta_all, total, last_round = None, [None], [()] * n_chunks
     cuts = 2 if groups % 2 == 0 and n_rows > 2 else 1
@@ -341,12 +345,10 @@
         pairs, blocks, fresh = [], [], []
 
         def ahead(*deps):
-            return [
-                fore(
-                    after(theta_all, *deps, *fresh), left, mpo_fore, right[h - 1], total[0], channels,
-                    len(fresh), cuts, F32, tile,
-                )
-            ]
+            return fore(
+                after(theta_all, *deps, *fresh), left, mpo_fore, right[h - 1], total[0], channels,
+                len(fresh), cuts, F32, tile,
+            )
 
         for c in range(n_chunks):
             piece = cut[:, c * per : (c + 1) * per].reshape(rows, per * lanes)
@@ -356,8 +358,12 @@
             came = list(pairs)
             if (h, t) == (0, 2):
                 pairs[0] = after(pairs[0], left, left_t)
+                if halves > 1:
+                    mpo_fore, mpo_back = mpo_pairs(*pairs)
+            if (h, t) == (0, 3) and halves > 1:
+                pairs[0] = after(pairs[0], mpo_fore, mpo_back)
             if (h, t) == (1, 2):
-                pairs = [after(pair, mpo_fore, mpo_back, right) for pair in pairs]
+                pairs = [after(pair, right, theta_all) for pair in pairs]
             if h > 0 and t > 2 and len(fresh) < cuts:
                 fresh += ahead(*sent)
                 pairs = [after(pair, fresh[-1]) for pair in pairs]
@@ -370,19 +376,19 @@
         total = fresh or total
         last_round = pairs
         if h == 0 and halves > 1:
-            mpo_fore, mpo_back, right = environments(*pairs)
+            right = far_parts(*pairs)
         theta_all = join(after(blocks, *fresh), n_rows)
 
     def forward(g, *deps):
         here = g * len(total) // groups
         return fore(
             after(theta_all, *deps), left, mpo_fore, right[-1], total[here], channels, g, groups,
-            BF16, tile, g % (groups // len(total)),
+            BF16, tile, g % (groups // len(total)), 2 if scattered else 1,
         )
 
     def backward(g, backs, *deps):
         parts = after(everyone[g], *deps)
-        return back(parts, mpo_back, right, backs, channels, phys_pair, g, groups, scattered, tile)
+        return back(parts, mpo_back, right, backs, channels, phys_pair, g, groups, tile)
 
     terms, near, own, far, everyone, backs = [], [], [], [], [], []
     step = 0
@@ -394,7 +400,7 @@
                 waits += done[step - lag : step - lag + 1] if step >= lag else []
         if step < groups:
             terms.append(forward(step, *waits))
-            out = terms[-1]
+            out = terms[-1][0]
         elif 0 <= g < len(everyone):
             backs = backward(g, backs, *waits)
             out = backs[-1]
@@ -411,10 +417,11 @@
         if len(far) < len(own):
             far.append(swapped(after(own[len(far)], out), "chan"))
         if len(own) < len(near):
-            mine, other = halved(after(near[len(own)], out), "chan")
-            own.append(add(mine, swapped(other, "chan")))
+            both = after(near[len(own)], out)
+            height = both.shape[0] // 2
+            own.append(add(both[:height], swapped(both[height:], "chan")))
         if len(near) < len(terms):
-            mine, other = halved(terms[len(near)], "col")
+            mine, other = terms[len(near)]
             near.append(add(mine, swapped(other, "col")))
     for g in range(step - groups, groups):
         backs = backward(g, backs)

time: 507 us -> 486 us (0.959)
  local copies, waits for them, and re-layouts: 21.1 us -> 13.2 us
  other arithmetic: 26.6 us -> 19.1 us
    ppermute x12, waiting for transfers between devices: 20.1 us -> 11.2 us  [gather_round(): lax.ppermute(pair[0], 'row', [(r, r + 1) for r in range(t - 1, n_rows - 1)])]
    ppermute x12, starting transfers between devices: 40.2 us -> 33.1 us  [gather_round(): lax.ppermute(pair[0], 'row', [(r, r + 1) for r in range(t - 1, n_rows - 1)])]
    ppermute x12, starting transfers between devices: 27.6 us -> 34.3 us  [gather_round(): lax.ppermute(pair[1], 'row', [(r, r - 1) for r in range(1, n_rows - t + 1)])]
    convert_element_type x16, other arithmetic: 16.3 us -> 9.95 us  [add(): return (x.astype(F32) + y.astype(F32)).astype(BF16)]
    ppermute x20, waiting for transfers between devices: 21.1 us -> 26.9 us  [swapped(): return lax.ppermute(block, axis, [(0, 1), (1, 0)])]
    dynamic_slice x8 -> x0, local copies, waits for them, and re-layouts: 5.38 us -> none  [halved(): lax.dynamic_slice_in_dim(term, k * height, height)]
  transfers between devices with their start and end apart: 68 -> 68, of which waited for: 14 -> 16; matrix products, arithmetic and copies ran while one was open for 8% -> 6% of each run, Pallas kernels for 37% -> 38%
where the time goes in v7:
time: 486 us; the launch traced here: 477 us
  Pallas kernels  222 us (46%)
  starting transfers between devices  149 us (31%)
  waiting for transfers between devices  68.8 us (14%)
  other arithmetic  19.1 us (4%)
  local copies, waits for them, and re-layouts  13.2 us (3%)
    pallas_call x6, Pallas kernels, fore(): pl.pallas_call(functools.partial(fore_kernel, channels, lanes, n_outs), g...  91.6 us
    pallas_call x4, Pallas kernels, back(): pl.pallas_call(functools.partial(back_kernel, channels, len(parts), count...  56.5 us
    ppermute x12, starting transfers between devices, scatter_round(): lax.ppermute(pair[1], 'row', [(n_rows - 1 - r, n_rows - 2 - r) for r in r...  50.3 us
    pallas_call x4, Pallas kernels, last(): pl.pallas_call(last_kernel, grid=(steps,), in_specs=[pl.BlockSpec(left_t....  43.2 us
    ppermute x12, starting transfers between devices, gather_round(): lax.ppermute(pair[1], 'row', [(r, r - 1) for r in range(1, n_rows - t + 1)])  34.3 us
    ppermute x12, starting transfers between devices, gather_round(): lax.ppermute(pair[0], 'row', [(r, r + 1) for r in range(t - 1, n_rows - 1)])  33.1 us
    ppermute x12, waiting for transfers between devices, scatter_round(): lax.ppermute(pair[1], 'row', [(n_rows - 1 - r, n_rows - 2 - r) for r in r...  27.2 us
    ppermute x20, waiting for transfers between devices, swapped(): return lax.ppermute(block, axis, [(0, 1), (1, 0)])  26.9 us
  transfers between devices with their start and end apart: 68, of which 16 were waited for; matrix products, arithmetic and copies ran while one was open for 6% of the time, Pallas kernels for 38%

profile of v7, /device:TPU:16, one launch (start us, length us, event | category | flops | bytes accessed | tf_op | source)
XLA Modules:
  0.0 476.6 jit_solution(10715843967202045317)
XLA Ops:
  28.5 12.0 %shard_map.68 = (bf16[3072,1024]{1,0:T(8,128)(2,1)}, bf16[1024,3072]{1,0:T(8,128)(2,1)}) custom-call(bf16[12,256,1024]{2,1,0:T(8,128)(2,1)} %bitcast.40, bf16[384,384]{1,0:T(8,128)(2,1)} %fusion.9.order_ref), custom_call_target="tpu_custom_call" | custom-call | flops 301989888 | bytes 1179648 | tf_op jit(solution)/shard_map/pallas_call | solution.py:50
  85.5 9.7 %shard_map.69 = (bf16[1024,1536]{1,0:T(8,128)(2,1)}, bf16[1024,1536]{1,0:T(8,128)(2,1)}) custom-call(bf16[12,1024,256]{2,1,0:T(8,128)(2,1)} %bitcast.41), custom_call_target="tpu_custom_call" | custom-call | bytes 786432 | tf_op jit(solution)/shard_map/pallas_call | solution.py:84
  116.1 21.4 %shard_map.71.refs_0_ = f32[1024,2048]{1,0:T(8,128)} custom-call(bf16[1024,2048]{1,0:T(8,128)(2,1)} %shard_map.70.theta_ref, bf16[3072,1024]{1,0:T(8,128)(2,1)} %get-tuple-element.150.left_ref, bf16[384,384]{1,0:T(8,128)(2,1)S(1)} %copy.25.mpo_ref, bf16[1024,1536]{1,0:T(8,128)(2,1)S(1)} %copy-done.3), custom_call_target="tpu_custom_call" | custom-call | flops 956301312 | bytes 1179648 | tf_op jit(solution)/shard_map/pallas_call | solution.py:130
  142.4 21.5 %shard_map.72.refs_0_ = f32[1024,2048]{1,0:T(8,128)} custom-call(bf16[1024,2048]{1,0:T(8,128)(2,1)} %shard_map.70.theta_ref, bf16[3072,1024]{1,0:T(8,128)(2,1)} %get-tuple-element.150.left_ref, bf16[384,384]{1,0:T(8,128)(2,1)S(1)} %copy.25.mpo_ref, bf16[1024,1536]{1,0:T(8,128)(2,1)S(1)} %copy-done.3), custom_call_target="tpu_custom_call" | custom-call | flops 956301312 | bytes 1179648 | tf_op jit(solution)/shard_map/pallas_call | solution.py:130
  169.4 12.1 %shard_map.74 = (bf16[512,1024]{1,0:T(8,128)(2,1)S(1)}, bf16[512,1024]{1,0:T(8,128)(2,1)S(1)}) custom-call(bf16[1024,2048]{1,0:T(8,128)(2,1)} %shard_map.73.theta_ref, bf16[3072,1024]{1,0:T(8,128)(2,1)} %get-tuple-element.150.left_ref, bf16[384,384]{1,0:T(8,128)(2,1)S(1)} %copy.25.mpo_ref, bf16[1024,1536]{1,0:T(8,128)(2,1)S(1)} %copy-done.2, ...), custom_call_target="tpu_custom_call" | custom-call | flops 478150656 | bytes 819200 | tf_op jit(solution)/shard_map/pallas_call | solution.py:130
  181.6 12.1 %shard_map.75 = (bf16[512,1024]{1,0:T(8,128)(2,1)S(1)}, bf16[512,1024]{1,0:T(8,128)(2,1)S(1)}) custom-call(bf16[1024,2048]{1,0:T(8,128)(2,1)} %shard_map.73.theta_ref, bf16[3072,1024]{1,0:T(8,128)(2,1)} %get-tuple-element.150.left_ref, bf16[384,384]{1,0:T(8,128)(2,1)S(1)} %copy.25.mpo_ref, bf16[1024,1536]{1,0:T(8,128)(2,1)S(1)} %copy-done.2, ...), custom_call_target="tpu_custom_call" | custom-call | flops 478150656 | bytes 819200 | tf_op jit(solution)/shard_map/pallas_call | solution.py:130
  196.3 12.5 %shard_map.76 = (bf16[512,1024]{1,0:T(8,128)(2,1)S(1)}, bf16[512,1024]{1,0:T(8,128)(2,1)S(1)}) custom-call(bf16[1024,2048]{1,0:T(8,128)(2,1)} %shard_map.73.theta_ref, bf16[3072,1024]{1,0:T(8,128)(2,1)} %get-tuple-element.150.left_ref, bf16[384,384]{1,0:T(8,128)(2,1)S(1)} %copy.25.mpo_ref, bf16[1024,1536]{1,0:T(8,128)(2,1)S(1)} %copy-done.2, ...), custom_call_target="tpu_custom_call" | custom-call | flops 478150656 | bytes 819200 | tf_op jit(solution)/shard_map/pallas_call | solution.py:130
  211.7 12.1 %shard_map.77 = (bf16[512,1024]{1,0:T(8,128)(2,1)S(1)}, bf16[512,1024]{1,0:T(8,128)(2,1)S(1)}) custom-call(bf16[1024,2048]{1,0:T(8,128)(2,1)} %shard_map.73.theta_ref, bf16[3072,1024]{1,0:T(8,128)(2,1)} %get-tuple-element.150.left_ref, bf16[384,384]{1,0:T(8,128)(2,1)S(1)} %copy.25.mpo_ref, bf16[1024,1536]{1,0:T(8,128)(2,1)S(1)} %copy-done.2, ...), custom_call_target="tpu_custom_call" | custom-call | flops 478150656 | bytes 819200 | tf_op jit(solution)/shard_map/pallas_call | solution.py:130
  224.9 10.4 %collective-permute-done.31.refs_1_ = bf16[256,1024]{1,0:T(8,128)(2,1)S(1)} collective-permute-done((bf16[256,1024]{1,0:T(8,128)(2,1)S(1)}, bf16[256,1024]{1,0:T(8,128)(2,1)S(1)}, u32[]{:S(2)}, u32[]{:S(2)}) %collective-permute-start.31) | collective-permute-done | bytes 524320 | tf_op jit(solution)/shard_map/ppermute | solution.py:309
  237.2 14.1 %shard_map.78 = (bf16[3072,2048]{1,0:T(8,128)(2,1)}, bf16[3072,2048]{1,0:T(8,128)(2,1)}) custom-call(bf16[256,1024]{1,0:T(8,128)(2,1)S(1)} %add_convert_fusion.19.refs_0_, bf16[256,1024]{1,0:T(8,128)(2,1)S(1)} %collective-permute-done.31.refs_1_, bf16[256,1024]{1,0:T(8,128)(2,1)S(1)} %collective-permute-done.32.refs_2_, ...), custom_call_target="tpu_custom_call" | custom-call | flops 553648128 | bytes 917504 | tf_op jit(solution)/shard_map/pallas_call | solution.py:194
  260.2 13.9 %shard_map.79 = (bf16[3072,2048]{1,0:T(8,128)(2,1)}, bf16[3072,2048]{1,0:T(8,128)(2,1)}) custom-call(bf16[256,1024]{1,0:T(8,128)(2,1)S(1)} %add_convert_fusion.18.refs_0_, bf16[256,1024]{1,0:T(8,128)(2,1)S(1)} %collective-permute-done.35.refs_1_, ...), custom_call_target="tpu_custom_call", output_to_operand_aliasing={{0}: (7, {}), {1}: (8, {})} | custom-call | flops 553648128 | bytes 917504 | tf_op jit(solution)/shard_map/pallas_call | solution.py:194
  274.7 7.8 %collective-permute-done.34 = bf16[256,1024]{1,0:T(8,128)(2,1)S(1)} collective-permute-done((bf16[256,1024]{1,0:T(8,128)(2,1)S(1)}, bf16[256,1024]{1,0:T(8,128)(2,1)S(1)}, u32[]{:S(2)}, u32[]{:S(2)}) %collective-permute-start.34) | collective-permute-done | bytes 524320 | tf_op jit(solution)/shard_map/ppermute | solution.py:309
  284.0 13.9 %shard_map.80 = (bf16[3072,2048]{1,0:T(8,128)(2,1)}, bf16[3072,2048]{1,0:T(8,128)(2,1)}) custom-call(bf16[256,1024]{1,0:T(8,128)(2,1)S(1)} %add_convert_fusion.17.refs_0_, bf16[256,1024]{1,0:T(8,128)(2,1)S(1)} %collective-permute-done.39.refs_1_, ...), custom_call_target="tpu_custom_call", output_to_operand_aliasing={{0}: (7, {}), {1}: (8, {})} | custom-call | flops 553648128 | bytes 917504 | tf_op jit(solution)/shard_map/pallas_call | solution.py:194
  300.3 14.5 %shard_map.81 = (bf16[3072,2048]{1,0:T(8,128)(2,1)}, bf16[3072,2048]{1,0:T(8,128)(2,1)}) custom-call(bf16[256,1024]{1,0:T(8,128)(2,1)} %add_convert_fusion.16.refs_0_, bf16[256,1024]{1,0:T(8,128)(2,1)} %collective-permute-done.38.refs_1_, bf16[256,1024]{1,0:T(8,128)(2,1)} %collective-permute-done.42.refs_2_, ...), custom_call_target="tpu_custom_call", output_to_operand_aliasing={{0}: (7, {}), {1}: (8, {})} | custom-call | flops 553648128 | bytes 917504 | tf_op jit(solution)/shard_map/pallas_call | solution.py:194
  314.9 10.7 %shard_map.82 = bf16[1024,1024]{1,0:T(8,128)(2,1)S(1)} custom-call(bf16[1024,3072]{1,0:T(8,128)(2,1)} %get-tuple-element.151.left_ref, bf16[3072,2048]{1,0:T(8,128)(2,1)} %get-tuple-element.252.back_ref), custom_call_target="tpu_custom_call" | custom-call | flops 402653184 | bytes 917504 | tf_op jit(solution)/shard_map/pallas_call | solution.py:227
  329.5 10.8 %shard_map.83 = bf16[1024,1024]{1,0:T(8,128)(2,1)S(1)} custom-call(bf16[1024,3072]{1,0:T(8,128)(2,1)} %get-tuple-element.151.left_ref, bf16[3072,2048]{1,0:T(8,128)(2,1)} %get-tuple-element.252.back_ref), custom_call_target="tpu_custom_call" | custom-call | flops 402653184 | bytes 917504 | tf_op jit(solution)/shard_map/pallas_call | solution.py:227
  352.2 10.7 %shard_map.84 = bf16[1024,1024]{1,0:T(8,128)(2,1)S(1)} custom-call(bf16[1024,3072]{1,0:T(8,128)(2,1)} %get-tuple-element.151.left_ref, bf16[3072,2048]{1,0:T(8,128)(2,1)} %get-tuple-element.271.back_ref), custom_call_target="tpu_custom_call" | custom-call | flops 402653184 | bytes 917504 | tf_op jit(solution)/shard_map/pallas_call | solution.py:227
  381.4 11.0 %shard_map.85 = bf16[1024,1024]{1,0:T(8,128)(2,1)S(1)} custom-call(bf16[1024,3072]{1,0:T(8,128)(2,1)} %get-tuple-element.151.left_ref, bf16[3072,2048]{1,0:T(8,128)(2,1)} %get-tuple-element.271.back_ref), custom_call_target="tpu_custom_call" | custom-call | flops 402653184 | bytes 917504 | tf_op jit(solution)/shard_map/pallas_call | solution.py:227
  402.5 7.5 %collective-permute-done.63 = bf16[256,1024]{1,0:T(8,128)(2,1)S(1)} collective-permute-done((bf16[256,1024]{1,0:T(8,128)(2,1)S(1)}, bf16[256,1024]{1,0:T(8,128)(2,1)S(1)}, u32[]{:S(2)}, u32[]{:S(2)}) %collective-permute-start.63) | collective-permute-done | bytes 524320 | tf_op jit(solution)/shard_map/ppermute | solution.py:300
  410.0 8.4 %collective-permute-start.59 = (bf16[256,1024]{1,0:T(8,128)(2,1)S(1)}, bf16[256,1024]{1,0:T(8,128)(2,1)S(1)}, u32[]{:S(2)}, u32[]{:S(2)}) collective-permute-start(bf16[256,1024]{1,0:T(8,128)(2,1)S(1)} %get-tuple-element.279), channel_id=1, source_target_pairs={{12,8},{8,4},{13,9},{9,5},{14,10},{10,6},{15,11},{11,7},{28,24},{2... | collective-permute-start | bytes 1572872 | tf_op jit(solution)/shard_map/ppermute | solution.py:300
  429.2 9.6 %collective-permute-start.55 = (bf16[256,1024]{1,0:T(8,128)(2,1)S(1)}, bf16[256,1024]{1,0:T(8,128)(2,1)S(1)}, u32[]{:S(2)}, u32[]{:S(2)}) collective-permute-start(bf16[256,1024]{1,0:T(8,128)(2,1)S(1)} %get-tuple-element.275), channel_id=1, source_target_pairs={{12,8},{8,4},{4,0},{13,9},{9,5},{5,1},{14,10},{10,6},{6,2},{15,11}... | collective-permute-start | bytes 1572872 | tf_op jit(solution)/shard_map/ppermute | solution.py:300
  441.2 8.9 %collective-permute-start.61 = (bf16[256,1024]{1,0:T(8,128)(2,1)S(1)}, bf16[256,1024]{1,0:T(8,128)(2,1)S(1)}, u32[]{:S(2)}, u32[]{:S(2)}) collective-permute-start(bf16[256,1024]{1,0:T(8,128)(2,1)S(1)} %get-tuple-element.283), channel_id=1, source_target_pairs={{12,8},{8,4},{4,0},{13,9},{9,5},{5,1},{14,10},{10,6},{6,2},{15,11}... | collective-permute-start | bytes 1572872 | tf_op jit(solution)/shard_map/ppermute | solution.py:300
  456.8 9.4 %collective-permute-done.61 = bf16[256,1024]{1,0:T(8,128)(2,1)S(1)} collective-permute-done((bf16[256,1024]{1,0:T(8,128)(2,1)S(1)}, bf16[256,1024]{1,0:T(8,128)(2,1)S(1)}, u32[]{:S(2)}, u32[]{:S(2)}) %collective-permute-start.61) | collective-permute-done | bytes 524320 | tf_op jit(solution)/shard_map/ppermute | solution.py:300
  466.5 7.7 %collective-permute-done.67 = bf16[256,1024]{1,0:T(8,128)(2,1)S(1)} collective-permute-done((bf16[256,1024]{1,0:T(8,128)(2,1)S(1)}, bf16[256,1024]{1,0:T(8,128)(2,1)S(1)}, u32[]{:S(2)}, u32[]{:S(2)}) %collective-permute-start.67) | collective-permute-done | bytes 524320 | tf_op jit(solution)/shard_map/ppermute | solution.py:300
  (230 shorter events, 191.7 us)
Async XLA Ops:
  9.4 31.1 %collective-permute-start = (bf16[256,1024]{1,0:T(8,128)(2,1)S(1)}, bf16[256,1024]{1,0:T(8,128)(2,1)}, u32[]{:S(2)}, u32[]{:S(2)}) collective-permute-start(bf16[256,1024]{1,0:T(8,128)(2,1)S(1)} %bitcast.46), channel_id=1, source_target_pairs={{0,4},{4,8},{8,12},{1,5},{5,9},{9,13},{2,6},{6,10},{10,14},{3,7},{... | collective-permute-start | bytes 1572872 | tf_op jit(solution)/shard_map/ppermute | solution.py:280
  13.7 26.8 %collective-permute-start.1 = (bf16[256,1024]{1,0:T(8,128)(2,1)S(1)}, bf16[256,1024]{1,0:T(8,128)(2,1)}, u32[]{:S(2)}, u32[]{:S(2)}) collective-permute-start(bf16[256,1024]{1,0:T(8,128)(2,1)S(1)} %bitcast.47), channel_id=1, source_target_pairs={{4,0},{8,4},{12,8},{5,1},{9,5},{13,9},{6,2},{10,6},{14,10},{7,3},{... | collective-permute-start | bytes 1572872 | tf_op jit(solution)/shard_map/ppermute | solution.py:281
  20.2 33.2 %collective-permute-start.10 = (bf16[256,1024]{1,0:T(8,128)(2,1)S(1)}, bf16[256,1024]{1,0:T(8,128)(2,1)}, u32[]{:S(2)}, u32[]{:S(2)}) collective-permute-start(bf16[256,1024]{1,0:T(8,128)(2,1)S(1)} %collective-permute-done.4.refs_9_), channel_id=1, source_target_pairs={{4,8},{8,12},{5,9},{9,13},{6,10},{10,14},{7,11},{11,15},{20,24},{2... | collective-permute-start | bytes 1572872 | tf_op jit(solution)/shard_map/ppermute | solution.py:280
  23.8 31.7 %collective-permute-start.12 = (bf16[256,1024]{1,0:T(8,128)(2,1)}, bf16[256,1024]{1,0:T(8,128)(2,1)}, u32[]{:S(2)}, u32[]{:S(2)}) collective-permute-start(bf16[256,1024]{1,0:T(8,128)(2,1)} %collective-permute-done.5.refs_11_), channel_id=1, source_target_pairs={{4,0},{8,4},{5,1},{9,5},{6,2},{10,6},{7,3},{11,7},{20,16},{24,20},... | collective-permute-start | bytes 1572872 | tf_op jit(solution)/shard_map/ppermute | solution.py:281
  66.7 33.0 %collective-permute-start.16 = (bf16[256,1024]{1,0:T(8,128)(2,1)S(1)}, bf16[256,1024]{1,0:T(8,128)(2,1)}, u32[]{:S(2)}, u32[]{:S(2)}) collective-permute-start(bf16[256,1024]{1,0:T(8,128)(2,1)S(1)} %bitcast.49), channel_id=1, source_target_pairs={{0,4},{4,8},{8,12},{1,5},{5,9},{9,13},{2,6},{6,10},{10,14},{3,7},{... | collective-permute-start | bytes 1572872 | tf_op jit(solution)/shard_map/ppermute | solution.py:280
  71.0 28.6 %collective-permute-start.17 = (bf16[256,1024]{1,0:T(8,128)(2,1)S(1)}, bf16[256,1024]{1,0:T(8,128)(2,1)}, u32[]{:S(2)}, u32[]{:S(2)}) collective-permute-start(bf16[256,1024]{1,0:T(8,128)(2,1)S(1)} %bitcast.50), channel_id=1, source_target_pairs={{4,0},{8,4},{12,8},{5,1},{9,5},{13,9},{6,2},{10,6},{14,10},{7,3},{... | collective-permute-start | bytes 1572872 | tf_op jit(solution)/shard_map/ppermute | solution.py:281
  77.9 29.4 %collective-permute-start.8 = (bf16[256,1024]{1,0:T(8,128)(2,1)S(1)}, bf16[256,1024]{1,0:T(8,128)(2,1)}, u32[]{:S(2)}, u32[]{:S(2)}) collective-permute-start(bf16[256,1024]{1,0:T(8,128)(2,1)S(1)} %bitcast.52), channel_id=1, source_target_pairs={{0,4},{4,8},{8,12},{1,5},{5,9},{9,13},{2,6},{6,10},{10,14},{3,7},{... | collective-permute-start | bytes 1572872 | tf_op jit(solution)/shard_map/ppermute | solution.py:280
  99.7 37.8 %collective-permute-start.20 = (bf16[256,1024]{1,0:T(8,128)(2,1)}, bf16[256,1024]{1,0:T(8,128)(2,1)}, u32[]{:S(2)}, u32[]{:S(2)}) collective-permute-start(bf16[256,1024]{1,0:T(8,128)(2,1)} %collective-permute-done.16.refs_9_), channel_id=1, source_target_pairs={{4,8},{8,12},{5,9},{9,13},{6,10},{10,14},{7,11},{11,15},{20,24},{2... | collective-permute-start | bytes 1572872 | tf_op jit(solution)/shard_map/ppermute | solution.py:280
  103.1 34.5 %collective-permute-start.21 = (bf16[256,1024]{1,0:T(8,128)(2,1)}, bf16[256,1024]{1,0:T(8,128)(2,1)}, u32[]{:S(2)}, u32[]{:S(2)}) collective-permute-start(bf16[256,1024]{1,0:T(8,128)(2,1)} %collective-permute-done.17.refs_11_), channel_id=1, source_target_pairs={{4,0},{8,4},{5,1},{9,5},{6,2},{10,6},{7,3},{11,7},{20,16},{24,20},... | collective-permute-start | bytes 1572872 | tf_op jit(solution)/shard_map/ppermute | solution.py:281
  107.3 32.3 %collective-permute-start.14 = (bf16[256,1024]{1,0:T(8,128)(2,1)}, bf16[256,1024]{1,0:T(8,128)(2,1)}, u32[]{:S(2)}, u32[]{:S(2)}) collective-permute-start(bf16[256,1024]{1,0:T(8,128)(2,1)} %collective-permute-done.8.refs_2_), channel_id=1, source_target_pairs={{4,8},{8,12},{5,9},{9,13},{6,10},{10,14},{7,11},{11,15},{20,24},{2... | collective-permute-start | bytes 1572872 | tf_op jit(solution)/shard_map/ppermute | solution.py:280
  109.2 30.4 %collective-permute-start.15 = (bf16[256,1024]{1,0:T(8,128)(2,1)}, bf16[256,1024]{1,0:T(8,128)(2,1)}, u32[]{:S(2)}, u32[]{:S(2)}) collective-permute-start(bf16[256,1024]{1,0:T(8,128)(2,1)} %collective-permute-done.9.refs_4_), channel_id=1, source_target_pairs={{4,0},{8,4},{5,1},{9,5},{6,2},{10,6},{7,3},{11,7},{20,16},{24,20},... | collective-permute-start | bytes 1572872 | tf_op jit(solution)/shard_map/ppermute | solution.py:281
  208.8 26.6 %collective-permute-start.28 = (bf16[512,1024]{1,0:T(8,128)(2,1)S(1)}, bf16[512,1024]{1,0:T(8,128)(2,1)S(1)}, u32[]{:S(2)}, u32[]{:S(2)}) collective-permute-start(bf16[512,1024]{1,0:T(8,128)(2,1)S(1)} %get-tuple-element.213), channel_id=1, source_target_pairs={{0,2},{2,0},{1,3},{3,1},{4,6},{6,4},{5,7},{7,5},{8,10},{10,8},{9,1... | collective-permute-start | bytes 3145736 | tf_op jit(solution)/shard_map/ppermute | solution.py:309
  224.3 27.0 %collective-permute-start.35 = (bf16[256,1024]{1,0:T(8,128)(2,1)S(1)}, bf16[256,1024]{1,0:T(8,128)(2,1)S(1)}, u32[]{:S(2)}, u32[]{:S(2)}) collective-permute-start(bf16[256,1024]{1,0:T(8,128)(2,1)S(1)} %add_convert_fusion.18.refs_0_), channel_id=1, source_target_pairs={{0,1},{1,0},{2,3},{3,2},{4,5},{5,4},{6,7},{7,6},{8,9},{9,8},{10,11... | collective-permute-start | bytes 1572872 | tf_op jit(solution)/shard_map/ppermute | solution.py:309
  224.9 33.3 %collective-permute-start.30 = (bf16[512,1024]{1,0:T(8,128)(2,1)S(1)}, bf16[512,1024]{1,0:T(8,128)(2,1)S(1)}, u32[]{:S(2)}, u32[]{:S(2)}) collective-permute-start(bf16[512,1024]{1,0:T(8,128)(2,1)S(1)} %get-tuple-element.217), channel_id=1, source_target_pairs={{0,2},{2,0},{1,3},{3,1},{4,6},{6,4},{5,7},{7,5},{8,10},{10,8},{9,1... | collective-permute-start | bytes 3145736 | tf_op jit(solution)/shard_map/ppermute | solution.py:309
  346.4 27.5 %collective-permute-start.46 = (bf16[256,1024]{1,0:T(8,128)(2,1)S(1)}, bf16[256,1024]{1,0:T(8,128)(2,1)S(1)}, u32[]{:S(2)}, u32[]{:S(2)}) collective-permute-start(bf16[256,1024]{1,0:T(8,128)(2,1)S(1)} %get-tuple-element.255), channel_id=1, source_target_pairs={{0,4},{4,8},{1,5},{5,9},{2,6},{6,10},{3,7},{7,11},{16,20},{20,24},... | collective-permute-start | bytes 1572872 | tf_op jit(solution)/shard_map/ppermute | solution.py:299
  347.7 27.5 %collective-permute-start.47 = (bf16[256,1024]{1,0:T(8,128)(2,1)S(1)}, bf16[256,1024]{1,0:T(8,128)(2,1)S(1)}, u32[]{:S(2)}, u32[]{:S(2)}) collective-permute-start(bf16[256,1024]{1,0:T(8,128)(2,1)S(1)} %get-tuple-element.256), channel_id=1, source_target_pairs={{12,8},{8,4},{13,9},{9,5},{14,10},{10,6},{15,11},{11,7},{28,24},{2... | collective-permute-start | bytes 1572872 | tf_op jit(solution)/shard_map/ppermute | solution.py:300
  364.7 27.8 %collective-permute-start.52 = (bf16[256,1024]{1,0:T(8,128)(2,1)S(1)}, bf16[256,1024]{1,0:T(8,128)(2,1)S(1)}, u32[]{:S(2)}, u32[]{:S(2)}) collective-permute-start(bf16[256,1024]{1,0:T(8,128)(2,1)S(1)} %get-tuple-element.267), channel_id=1, source_target_pairs={{0,4},{4,8},{1,5},{5,9},{2,6},{6,10},{3,7},{7,11},{16,20},{20,24},... | collective-permute-start | bytes 1572872 | tf_op jit(solution)/shard_map/ppermute | solution.py:299
  366.0 26.5 %collective-permute-start.53 = (bf16[256,1024]{1,0:T(8,128)(2,1)S(1)}, bf16[256,1024]{1,0:T(8,128)(2,1)S(1)}, u32[]{:S(2)}, u32[]{:S(2)}) collective-permute-start(bf16[256,1024]{1,0:T(8,128)(2,1)S(1)} %get-tuple-element.268), channel_id=1, source_target_pairs={{12,8},{8,4},{13,9},{9,5},{14,10},{10,6},{15,11},{11,7},{28,24},{2... | collective-permute-start | bytes 1572872 | tf_op jit(solution)/shard_map/ppermute | solution.py:300
  376.8 41.9 %collective-permute-start.48 = (bf16[256,1024]{1,0:T(8,128)(2,1)S(1)}, bf16[256,1024]{1,0:T(8,128)(2,1)S(1)}, u32[]{:S(2)}, u32[]{:S(2)}) collective-permute-start(bf16[256,1024]{1,0:T(8,128)(2,1)S(1)} %get-tuple-element.263), channel_id=1, source_target_pairs={{0,4},{4,8},{8,12},{1,5},{5,9},{9,13},{2,6},{6,10},{10,14},{3,7},{... | collective-permute-start | bytes 1572872 | tf_op jit(solution)/shard_map/ppermute | solution.py:299
  396.9 55.6 %collective-permute-start.54 = (bf16[256,1024]{1,0:T(8,128)(2,1)S(1)}, bf16[256,1024]{1,0:T(8,128)(2,1)S(1)}, u32[]{:S(2)}, u32[]{:S(2)}) collective-permute-start(bf16[256,1024]{1,0:T(8,128)(2,1)S(1)} %get-tuple-element.274), channel_id=1, source_target_pairs={{0,4},{4,8},{8,12},{1,5},{5,9},{9,13},{2,6},{6,10},{10,14},{3,7},{... | collective-permute-start | bytes 1572872 | tf_op jit(solution)/shard_map/ppermute | solution.py:299
  401.2 28.0 %collective-permute-start.58 = (bf16[256,1024]{1,0:T(8,128)(2,1)S(1)}, bf16[256,1024]{1,0:T(8,128)(2,1)S(1)}, u32[]{:S(2)}, u32[]{:S(2)}) collective-permute-start(bf16[256,1024]{1,0:T(8,128)(2,1)S(1)} %get-tuple-element.278), channel_id=1, source_target_pairs={{0,4},{4,8},{1,5},{5,9},{2,6},{6,10},{3,7},{7,11},{16,20},{20,24},... | collective-permute-start | bytes 1572872 | tf_op jit(solution)/shard_map/ppermute | solution.py:299
  410.0 28.9 %collective-permute-start.59 = (bf16[256,1024]{1,0:T(8,128)(2,1)S(1)}, bf16[256,1024]{1,0:T(8,128)(2,1)S(1)}, u32[]{:S(2)}, u32[]{:S(2)}) collective-permute-start(bf16[256,1024]{1,0:T(8,128)(2,1)S(1)} %get-tuple-element.279), channel_id=1, source_target_pairs={{12,8},{8,4},{13,9},{9,5},{14,10},{10,6},{15,11},{11,7},{28,24},{2... | collective-permute-start | bytes 1572872 | tf_op jit(solution)/shard_map/ppermute | solution.py:300
  421.2 28.9 %collective-permute-start.65 = (bf16[256,1024]{1,0:T(8,128)(2,1)S(1)}, bf16[256,1024]{1,0:T(8,128)(2,1)S(1)}, u32[]{:S(2)}, u32[]{:S(2)}) collective-permute-start(bf16[256,1024]{1,0:T(8,128)(2,1)S(1)} %get-tuple-element.289), channel_id=1, source_target_pairs={{12,8},{8,4},{13,9},{9,5},{14,10},{10,6},{15,11},{11,7},{28,24},{2... | collective-permute-start | bytes 1572872 | tf_op jit(solution)/shard_map/ppermute | solution.py:300
  429.2 27.2 %collective-permute-start.55 = (bf16[256,1024]{1,0:T(8,128)(2,1)S(1)}, bf16[256,1024]{1,0:T(8,128)(2,1)S(1)}, u32[]{:S(2)}, u32[]{:S(2)}) collective-permute-start(bf16[256,1024]{1,0:T(8,128)(2,1)S(1)} %get-tuple-element.275), channel_id=1, source_target_pairs={{12,8},{8,4},{4,0},{13,9},{9,5},{5,1},{14,10},{10,6},{6,2},{15,11}... | collective-permute-start | bytes 1572872 | tf_op jit(solution)/shard_map/ppermute | solution.py:300
  (70 other events, 1207.8 us)

commit v8 on v7

--- a/solution.py
+++ b/solution.py
@@ -26,7 +26,7 @@
 
 
 def cost(flops, moved):
-    return pl.CostEstimate(flops=int(flops) // 16, bytes_accessed=int(moved) // 16, transcendentals=0)
+    return pl.CostEstimate(flops=int(flops), bytes_accessed=int(moved), transcendentals=0)
 
 
 def block_of(k):
@@ -309,6 +309,11 @@
     return lax.ppermute(block, axis, [(0, 1), (1, 0)])
 
 
+def scattered_along(both):
+    height = both.shape[0] // 2
+    return add(both[:height], swapped(both[height:], "chan"))
+
+
 def shards(theta, left_env, right_env, mpo_left, mpo_right):
     bonds, channels, depth = left_env.shape
     rows, phys_pair, width = theta.shape
@@ -398,6 +403,7 @@
         if scattered:
             for lag, done in ((2, near), (3, own), (4, far)):
                 waits += done[step - lag : step - lag + 1] if step >= lag else []
+                waits += done[:1] if step == lag - 1 else []
         if step < groups:
             terms.append(forward(step, *waits))
             out = terms[-1][0]
@@ -417,12 +423,12 @@
         if len(far) < len(own):
             far.append(swapped(after(own[len(far)], out), "chan"))
         if len(own) < len(near):
-            both = after(near[len(own)], out)
-            height = both.shape[0] // 2
-            own.append(add(both[:height], swapped(both[height:], "chan")))
+            own.append(scattered_along(after(near[len(own)], out)))
         if len(near) < len(terms):
             mine, other = terms[len(near)]
             near.append(add(mine, swapped(other, "col")))
+        if step == 1:
+            own.append(scattered_along(near[0]))
     for g in range(step - groups, groups):
         backs = backward(g, backs)
 

time: 486 us -> 480 us (0.988)
  the two profiles are of different devices: /device:TPU:16 before, /device:TPU:8 now
where the time goes in v8:
time: 480 us; the launch traced here: 471 us
  Pallas kernels  222 us (46%)
  starting transfers between devices  127 us (26%)
  waiting for transfers between devices  87 us (18%)
  other arithmetic  15.8 us (3%)
  local copies, waits for them, and re-layouts  14.4 us (3%)
    pallas_call x6, Pallas kernels, fore(): pl.pallas_call(functools.partial(fore_kernel, channels, lanes, n_outs), g...  91.6 us
    pallas_call x4, Pallas kernels, back(): pl.pallas_call(functools.partial(back_kernel, channels, len(parts), count...  56.5 us
    ppermute x12, waiting for transfers between devices, scatter_round(): up = lax.ppermute(pair[0], 'row', [(r, r + 1) for r in range(t)])  44.3 us
    pallas_call x4, Pallas kernels, last(): pl.pallas_call(last_kernel, grid=(steps,), in_specs=[pl.BlockSpec(left_t....  43.2 us
    ppermute x12, starting transfers between devices, scatter_round(): up = lax.ppermute(pair[0], 'row', [(r, r + 1) for r in range(t)])  37.1 us
    ppermute x12, starting transfers between devices, gather_round(): lax.ppermute(pair[1], 'row', [(r, r - 1) for r in range(1, n_rows - t + 1)])  32.8 us
    ppermute x12, starting transfers between devices, gather_round(): lax.ppermute(pair[0], 'row', [(r, r + 1) for r in range(t - 1, n_rows - 1)])  30.2 us
    ppermute x20, waiting for transfers between devices, swapped(): return lax.ppermute(block, axis, [(0, 1), (1, 0)])  20.1 us
  transfers between devices with their start and end apart: 68, of which 19 were waited for; matrix products, arithmetic and copies ran while one was open for 5% of the time, Pallas kernels for 38%

profile of v8, /device:TPU:8, one launch (start us, length us, event | category | flops | bytes accessed | tf_op | source)
XLA Modules:
  0.0 470.7 jit_solution(9919547284806548153)
XLA Ops:
  26.4 12.0 %shard_map.68 = (bf16[3072,1024]{1,0:T(8,128)(2,1)}, bf16[1024,3072]{1,0:T(8,128)(2,1)}) custom-call(bf16[12,256,1024]{2,1,0:T(8,128)(2,1)} %bitcast.57, bf16[384,384]{1,0:T(8,128)(2,1)} %fusion.9.order_ref), custom_call_target="tpu_custom_call" | custom-call | flops 4831838208 | bytes 18874368 | tf_op jit(solution)/shard_map/pallas_call | solution.py:50
  38.4 5.6 %collective-permute-start.2 = (bf16[256,1024]{1,0:T(8,128)(2,1)}, bf16[256,1024]{1,0:T(8,128)(2,1)}, u32[]{:S(2)}, u32[]{:S(2)}) collective-permute-start(bf16[256,1024]{1,0:T(8,128)(2,1)} %collective-permute-done.refs_2_), channel_id=1, source_target_pairs={{4,8},{8,12},{5,9},{9,13},{6,10},{10,14},{7,11},{11,15},{20,24},{2... | collective-permute-start | bytes 1572872 | tf_op jit(solution)/shard_map/ppermute | solution.py:280
  87.9 9.8 %shard_map.69 = (bf16[1024,1536]{1,0:T(8,128)(2,1)}, bf16[1024,1536]{1,0:T(8,128)(2,1)}) custom-call(bf16[12,1024,256]{2,1,0:T(8,128)(2,1)} %bitcast.40), custom_call_target="tpu_custom_call" | custom-call | bytes 12582912 | tf_op jit(solution)/shard_map/pallas_call | solution.py:84
  111.6 21.5 %shard_map.71.refs_0_ = f32[1024,2048]{1,0:T(8,128)} custom-call(bf16[1024,2048]{1,0:T(8,128)(2,1)} %shard_map.70.theta_ref, bf16[3072,1024]{1,0:T(8,128)(2,1)} %get-tuple-element.150.left_ref, bf16[384,384]{1,0:T(8,128)(2,1)S(1)} %copy-done.7, bf16[1024,1536]{1,0:T(8,128)(2,1)S(1)} %copy-done.2), custom_call_target="tpu_custom_call" | custom-call | flops 15300820992 | bytes 18874368 | tf_op jit(solution)/shard_map/pallas_call | solution.py:130
  138.0 21.4 %shard_map.72.refs_0_ = f32[1024,2048]{1,0:T(8,128)} custom-call(bf16[1024,2048]{1,0:T(8,128)(2,1)} %shard_map.70.theta_ref, bf16[3072,1024]{1,0:T(8,128)(2,1)} %get-tuple-element.150.left_ref, bf16[384,384]{1,0:T(8,128)(2,1)S(1)} %copy-done.7, bf16[1024,1536]{1,0:T(8,128)(2,1)S(1)} %copy-done.2), custom_call_target="tpu_custom_call" | custom-call | flops 15300820992 | bytes 18874368 | tf_op jit(solution)/shard_map/pallas_call | solution.py:130
  165.5 12.1 %shard_map.74 = (bf16[512,1024]{1,0:T(8,128)(2,1)S(1)}, bf16[512,1024]{1,0:T(8,128)(2,1)S(1)}) custom-call(bf16[1024,2048]{1,0:T(8,128)(2,1)} %shard_map.73.theta_ref, bf16[3072,1024]{1,0:T(8,128)(2,1)} %get-tuple-element.150.left_ref, bf16[384,384]{1,0:T(8,128)(2,1)S(1)} %copy-done.8, bf16[1024,1536]{1,0:T(8,128)(2,1)S(1)} %copy-done.3, ...), custom_call_target="tpu_custom_call" | custom-call | flops 7650410496 | bytes 13107200 | tf_op jit(solution)/shard_map/pallas_call | solution.py:130
  182.4 12.1 %shard_map.75 = (bf16[512,1024]{1,0:T(8,128)(2,1)S(1)}, bf16[512,1024]{1,0:T(8,128)(2,1)S(1)}) custom-call(bf16[1024,2048]{1,0:T(8,128)(2,1)} %shard_map.73.theta_ref, bf16[3072,1024]{1,0:T(8,128)(2,1)} %get-tuple-element.150.left_ref, bf16[384,384]{1,0:T(8,128)(2,1)S(1)} %copy-done.8, bf16[1024,1536]{1,0:T(8,128)(2,1)S(1)} %copy-done.3, ...), custom_call_target="tpu_custom_call" | custom-call | flops 7650410496 | bytes 13107200 | tf_op jit(solution)/shard_map/pallas_call | solution.py:130
  196.7 12.5 %shard_map.76 = (bf16[512,1024]{1,0:T(8,128)(2,1)S(1)}, bf16[512,1024]{1,0:T(8,128)(2,1)S(1)}) custom-call(bf16[1024,2048]{1,0:T(8,128)(2,1)} %shard_map.73.theta_ref, bf16[3072,1024]{1,0:T(8,128)(2,1)} %get-tuple-element.150.left_ref, bf16[384,384]{1,0:T(8,128)(2,1)S(1)} %copy-done.8, bf16[1024,1536]{1,0:T(8,128)(2,1)S(1)} %copy-done.3, ...), custom_call_target="tpu_custom_call" | custom-call | flops 7650410496 | bytes 13107200 | tf_op jit(solution)/shard_map/pallas_call | solution.py:130
  211.5 12.1 %shard_map.77 = (bf16[512,1024]{1,0:T(8,128)(2,1)S(1)}, bf16[512,1024]{1,0:T(8,128)(2,1)S(1)}) custom-call(bf16[1024,2048]{1,0:T(8,128)(2,1)} %shard_map.73.theta_ref, bf16[3072,1024]{1,0:T(8,128)(2,1)} %get-tuple-element.150.left_ref, bf16[384,384]{1,0:T(8,128)(2,1)S(1)} %copy-done.8, bf16[1024,1536]{1,0:T(8,128)(2,1)S(1)} %copy-done.3, ...), custom_call_target="tpu_custom_call" | custom-call | flops 7650410496 | bytes 13107200 | tf_op jit(solution)/shard_map/pallas_call | solution.py:130
  228.5 14.0 %shard_map.78 = (bf16[3072,2048]{1,0:T(8,128)(2,1)}, bf16[3072,2048]{1,0:T(8,128)(2,1)}) custom-call(bf16[256,1024]{1,0:T(8,128)(2,1)S(1)} %add_convert_fusion.19.refs_0_, bf16[256,1024]{1,0:T(8,128)(2,1)S(1)} %collective-permute-done.29.refs_1_, bf16[256,1024]{1,0:T(8,128)(2,1)S(1)} %collective-permute-done.32.refs_2_, ...), custom_call_target="tpu_custom_call" | custom-call | flops 8858370048 | bytes 14680064 | tf_op jit(solution)/shard_map/pallas_call | solution.py:194
  242.6 7.6 %collective-permute-done.30 = bf16[256,1024]{1,0:T(8,128)(2,1)S(1)} collective-permute-done((bf16[256,1024]{1,0:T(8,128)(2,1)S(1)}, bf16[256,1024]{1,0:T(8,128)(2,1)S(1)}, u32[]{:S(2)}, u32[]{:S(2)}) %collective-permute-start.30) | collective-permute-done | bytes 524320 | tf_op jit(solution)/shard_map/ppermute | solution.py:309
  253.1 14.0 %shard_map.79 = (bf16[3072,2048]{1,0:T(8,128)(2,1)}, bf16[3072,2048]{1,0:T(8,128)(2,1)}) custom-call(bf16[256,1024]{1,0:T(8,128)(2,1)S(1)} %add_convert_fusion.18.refs_0_, bf16[256,1024]{1,0:T(8,128)(2,1)S(1)} %collective-permute-done.35.refs_1_, ...), custom_call_target="tpu_custom_call", output_to_operand_aliasing={{0}: (7, {}), {1}: (8, {})} | custom-call | flops 8858370048 | bytes 14680064 | tf_op jit(solution)/shard_map/pallas_call | solution.py:194
  267.1 9.0 %collective-permute-done.34 = bf16[256,1024]{1,0:T(8,128)(2,1)S(1)} collective-permute-done((bf16[256,1024]{1,0:T(8,128)(2,1)S(1)}, bf16[256,1024]{1,0:T(8,128)(2,1)S(1)}, u32[]{:S(2)}, u32[]{:S(2)}) %collective-permute-start.34) | collective-permute-done | bytes 524320 | tf_op jit(solution)/shard_map/ppermute | solution.py:309
  278.5 14.0 %shard_map.80 = (bf16[3072,2048]{1,0:T(8,128)(2,1)}, bf16[3072,2048]{1,0:T(8,128)(2,1)}) custom-call(bf16[256,1024]{1,0:T(8,128)(2,1)S(1)} %add_convert_fusion.17.refs_0_, bf16[256,1024]{1,0:T(8,128)(2,1)S(1)} %collective-permute-done.39.refs_1_, ...), custom_call_target="tpu_custom_call", output_to_operand_aliasing={{0}: (7, {}), {1}: (8, {})} | custom-call | flops 8858370048 | bytes 14680064 | tf_op jit(solution)/shard_map/pallas_call | solution.py:194
  295.8 14.5 %shard_map.81 = (bf16[3072,2048]{1,0:T(8,128)(2,1)}, bf16[3072,2048]{1,0:T(8,128)(2,1)}) custom-call(bf16[256,1024]{1,0:T(8,128)(2,1)} %add_convert_fusion.16.refs_0_, bf16[256,1024]{1,0:T(8,128)(2,1)} %collective-permute-done.38.refs_1_, bf16[256,1024]{1,0:T(8,128)(2,1)} %collective-permute-done.42.refs_2_, ...), custom_call_target="tpu_custom_call", output_to_operand_aliasing={{0}: (7, {}), {1}: (8, {})} | custom-call | flops 8858370048 | bytes 14680064 | tf_op jit(solution)/shard_map/pallas_call | solution.py:194
  310.3 10.7 %shard_map.82 = bf16[1024,1024]{1,0:T(8,128)(2,1)S(1)} custom-call(bf16[1024,3072]{1,0:T(8,128)(2,1)} %get-tuple-element.151.left_ref, bf16[3072,2048]{1,0:T(8,128)(2,1)} %get-tuple-element.252.back_ref), custom_call_target="tpu_custom_call" | custom-call | flops 6442450944 | bytes 14680064 | tf_op jit(solution)/shard_map/pallas_call | solution.py:227
  323.1 10.8 %shard_map.83 = bf16[1024,1024]{1,0:T(8,128)(2,1)S(1)} custom-call(bf16[1024,3072]{1,0:T(8,128)(2,1)} %get-tuple-element.151.left_ref, bf16[3072,2048]{1,0:T(8,128)(2,1)} %get-tuple-element.252.back_ref), custom_call_target="tpu_custom_call" | custom-call | flops 6442450944 | bytes 14680064 | tf_op jit(solution)/shard_map/pallas_call | solution.py:227
  343.4 10.7 %shard_map.84 = bf16[1024,1024]{1,0:T(8,128)(2,1)S(1)} custom-call(bf16[1024,3072]{1,0:T(8,128)(2,1)} %get-tuple-element.151.left_ref, bf16[3072,2048]{1,0:T(8,128)(2,1)} %get-tuple-element.271.back_ref), custom_call_target="tpu_custom_call" | custom-call | flops 6442450944 | bytes 14680064 | tf_op jit(solution)/shard_map/pallas_call | solution.py:227
  367.5 11.0 %shard_map.85 = bf16[1024,1024]{1,0:T(8,128)(2,1)S(1)} custom-call(bf16[1024,3072]{1,0:T(8,128)(2,1)} %get-tuple-element.151.left_ref, bf16[3072,2048]{1,0:T(8,128)(2,1)} %get-tuple-element.271.back_ref), custom_call_target="tpu_custom_call" | custom-call | flops 6442450944 | bytes 14680064 | tf_op jit(solution)/shard_map/pallas_call | solution.py:227
  390.5 16.3 %collective-permute-done.62 = bf16[256,1024]{1,0:T(8,128)(2,1)S(1)} collective-permute-done((bf16[256,1024]{1,0:T(8,128)(2,1)S(1)}, bf16[256,1024]{1,0:T(8,128)(2,1)S(1)}, u32[]{:S(2)}, u32[]{:S(2)}) %collective-permute-start.62) | collective-permute-done | bytes 524320 | tf_op jit(solution)/shard_map/ppermute | solution.py:299
  416.6 12.7 %collective-permute-done.58 = bf16[256,1024]{1,0:T(8,128)(2,1)S(1)} collective-permute-done((bf16[256,1024]{1,0:T(8,128)(2,1)S(1)}, bf16[256,1024]{1,0:T(8,128)(2,1)S(1)}, u32[]{:S(2)}, u32[]{:S(2)}) %collective-permute-start.58) | collective-permute-done | bytes 524320 | tf_op jit(solution)/shard_map/ppermute | solution.py:299
  435.6 5.0 %collective-permute-done.64 = bf16[256,1024]{1,0:T(8,128)(2,1)S(1)} collective-permute-done((bf16[256,1024]{1,0:T(8,128)(2,1)S(1)}, bf16[256,1024]{1,0:T(8,128)(2,1)S(1)}, u32[]{:S(2)}, u32[]{:S(2)}) %collective-permute-start.64) | collective-permute-done | bytes 524320 | tf_op jit(solution)/shard_map/ppermute | solution.py:299
  451.8 7.1 %collective-permute-done.61 = bf16[256,1024]{1,0:T(8,128)(2,1)S(1)} collective-permute-done((bf16[256,1024]{1,0:T(8,128)(2,1)S(1)}, bf16[256,1024]{1,0:T(8,128)(2,1)S(1)}, u32[]{:S(2)}, u32[]{:S(2)}) %collective-permute-start.61) | collective-permute-done | bytes 524320 | tf_op jit(solution)/shard_map/ppermute | solution.py:300
  462.4 5.9 %collective-permute-done.67 = bf16[256,1024]{1,0:T(8,128)(2,1)S(1)} collective-permute-done((bf16[256,1024]{1,0:T(8,128)(2,1)S(1)}, bf16[256,1024]{1,0:T(8,128)(2,1)S(1)}, u32[]{:S(2)}, u32[]{:S(2)}) %collective-permute-start.67) | collective-permute-done | bytes 524320 | tf_op jit(solution)/shard_map/ppermute | solution.py:300
  (220 shorter events, 186.1 us)
Async XLA Ops:
  9.5 28.9 %collective-permute-start = (bf16[256,1024]{1,0:T(8,128)(2,1)S(1)}, bf16[256,1024]{1,0:T(8,128)(2,1)}, u32[]{:S(2)}, u32[]{:S(2)}) collective-permute-start(bf16[256,1024]{1,0:T(8,128)(2,1)S(1)} %bitcast.45), channel_id=1, source_target_pairs={{0,4},{4,8},{8,12},{1,5},{5,9},{9,13},{2,6},{6,10},{10,14},{3,7},{... | collective-permute-start | bytes 1572872 | tf_op jit(solution)/shard_map/ppermute | solution.py:280
  12.9 25.5 %collective-permute-start.1 = (bf16[256,1024]{1,0:T(8,128)(2,1)S(1)}, bf16[256,1024]{1,0:T(8,128)(2,1)}, u32[]{:S(2)}, u32[]{:S(2)}) collective-permute-start(bf16[256,1024]{1,0:T(8,128)(2,1)S(1)} %bitcast.46), channel_id=1, source_target_pairs={{4,0},{8,4},{12,8},{5,1},{9,5},{13,9},{6,2},{10,6},{14,10},{7,3},{... | collective-permute-start | bytes 1572872 | tf_op jit(solution)/shard_map/ppermute | solution.py:281
  20.2 31.2 %collective-permute-start.10 = (bf16[256,1024]{1,0:T(8,128)(2,1)S(1)}, bf16[256,1024]{1,0:T(8,128)(2,1)}, u32[]{:S(2)}, u32[]{:S(2)}) collective-permute-start(bf16[256,1024]{1,0:T(8,128)(2,1)S(1)} %collective-permute-done.4.refs_9_), channel_id=1, source_target_pairs={{4,8},{8,12},{5,9},{9,13},{6,10},{10,14},{7,11},{11,15},{20,24},{2... | collective-permute-start | bytes 1572872 | tf_op jit(solution)/shard_map/ppermute | solution.py:280
  24.4 28.4 %collective-permute-start.12 = (bf16[256,1024]{1,0:T(8,128)(2,1)}, bf16[256,1024]{1,0:T(8,128)(2,1)}, u32[]{:S(2)}, u32[]{:S(2)}) collective-permute-start(bf16[256,1024]{1,0:T(8,128)(2,1)} %collective-permute-done.5.refs_11_), channel_id=1, source_target_pairs={{4,0},{8,4},{5,1},{9,5},{6,2},{10,6},{7,3},{11,7},{20,16},{24,20},... | collective-permute-start | bytes 1572872 | tf_op jit(solution)/shard_map/ppermute | solution.py:281
  69.1 33.1 %collective-permute-start.16 = (bf16[256,1024]{1,0:T(8,128)(2,1)}, bf16[256,1024]{1,0:T(8,128)(2,1)}, u32[]{:S(2)}, u32[]{:S(2)}) collective-permute-start(bf16[256,1024]{1,0:T(8,128)(2,1)} %bitcast.34.refs_10_), channel_id=1, source_target_pairs={{0,4},{4,8},{8,12},{1,5},{5,9},{9,13},{2,6},{6,10},{10,14},{3,7},{... | collective-permute-start | bytes 1572872 | tf_op jit(solution)/shard_map/ppermute | solution.py:280
  71.0 31.1 %collective-permute-start.17 = (bf16[256,1024]{1,0:T(8,128)(2,1)}, bf16[256,1024]{1,0:T(8,128)(2,1)}, u32[]{:S(2)}, u32[]{:S(2)}) collective-permute-start(bf16[256,1024]{1,0:T(8,128)(2,1)} %bitcast.34.refs_10_), channel_id=1, source_target_pairs={{4,0},{8,4},{12,8},{5,1},{9,5},{13,9},{6,2},{10,6},{14,10},{7,3},{... | collective-permute-start | bytes 1572872 | tf_op jit(solution)/shard_map/ppermute | solution.py:281
  80.3 25.1 %collective-permute-start.8 = (bf16[256,1024]{1,0:T(8,128)(2,1)}, bf16[256,1024]{1,0:T(8,128)(2,1)}, u32[]{:S(2)}, u32[]{:S(2)}) collective-permute-start(bf16[256,1024]{1,0:T(8,128)(2,1)} %bitcast.37.refs_3_), channel_id=1, source_target_pairs={{0,4},{4,8},{8,12},{1,5},{5,9},{9,13},{2,6},{6,10},{10,14},{3,7},{... | collective-permute-start | bytes 1572872 | tf_op jit(solution)/shard_map/ppermute | solution.py:280
  102.2 30.9 %collective-permute-start.20 = (bf16[256,1024]{1,0:T(8,128)(2,1)}, bf16[256,1024]{1,0:T(8,128)(2,1)S(1)}, u32[]{:S(2)}, u32[]{:S(2)}) collective-permute-start(bf16[256,1024]{1,0:T(8,128)(2,1)} %collective-permute-done.16.refs_9_), channel_id=1, source_target_pairs={{4,8},{8,12},{5,9},{9,13},{6,10},{10,14},{7,11},{11,15},{20,24},{2... | collective-permute-start | bytes 1572872 | tf_op jit(solution)/shard_map/ppermute | solution.py:280
  103.5 29.6 %collective-permute-start.21 = (bf16[256,1024]{1,0:T(8,128)(2,1)}, bf16[256,1024]{1,0:T(8,128)(2,1)S(1)}, u32[]{:S(2)}, u32[]{:S(2)}) collective-permute-start(bf16[256,1024]{1,0:T(8,128)(2,1)} %collective-permute-done.17.refs_11_), channel_id=1, source_target_pairs={{4,0},{8,4},{5,1},{9,5},{6,2},{10,6},{7,3},{11,7},{20,16},{24,20},... | collective-permute-start | bytes 1572872 | tf_op jit(solution)/shard_map/ppermute | solution.py:281
  105.5 27.7 %collective-permute-start.14 = (bf16[256,1024]{1,0:T(8,128)(2,1)}, bf16[256,1024]{1,0:T(8,128)(2,1)S(1)}, u32[]{:S(2)}, u32[]{:S(2)}) collective-permute-start(bf16[256,1024]{1,0:T(8,128)(2,1)} %collective-permute-done.8.refs_2_), channel_id=1, source_target_pairs={{4,8},{8,12},{5,9},{9,13},{6,10},{10,14},{7,11},{11,15},{20,24},{2... | collective-permute-start | bytes 1572872 | tf_op jit(solution)/shard_map/ppermute | solution.py:280
  133.1 26.3 %collective-permute-start.22 = (bf16[256,1024]{1,0:T(8,128)(2,1)S(1)}, bf16[256,1024]{1,0:T(8,128)(2,1)S(1)}, u32[]{:S(2)}, u32[]{:S(2)}) collective-permute-start(bf16[256,1024]{1,0:T(8,128)(2,1)S(1)} %collective-permute-done.20.refs_8_), channel_id=1, source_target_pairs={{8,12},{9,13},{10,14},{11,15},{24,28},{25,29},{26,30},{27,31}} | collective-permute-start | bytes 1572872 | tf_op jit(solution)/shard_map/ppermute | solution.py:280
  133.8 25.6 %collective-permute-start.23 = (bf16[256,1024]{1,0:T(8,128)(2,1)S(1)}, bf16[256,1024]{1,0:T(8,128)(2,1)S(1)}, u32[]{:S(2)}, u32[]{:S(2)}) collective-permute-start(bf16[256,1024]{1,0:T(8,128)(2,1)S(1)} %collective-permute-done.21.refs_12_), channel_id=1, source_target_pairs={{4,0},{5,1},{6,2},{7,3},{20,16},{21,17},{22,18},{23,19}} | collective-permute-start | bytes 1572872 | tf_op jit(solution)/shard_map/ppermute | solution.py:281
  135.9 25.3 %collective-permute-start.19 = (bf16[256,1024]{1,0:T(8,128)(2,1)S(1)}, bf16[256,1024]{1,0:T(8,128)(2,1)}, u32[]{:S(2)}, u32[]{:S(2)}) collective-permute-start(bf16[256,1024]{1,0:T(8,128)(2,1)S(1)} %collective-permute-done.15.refs_5_), channel_id=1, source_target_pairs={{4,0},{5,1},{6,2},{7,3},{20,16},{21,17},{22,18},{23,19}} | collective-permute-start | bytes 1572872 | tf_op jit(solution)/shard_map/ppermute | solution.py:281
  195.0 32.8 %collective-permute-start.32 = (bf16[256,1024]{1,0:T(8,128)(2,1)S(1)}, bf16[256,1024]{1,0:T(8,128)(2,1)S(1)}, u32[]{:S(2)}, u32[]{:S(2)}) collective-permute-start(bf16[256,1024]{1,0:T(8,128)(2,1)S(1)} %add_convert_fusion.19.refs_0_), channel_id=1, source_target_pairs={{0,2},{2,0},{1,3},{3,1},{4,6},{6,4},{5,7},{7,5},{8,10},{10,8},{9,1... | collective-permute-start | bytes 1572872 | tf_op jit(solution)/shard_map/ppermute | solution.py:309
  223.6 28.5 %collective-permute-start.31 = (bf16[512,1024]{1,0:T(8,128)(2,1)S(1)}, bf16[512,1024]{1,0:T(8,128)(2,1)S(1)}, u32[]{:S(2)}, u32[]{:S(2)}) collective-permute-start(bf16[512,1024]{1,0:T(8,128)(2,1)S(1)} %get-tuple-element.218), channel_id=1, source_target_pairs={{0,2},{2,0},{1,3},{3,1},{4,6},{6,4},{5,7},{7,5},{8,10},{10,8},{9,1... | collective-permute-start | bytes 3145736 | tf_op jit(solution)/shard_map/ppermute | solution.py:309
  224.5 28.6 %collective-permute-start.36 = (bf16[256,1024]{1,0:T(8,128)(2,1)S(1)}, bf16[256,1024]{1,0:T(8,128)(2,1)S(1)}, u32[]{:S(2)}, u32[]{:S(2)}) collective-permute-start(bf16[256,1024]{1,0:T(8,128)(2,1)S(1)} %add_convert_fusion.18.refs_0_), channel_id=1, source_target_pairs={{0,2},{2,0},{1,3},{3,1},{4,6},{6,4},{5,7},{7,5},{8,10},{10,8},{9,1... | collective-permute-start | bytes 1572872 | tf_op jit(solution)/shard_map/ppermute | solution.py:309
  250.4 28.1 %collective-permute-start.40 = (bf16[256,1024]{1,0:T(8,128)(2,1)S(1)}, bf16[256,1024]{1,0:T(8,128)(2,1)S(1)}, u32[]{:S(2)}, u32[]{:S(2)}) collective-permute-start(bf16[256,1024]{1,0:T(8,128)(2,1)S(1)} %add_convert_fusion.17.refs_0_), channel_id=1, source_target_pairs={{0,2},{2,0},{1,3},{3,1},{4,6},{6,4},{5,7},{7,5},{8,10},{10,8},{9,1... | collective-permute-start | bytes 1572872 | tf_op jit(solution)/shard_map/ppermute | solution.py:309
  363.0 47.4 %collective-permute-start.48 = (bf16[256,1024]{1,0:T(8,128)(2,1)S(1)}, bf16[256,1024]{1,0:T(8,128)(2,1)S(1)}, u32[]{:S(2)}, u32[]{:S(2)}) collective-permute-start(bf16[256,1024]{1,0:T(8,128)(2,1)S(1)} %get-tuple-element.263), channel_id=1, source_target_pairs={{0,4},{4,8},{8,12},{1,5},{5,9},{9,13},{2,6},{6,10},{10,14},{3,7},{... | collective-permute-start | bytes 1572872 | tf_op jit(solution)/shard_map/ppermute | solution.py:299
  378.6 28.2 %collective-permute-start.62 = (bf16[256,1024]{1,0:T(8,128)(2,1)S(1)}, bf16[256,1024]{1,0:T(8,128)(2,1)S(1)}, u32[]{:S(2)}, u32[]{:S(2)}) collective-permute-start(bf16[256,1024]{1,0:T(8,128)(2,1)S(1)} %get-tuple-element.284), channel_id=1, source_target_pairs={{0,4},{1,5},{2,6},{3,7},{16,20},{17,21},{18,22},{19,23}} | collective-permute-start | bytes 1572872 | tf_op jit(solution)/shard_map/ppermute | solution.py:299
  379.9 28.8 %collective-permute-start.63 = (bf16[256,1024]{1,0:T(8,128)(2,1)S(1)}, bf16[256,1024]{1,0:T(8,128)(2,1)S(1)}, u32[]{:S(2)}, u32[]{:S(2)}) collective-permute-start(bf16[256,1024]{1,0:T(8,128)(2,1)S(1)} %get-tuple-element.285), channel_id=1, source_target_pairs={{12,8},{13,9},{14,10},{15,11},{28,24},{29,25},{30,26},{31,27}} | collective-permute-start | bytes 1572872 | tf_op jit(solution)/shard_map/ppermute | solution.py:300
  384.4 30.6 %collective-permute-start.49 = (bf16[256,1024]{1,0:T(8,128)(2,1)S(1)}, bf16[256,1024]{1,0:T(8,128)(2,1)S(1)}, u32[]{:S(2)}, u32[]{:S(2)}) collective-permute-start(bf16[256,1024]{1,0:T(8,128)(2,1)S(1)} %get-tuple-element.264), channel_id=1, source_target_pairs={{12,8},{8,4},{4,0},{13,9},{9,5},{5,1},{14,10},{10,6},{6,2},{15,11}... | collective-permute-start | bytes 1572872 | tf_op jit(solution)/shard_map/ppermute | solution.py:300
  386.3 60.5 %collective-permute-start.54 = (bf16[256,1024]{1,0:T(8,128)(2,1)S(1)}, bf16[256,1024]{1,0:T(8,128)(2,1)S(1)}, u32[]{:S(2)}, u32[]{:S(2)}) collective-permute-start(bf16[256,1024]{1,0:T(8,128)(2,1)S(1)} %get-tuple-element.274), channel_id=1, source_target_pairs={{0,4},{4,8},{8,12},{1,5},{5,9},{9,13},{2,6},{6,10},{10,14},{3,7},{... | collective-permute-start | bytes 1572872 | tf_op jit(solution)/shard_map/ppermute | solution.py:299
  410.4 30.2 %collective-permute-start.64 = (bf16[256,1024]{1,0:T(8,128)(2,1)S(1)}, bf16[256,1024]{1,0:T(8,128)(2,1)S(1)}, u32[]{:S(2)}, u32[]{:S(2)}) collective-permute-start(bf16[256,1024]{1,0:T(8,128)(2,1)S(1)} %get-tuple-element.288), channel_id=1, source_target_pairs={{0,4},{4,8},{1,5},{5,9},{2,6},{6,10},{3,7},{7,11},{16,20},{20,24},... | collective-permute-start | bytes 1572872 | tf_op jit(solution)/shard_map/ppermute | solution.py:299
  415.0 27.5 %collective-permute-start.65 = (bf16[256,1024]{1,0:T(8,128)(2,1)S(1)}, bf16[256,1024]{1,0:T(8,128)(2,1)S(1)}, u32[]{:S(2)}, u32[]{:S(2)}) collective-permute-start(bf16[256,1024]{1,0:T(8,128)(2,1)S(1)} %get-tuple-element.289), channel_id=1, source_target_pairs={{12,8},{8,4},{13,9},{9,5},{14,10},{10,6},{15,11},{11,7},{28,24},{2... | collective-permute-start | bytes 1572872 | tf_op jit(solution)/shard_map/ppermute | solution.py:300
  (65 other events, 1167.9 us)

commit v9 on v8

--- a/solution.py
+++ b/solution.py
@@ -223,7 +223,7 @@
 
 def last(left_t, backs, chunk, n_chunks):
     columns = backs.shape[1] // n_chunks
-    steps = 2
+    steps = 4
     return pl.pallas_call(
         last_kernel,
         grid=(steps,),

time: 480 us -> 479 us (level)
  no operation moved by 1% of the time
where the time goes in v9:
time: 479 us; the launch traced here: 470 us
  Pallas kernels  222 us (46%)
  starting transfers between devices  128 us (27%)
  waiting for transfers between devices  87 us (18%)
  other arithmetic  15.9 us (3%)
  local copies, waits for them, and re-layouts  14.4 us (3%)
    pallas_call x6, Pallas kernels, fore(): pl.pallas_call(functools.partial(fore_kernel, channels, lanes, n_outs), g...  91.4 us
    pallas_call x4, Pallas kernels, back(): pl.pallas_call(functools.partial(back_kernel, channels, len(parts), count...  56.7 us
    ppermute x12, waiting for transfers between devices, scatter_round(): up = lax.ppermute(pair[0], 'row', [(r, r + 1) for r in range(t)])  44.4 us
    pallas_call x4, Pallas kernels, last(): pl.pallas_call(last_kernel, grid=(steps,), in_specs=[pl.BlockSpec(left_t....  42.8 us
    ppermute x12, starting transfers between devices, scatter_round(): up = lax.ppermute(pair[0], 'row', [(r, r + 1) for r in range(t)])  37.3 us
    ppermute x12, starting transfers between devices, gather_round(): lax.ppermute(pair[1], 'row', [(r, r - 1) for r in range(1, n_rows - t + 1)])  32.8 us
    ppermute x12, starting transfers between devices, gather_round(): lax.ppermute(pair[0], 'row', [(r, r + 1) for r in range(t - 1, n_rows - 1)])  30.2 us
    ppermute x20, waiting for transfers between devices, swapped(): return lax.ppermute(block, axis, [(0, 1), (1, 0)])  20 us
  transfers between devices with their start and end apart: 68, of which 19 were waited for; matrix products, arithmetic and copies ran while one was open for 5% of the time, Pallas kernels for 38%

profile of v9, /device:TPU:8, one launch (start us, length us, event | category | flops | bytes accessed | tf_op | source)
XLA Modules:
  0.0 470.3 jit_solution(14777717545070384788)
XLA Ops:
  26.4 12.0 %shard_map.68 = (bf16[3072,1024]{1,0:T(8,128)(2,1)}, bf16[1024,3072]{1,0:T(8,128)(2,1)}) custom-call(bf16[12,256,1024]{2,1,0:T(8,128)(2,1)} %bitcast.57, bf16[384,384]{1,0:T(8,128)(2,1)} %fusion.9.order_ref), custom_call_target="tpu_custom_call" | custom-call | flops 4831838208 | bytes 18874368 | tf_op jit(solution)/shard_map/pallas_call | solution.py:50
  38.4 5.5 %collective-permute-start.2 = (bf16[256,1024]{1,0:T(8,128)(2,1)}, bf16[256,1024]{1,0:T(8,128)(2,1)}, u32[]{:S(2)}, u32[]{:S(2)}) collective-permute-start(bf16[256,1024]{1,0:T(8,128)(2,1)} %collective-permute-done.refs_2_), channel_id=1, source_target_pairs={{4,8},{8,12},{5,9},{9,13},{6,10},{10,14},{7,11},{11,15},{20,24},{2... | collective-permute-start | bytes 1572872 | tf_op jit(solution)/shard_map/ppermute | solution.py:280
  87.9 9.8 %shard_map.69 = (bf16[1024,1536]{1,0:T(8,128)(2,1)}, bf16[1024,1536]{1,0:T(8,128)(2,1)}) custom-call(bf16[12,1024,256]{2,1,0:T(8,128)(2,1)} %bitcast.40), custom_call_target="tpu_custom_call" | custom-call | bytes 12582912 | tf_op jit(solution)/shard_map/pallas_call | solution.py:84
  111.6 21.5 %shard_map.71.refs_0_ = f32[1024,2048]{1,0:T(8,128)} custom-call(bf16[1024,2048]{1,0:T(8,128)(2,1)} %shard_map.70.theta_ref, bf16[3072,1024]{1,0:T(8,128)(2,1)} %get-tuple-element.150.left_ref, bf16[384,384]{1,0:T(8,128)(2,1)S(1)} %copy-done.7, bf16[1024,1536]{1,0:T(8,128)(2,1)S(1)} %copy-done.2), custom_call_target="tpu_custom_call" | custom-call | flops 15300820992 | bytes 18874368 | tf_op jit(solution)/shard_map/pallas_call | solution.py:130
  137.9 21.4 %shard_map.72.refs_0_ = f32[1024,2048]{1,0:T(8,128)} custom-call(bf16[1024,2048]{1,0:T(8,128)(2,1)} %shard_map.70.theta_ref, bf16[3072,1024]{1,0:T(8,128)(2,1)} %get-tuple-element.150.left_ref, bf16[384,384]{1,0:T(8,128)(2,1)S(1)} %copy-done.7, bf16[1024,1536]{1,0:T(8,128)(2,1)S(1)} %copy-done.2), custom_call_target="tpu_custom_call" | custom-call | flops 15300820992 | bytes 18874368 | tf_op jit(solution)/shard_map/pallas_call | solution.py:130
  165.5 12.1 %shard_map.74 = (bf16[512,1024]{1,0:T(8,128)(2,1)S(1)}, bf16[512,1024]{1,0:T(8,128)(2,1)S(1)}) custom-call(bf16[1024,2048]{1,0:T(8,128)(2,1)} %shard_map.73.theta_ref, bf16[3072,1024]{1,0:T(8,128)(2,1)} %get-tuple-element.150.left_ref, bf16[384,384]{1,0:T(8,128)(2,1)S(1)} %copy-done.8, bf16[1024,1536]{1,0:T(8,128)(2,1)S(1)} %copy-done.3, ...), custom_call_target="tpu_custom_call" | custom-call | flops 7650410496 | bytes 13107200 | tf_op jit(solution)/shard_map/pallas_call | solution.py:130
  182.3 12.1 %shard_map.75 = (bf16[512,1024]{1,0:T(8,128)(2,1)S(1)}, bf16[512,1024]{1,0:T(8,128)(2,1)S(1)}) custom-call(bf16[1024,2048]{1,0:T(8,128)(2,1)} %shard_map.73.theta_ref, bf16[3072,1024]{1,0:T(8,128)(2,1)} %get-tuple-element.150.left_ref, bf16[384,384]{1,0:T(8,128)(2,1)S(1)} %copy-done.8, bf16[1024,1536]{1,0:T(8,128)(2,1)S(1)} %copy-done.3, ...), custom_call_target="tpu_custom_call" | custom-call | flops 7650410496 | bytes 13107200 | tf_op jit(solution)/shard_map/pallas_call | solution.py:130
  196.6 12.3 %shard_map.76 = (bf16[512,1024]{1,0:T(8,128)(2,1)S(1)}, bf16[512,1024]{1,0:T(8,128)(2,1)S(1)}) custom-call(bf16[1024,2048]{1,0:T(8,128)(2,1)} %shard_map.73.theta_ref, bf16[3072,1024]{1,0:T(8,128)(2,1)} %get-tuple-element.150.left_ref, bf16[384,384]{1,0:T(8,128)(2,1)S(1)} %copy-done.8, bf16[1024,1536]{1,0:T(8,128)(2,1)S(1)} %copy-done.3, ...), custom_call_target="tpu_custom_call" | custom-call | flops 7650410496 | bytes 13107200 | tf_op jit(solution)/shard_map/pallas_call | solution.py:130
  211.4 12.1 %shard_map.77 = (bf16[512,1024]{1,0:T(8,128)(2,1)S(1)}, bf16[512,1024]{1,0:T(8,128)(2,1)S(1)}) custom-call(bf16[1024,2048]{1,0:T(8,128)(2,1)} %shard_map.73.theta_ref, bf16[3072,1024]{1,0:T(8,128)(2,1)} %get-tuple-element.150.left_ref, bf16[384,384]{1,0:T(8,128)(2,1)S(1)} %copy-done.8, bf16[1024,1536]{1,0:T(8,128)(2,1)S(1)} %copy-done.3, ...), custom_call_target="tpu_custom_call" | custom-call | flops 7650410496 | bytes 13107200 | tf_op jit(solution)/shard_map/pallas_call | solution.py:130
  228.5 14.3 %shard_map.78 = (bf16[3072,2048]{1,0:T(8,128)(2,1)}, bf16[3072,2048]{1,0:T(8,128)(2,1)}) custom-call(bf16[256,1024]{1,0:T(8,128)(2,1)S(1)} %add_convert_fusion.19.refs_0_, bf16[256,1024]{1,0:T(8,128)(2,1)S(1)} %collective-permute-done.29.refs_1_, bf16[256,1024]{1,0:T(8,128)(2,1)S(1)} %collective-permute-done.32.refs_2_, ...), custom_call_target="tpu_custom_call" | custom-call | flops 8858370048 | bytes 14680064 | tf_op jit(solution)/shard_map/pallas_call | solution.py:194
  242.8 7.3 %collective-permute-done.30 = bf16[256,1024]{1,0:T(8,128)(2,1)S(1)} collective-permute-done((bf16[256,1024]{1,0:T(8,128)(2,1)S(1)}, bf16[256,1024]{1,0:T(8,128)(2,1)S(1)}, u32[]{:S(2)}, u32[]{:S(2)}) %collective-permute-start.30) | collective-permute-done | bytes 524320 | tf_op jit(solution)/shard_map/ppermute | solution.py:309
  253.1 14.0 %shard_map.79 = (bf16[3072,2048]{1,0:T(8,128)(2,1)}, bf16[3072,2048]{1,0:T(8,128)(2,1)}) custom-call(bf16[256,1024]{1,0:T(8,128)(2,1)S(1)} %add_convert_fusion.18.refs_0_, bf16[256,1024]{1,0:T(8,128)(2,1)S(1)} %collective-permute-done.35.refs_1_, ...), custom_call_target="tpu_custom_call", output_to_operand_aliasing={{0}: (7, {}), {1}: (8, {})} | custom-call | flops 8858370048 | bytes 14680064 | tf_op jit(solution)/shard_map/pallas_call | solution.py:194
  267.0 9.0 %collective-permute-done.34 = bf16[256,1024]{1,0:T(8,128)(2,1)S(1)} collective-permute-done((bf16[256,1024]{1,0:T(8,128)(2,1)S(1)}, bf16[256,1024]{1,0:T(8,128)(2,1)S(1)}, u32[]{:S(2)}, u32[]{:S(2)}) %collective-permute-start.34) | collective-permute-done | bytes 524320 | tf_op jit(solution)/shard_map/ppermute | solution.py:309
  278.5 14.0 %shard_map.80 = (bf16[3072,2048]{1,0:T(8,128)(2,1)}, bf16[3072,2048]{1,0:T(8,128)(2,1)}) custom-call(bf16[256,1024]{1,0:T(8,128)(2,1)S(1)} %add_convert_fusion.17.refs_0_, bf16[256,1024]{1,0:T(8,128)(2,1)S(1)} %collective-permute-done.39.refs_1_, ...), custom_call_target="tpu_custom_call", output_to_operand_aliasing={{0}: (7, {}), {1}: (8, {})} | custom-call | flops 8858370048 | bytes 14680064 | tf_op jit(solution)/shard_map/pallas_call | solution.py:194
  295.7 14.5 %shard_map.81 = (bf16[3072,2048]{1,0:T(8,128)(2,1)}, bf16[3072,2048]{1,0:T(8,128)(2,1)}) custom-call(bf16[256,1024]{1,0:T(8,128)(2,1)} %add_convert_fusion.16.refs_0_, bf16[256,1024]{1,0:T(8,128)(2,1)} %collective-permute-done.38.refs_1_, bf16[256,1024]{1,0:T(8,128)(2,1)} %collective-permute-done.42.refs_2_, ...), custom_call_target="tpu_custom_call", output_to_operand_aliasing={{0}: (7, {}), {1}: (8, {})} | custom-call | flops 8858370048 | bytes 14680064 | tf_op jit(solution)/shard_map/pallas_call | solution.py:194
  310.2 10.7 %shard_map.82 = bf16[1024,1024]{1,0:T(8,128)(2,1)S(1)} custom-call(bf16[1024,3072]{1,0:T(8,128)(2,1)} %get-tuple-element.151.left_ref, bf16[3072,2048]{1,0:T(8,128)(2,1)} %get-tuple-element.252.back_ref), custom_call_target="tpu_custom_call" | custom-call | flops 6442450944 | bytes 14680064 | tf_op jit(solution)/shard_map/pallas_call | solution.py:227
  323.0 10.7 %shard_map.83 = bf16[1024,1024]{1,0:T(8,128)(2,1)S(1)} custom-call(bf16[1024,3072]{1,0:T(8,128)(2,1)} %get-tuple-element.151.left_ref, bf16[3072,2048]{1,0:T(8,128)(2,1)} %get-tuple-element.252.back_ref), custom_call_target="tpu_custom_call" | custom-call | flops 6442450944 | bytes 14680064 | tf_op jit(solution)/shard_map/pallas_call | solution.py:227
  343.3 10.7 %shard_map.84 = bf16[1024,1024]{1,0:T(8,128)(2,1)S(1)} custom-call(bf16[1024,3072]{1,0:T(8,128)(2,1)} %get-tuple-element.151.left_ref, bf16[3072,2048]{1,0:T(8,128)(2,1)} %get-tuple-element.271.back_ref), custom_call_target="tpu_custom_call" | custom-call | flops 6442450944 | bytes 14680064 | tf_op jit(solution)/shard_map/pallas_call | solution.py:227
  367.4 10.7 %shard_map.85 = bf16[1024,1024]{1,0:T(8,128)(2,1)S(1)} custom-call(bf16[1024,3072]{1,0:T(8,128)(2,1)} %get-tuple-element.151.left_ref, bf16[3072,2048]{1,0:T(8,128)(2,1)} %get-tuple-element.271.back_ref), custom_call_target="tpu_custom_call" | custom-call | flops 6442450944 | bytes 14680064 | tf_op jit(solution)/shard_map/pallas_call | solution.py:227
  390.6 16.1 %collective-permute-done.62 = bf16[256,1024]{1,0:T(8,128)(2,1)S(1)} collective-permute-done((bf16[256,1024]{1,0:T(8,128)(2,1)S(1)}, bf16[256,1024]{1,0:T(8,128)(2,1)S(1)}, u32[]{:S(2)}, u32[]{:S(2)}) %collective-permute-start.62) | collective-permute-done | bytes 524320 | tf_op jit(solution)/shard_map/ppermute | solution.py:299
  416.5 12.7 %collective-permute-done.58 = bf16[256,1024]{1,0:T(8,128)(2,1)S(1)} collective-permute-done((bf16[256,1024]{1,0:T(8,128)(2,1)S(1)}, bf16[256,1024]{1,0:T(8,128)(2,1)S(1)}, u32[]{:S(2)}, u32[]{:S(2)}) %collective-permute-start.58) | collective-permute-done | bytes 524320 | tf_op jit(solution)/shard_map/ppermute | solution.py:299
  435.4 5.0 %collective-permute-done.64 = bf16[256,1024]{1,0:T(8,128)(2,1)S(1)} collective-permute-done((bf16[256,1024]{1,0:T(8,128)(2,1)S(1)}, bf16[256,1024]{1,0:T(8,128)(2,1)S(1)}, u32[]{:S(2)}, u32[]{:S(2)}) %collective-permute-start.64) | collective-permute-done | bytes 524320 | tf_op jit(solution)/shard_map/ppermute | solution.py:299
  451.6 7.1 %collective-permute-done.61 = bf16[256,1024]{1,0:T(8,128)(2,1)S(1)} collective-permute-done((bf16[256,1024]{1,0:T(8,128)(2,1)S(1)}, bf16[256,1024]{1,0:T(8,128)(2,1)S(1)}, u32[]{:S(2)}, u32[]{:S(2)}) %collective-permute-start.61) | collective-permute-done | bytes 524320 | tf_op jit(solution)/shard_map/ppermute | solution.py:300
  462.2 5.9 %collective-permute-done.67 = bf16[256,1024]{1,0:T(8,128)(2,1)S(1)} collective-permute-done((bf16[256,1024]{1,0:T(8,128)(2,1)S(1)}, bf16[256,1024]{1,0:T(8,128)(2,1)S(1)}, u32[]{:S(2)}, u32[]{:S(2)}) %collective-permute-start.67) | collective-permute-done | bytes 524320 | tf_op jit(solution)/shard_map/ppermute | solution.py:300
  (220 shorter events, 186.8 us)
Async XLA Ops:
  9.5 28.9 %collective-permute-start = (bf16[256,1024]{1,0:T(8,128)(2,1)S(1)}, bf16[256,1024]{1,0:T(8,128)(2,1)}, u32[]{:S(2)}, u32[]{:S(2)}) collective-permute-start(bf16[256,1024]{1,0:T(8,128)(2,1)S(1)} %bitcast.45), channel_id=1, source_target_pairs={{0,4},{4,8},{8,12},{1,5},{5,9},{9,13},{2,6},{6,10},{10,14},{3,7},{... | collective-permute-start | bytes 1572872 | tf_op jit(solution)/shard_map/ppermute | solution.py:280
  12.9 25.5 %collective-permute-start.1 = (bf16[256,1024]{1,0:T(8,128)(2,1)S(1)}, bf16[256,1024]{1,0:T(8,128)(2,1)}, u32[]{:S(2)}, u32[]{:S(2)}) collective-permute-start(bf16[256,1024]{1,0:T(8,128)(2,1)S(1)} %bitcast.46), channel_id=1, source_target_pairs={{4,0},{8,4},{12,8},{5,1},{9,5},{13,9},{6,2},{10,6},{14,10},{7,3},{... | collective-permute-start | bytes 1572872 | tf_op jit(solution)/shard_map/ppermute | solution.py:281
  20.2 31.2 %collective-permute-start.10 = (bf16[256,1024]{1,0:T(8,128)(2,1)S(1)}, bf16[256,1024]{1,0:T(8,128)(2,1)}, u32[]{:S(2)}, u32[]{:S(2)}) collective-permute-start(bf16[256,1024]{1,0:T(8,128)(2,1)S(1)} %collective-permute-done.4.refs_9_), channel_id=1, source_target_pairs={{4,8},{8,12},{5,9},{9,13},{6,10},{10,14},{7,11},{11,15},{20,24},{2... | collective-permute-start | bytes 1572872 | tf_op jit(solution)/shard_map/ppermute | solution.py:280
  24.4 28.3 %collective-permute-start.12 = (bf16[256,1024]{1,0:T(8,128)(2,1)}, bf16[256,1024]{1,0:T(8,128)(2,1)}, u32[]{:S(2)}, u32[]{:S(2)}) collective-permute-start(bf16[256,1024]{1,0:T(8,128)(2,1)} %collective-permute-done.5.refs_11_), channel_id=1, source_target_pairs={{4,0},{8,4},{5,1},{9,5},{6,2},{10,6},{7,3},{11,7},{20,16},{24,20},... | collective-permute-start | bytes 1572872 | tf_op jit(solution)/shard_map/ppermute | solution.py:281
  69.1 33.1 %collective-permute-start.16 = (bf16[256,1024]{1,0:T(8,128)(2,1)}, bf16[256,1024]{1,0:T(8,128)(2,1)}, u32[]{:S(2)}, u32[]{:S(2)}) collective-permute-start(bf16[256,1024]{1,0:T(8,128)(2,1)} %bitcast.34.refs_10_), channel_id=1, source_target_pairs={{0,4},{4,8},{8,12},{1,5},{5,9},{9,13},{2,6},{6,10},{10,14},{3,7},{... | collective-permute-start | bytes 1572872 | tf_op jit(solution)/shard_map/ppermute | solution.py:280
  71.0 31.1 %collective-permute-start.17 = (bf16[256,1024]{1,0:T(8,128)(2,1)}, bf16[256,1024]{1,0:T(8,128)(2,1)}, u32[]{:S(2)}, u32[]{:S(2)}) collective-permute-start(bf16[256,1024]{1,0:T(8,128)(2,1)} %bitcast.34.refs_10_), channel_id=1, source_target_pairs={{4,0},{8,4},{12,8},{5,1},{9,5},{13,9},{6,2},{10,6},{14,10},{7,3},{... | collective-permute-start | bytes 1572872 | tf_op jit(solution)/shard_map/ppermute | solution.py:281
  80.3 25.1 %collective-permute-start.8 = (bf16[256,1024]{1,0:T(8,128)(2,1)}, bf16[256,1024]{1,0:T(8,128)(2,1)}, u32[]{:S(2)}, u32[]{:S(2)}) collective-permute-start(bf16[256,1024]{1,0:T(8,128)(2,1)} %bitcast.37.refs_3_), channel_id=1, source_target_pairs={{0,4},{4,8},{8,12},{1,5},{5,9},{9,13},{2,6},{6,10},{10,14},{3,7},{... | collective-permute-start | bytes 1572872 | tf_op jit(solution)/shard_map/ppermute | solution.py:280
  102.2 30.9 %collective-permute-start.20 = (bf16[256,1024]{1,0:T(8,128)(2,1)}, bf16[256,1024]{1,0:T(8,128)(2,1)S(1)}, u32[]{:S(2)}, u32[]{:S(2)}) collective-permute-start(bf16[256,1024]{1,0:T(8,128)(2,1)} %collective-permute-done.16.refs_9_), channel_id=1, source_target_pairs={{4,8},{8,12},{5,9},{9,13},{6,10},{10,14},{7,11},{11,15},{20,24},{2... | collective-permute-start | bytes 1572872 | tf_op jit(solution)/shard_map/ppermute | solution.py:280
  103.5 29.5 %collective-permute-start.21 = (bf16[256,1024]{1,0:T(8,128)(2,1)}, bf16[256,1024]{1,0:T(8,128)(2,1)S(1)}, u32[]{:S(2)}, u32[]{:S(2)}) collective-permute-start(bf16[256,1024]{1,0:T(8,128)(2,1)} %collective-permute-done.17.refs_11_), channel_id=1, source_target_pairs={{4,0},{8,4},{5,1},{9,5},{6,2},{10,6},{7,3},{11,7},{20,16},{24,20},... | collective-permute-start | bytes 1572872 | tf_op jit(solution)/shard_map/ppermute | solution.py:281
  105.5 27.6 %collective-permute-start.14 = (bf16[256,1024]{1,0:T(8,128)(2,1)}, bf16[256,1024]{1,0:T(8,128)(2,1)S(1)}, u32[]{:S(2)}, u32[]{:S(2)}) collective-permute-start(bf16[256,1024]{1,0:T(8,128)(2,1)} %collective-permute-done.8.refs_2_), channel_id=1, source_target_pairs={{4,8},{8,12},{5,9},{9,13},{6,10},{10,14},{7,11},{11,15},{20,24},{2... | collective-permute-start | bytes 1572872 | tf_op jit(solution)/shard_map/ppermute | solution.py:280
  133.1 26.3 %collective-permute-start.22 = (bf16[256,1024]{1,0:T(8,128)(2,1)S(1)}, bf16[256,1024]{1,0:T(8,128)(2,1)S(1)}, u32[]{:S(2)}, u32[]{:S(2)}) collective-permute-start(bf16[256,1024]{1,0:T(8,128)(2,1)S(1)} %collective-permute-done.20.refs_8_), channel_id=1, source_target_pairs={{8,12},{9,13},{10,14},{11,15},{24,28},{25,29},{26,30},{27,31}} | collective-permute-start | bytes 1572872 | tf_op jit(solution)/shard_map/ppermute | solution.py:280
  133.8 25.6 %collective-permute-start.23 = (bf16[256,1024]{1,0:T(8,128)(2,1)S(1)}, bf16[256,1024]{1,0:T(8,128)(2,1)S(1)}, u32[]{:S(2)}, u32[]{:S(2)}) collective-permute-start(bf16[256,1024]{1,0:T(8,128)(2,1)S(1)} %collective-permute-done.21.refs_12_), channel_id=1, source_target_pairs={{4,0},{5,1},{6,2},{7,3},{20,16},{21,17},{22,18},{23,19}} | collective-permute-start | bytes 1572872 | tf_op jit(solution)/shard_map/ppermute | solution.py:281
  135.8 25.3 %collective-permute-start.19 = (bf16[256,1024]{1,0:T(8,128)(2,1)S(1)}, bf16[256,1024]{1,0:T(8,128)(2,1)}, u32[]{:S(2)}, u32[]{:S(2)}) collective-permute-start(bf16[256,1024]{1,0:T(8,128)(2,1)S(1)} %collective-permute-done.15.refs_5_), channel_id=1, source_target_pairs={{4,0},{5,1},{6,2},{7,3},{20,16},{21,17},{22,18},{23,19}} | collective-permute-start | bytes 1572872 | tf_op jit(solution)/shard_map/ppermute | solution.py:281
  195.0 32.8 %collective-permute-start.32 = (bf16[256,1024]{1,0:T(8,128)(2,1)S(1)}, bf16[256,1024]{1,0:T(8,128)(2,1)S(1)}, u32[]{:S(2)}, u32[]{:S(2)}) collective-permute-start(bf16[256,1024]{1,0:T(8,128)(2,1)S(1)} %add_convert_fusion.19.refs_0_), channel_id=1, source_target_pairs={{0,2},{2,0},{1,3},{3,1},{4,6},{6,4},{5,7},{7,5},{8,10},{10,8},{9,1... | collective-permute-start | bytes 1572872 | tf_op jit(solution)/shard_map/ppermute | solution.py:309
  223.5 28.5 %collective-permute-start.31 = (bf16[512,1024]{1,0:T(8,128)(2,1)S(1)}, bf16[512,1024]{1,0:T(8,128)(2,1)S(1)}, u32[]{:S(2)}, u32[]{:S(2)}) collective-permute-start(bf16[512,1024]{1,0:T(8,128)(2,1)S(1)} %get-tuple-element.218), channel_id=1, source_target_pairs={{0,2},{2,0},{1,3},{3,1},{4,6},{6,4},{5,7},{7,5},{8,10},{10,8},{9,1... | collective-permute-start | bytes 3145736 | tf_op jit(solution)/shard_map/ppermute | solution.py:309
  224.5 28.6 %collective-permute-start.36 = (bf16[256,1024]{1,0:T(8,128)(2,1)S(1)}, bf16[256,1024]{1,0:T(8,128)(2,1)S(1)}, u32[]{:S(2)}, u32[]{:S(2)}) collective-permute-start(bf16[256,1024]{1,0:T(8,128)(2,1)S(1)} %add_convert_fusion.18.refs_0_), channel_id=1, source_target_pairs={{0,2},{2,0},{1,3},{3,1},{4,6},{6,4},{5,7},{7,5},{8,10},{10,8},{9,1... | collective-permute-start | bytes 1572872 | tf_op jit(solution)/shard_map/ppermute | solution.py:309
  250.4 28.1 %collective-permute-start.40 = (bf16[256,1024]{1,0:T(8,128)(2,1)S(1)}, bf16[256,1024]{1,0:T(8,128)(2,1)S(1)}, u32[]{:S(2)}, u32[]{:S(2)}) collective-permute-start(bf16[256,1024]{1,0:T(8,128)(2,1)S(1)} %add_convert_fusion.17.refs_0_), channel_id=1, source_target_pairs={{0,2},{2,0},{1,3},{3,1},{4,6},{6,4},{5,7},{7,5},{8,10},{10,8},{9,1... | collective-permute-start | bytes 1572872 | tf_op jit(solution)/shard_map/ppermute | solution.py:309
  362.9 47.4 %collective-permute-start.48 = (bf16[256,1024]{1,0:T(8,128)(2,1)S(1)}, bf16[256,1024]{1,0:T(8,128)(2,1)S(1)}, u32[]{:S(2)}, u32[]{:S(2)}) collective-permute-start(bf16[256,1024]{1,0:T(8,128)(2,1)S(1)} %get-tuple-element.263), channel_id=1, source_target_pairs={{0,4},{4,8},{8,12},{1,5},{5,9},{9,13},{2,6},{6,10},{10,14},{3,7},{... | collective-permute-start | bytes 1572872 | tf_op jit(solution)/shard_map/ppermute | solution.py:299
  378.2 28.5 %collective-permute-start.62 = (bf16[256,1024]{1,0:T(8,128)(2,1)S(1)}, bf16[256,1024]{1,0:T(8,128)(2,1)S(1)}, u32[]{:S(2)}, u32[]{:S(2)}) collective-permute-start(bf16[256,1024]{1,0:T(8,128)(2,1)S(1)} %get-tuple-element.284), channel_id=1, source_target_pairs={{0,4},{1,5},{2,6},{3,7},{16,20},{17,21},{18,22},{19,23}} | collective-permute-start | bytes 1572872 | tf_op jit(solution)/shard_map/ppermute | solution.py:299
  379.5 29.1 %collective-permute-start.63 = (bf16[256,1024]{1,0:T(8,128)(2,1)S(1)}, bf16[256,1024]{1,0:T(8,128)(2,1)S(1)}, u32[]{:S(2)}, u32[]{:S(2)}) collective-permute-start(bf16[256,1024]{1,0:T(8,128)(2,1)S(1)} %get-tuple-element.285), channel_id=1, source_target_pairs={{12,8},{13,9},{14,10},{15,11},{28,24},{29,25},{30,26},{31,27}} | collective-permute-start | bytes 1572872 | tf_op jit(solution)/shard_map/ppermute | solution.py:300
  384.2 30.6 %collective-permute-start.49 = (bf16[256,1024]{1,0:T(8,128)(2,1)S(1)}, bf16[256,1024]{1,0:T(8,128)(2,1)S(1)}, u32[]{:S(2)}, u32[]{:S(2)}) collective-permute-start(bf16[256,1024]{1,0:T(8,128)(2,1)S(1)} %get-tuple-element.264), channel_id=1, source_target_pairs={{12,8},{8,4},{4,0},{13,9},{9,5},{5,1},{14,10},{10,6},{6,2},{15,11}... | collective-permute-start | bytes 1572872 | tf_op jit(solution)/shard_map/ppermute | solution.py:300
  386.2 60.5 %collective-permute-start.54 = (bf16[256,1024]{1,0:T(8,128)(2,1)S(1)}, bf16[256,1024]{1,0:T(8,128)(2,1)S(1)}, u32[]{:S(2)}, u32[]{:S(2)}) collective-permute-start(bf16[256,1024]{1,0:T(8,128)(2,1)S(1)} %get-tuple-element.274), channel_id=1, source_target_pairs={{0,4},{4,8},{8,12},{1,5},{5,9},{9,13},{2,6},{6,10},{10,14},{3,7},{... | collective-permute-start | bytes 1572872 | tf_op jit(solution)/shard_map/ppermute | solution.py:299
  410.2 30.2 %collective-permute-start.64 = (bf16[256,1024]{1,0:T(8,128)(2,1)S(1)}, bf16[256,1024]{1,0:T(8,128)(2,1)S(1)}, u32[]{:S(2)}, u32[]{:S(2)}) collective-permute-start(bf16[256,1024]{1,0:T(8,128)(2,1)S(1)} %get-tuple-element.288), channel_id=1, source_target_pairs={{0,4},{4,8},{1,5},{5,9},{2,6},{6,10},{3,7},{7,11},{16,20},{20,24},... | collective-permute-start | bytes 1572872 | tf_op jit(solution)/shard_map/ppermute | solution.py:299
  414.8 27.5 %collective-permute-start.65 = (bf16[256,1024]{1,0:T(8,128)(2,1)S(1)}, bf16[256,1024]{1,0:T(8,128)(2,1)S(1)}, u32[]{:S(2)}, u32[]{:S(2)}) collective-permute-start(bf16[256,1024]{1,0:T(8,128)(2,1)S(1)} %get-tuple-element.289), channel_id=1, source_target_pairs={{12,8},{8,4},{13,9},{9,5},{14,10},{10,6},{15,11},{11,7},{28,24},{2... | collective-permute-start | bytes 1572872 | tf_op jit(solution)/shard_map/ppermute | solution.py:300
  (65 other events, 1167.3 us)
